TPU v7x, 32 devices: a whole 2x2x4 slice. The times are simulated.
32 devices in a mesh: dp: 16 (over z, x, core), expert: 2 (over y).
Axes of the slice: x: 2, y: 2, z: 4, core: 2. Of those that a mesh axis runs over, the one named last changes fastest.
Arguments:
- grad_out: bfloat16 [8192, 1024], P(('dp', 'expert')), may hold values from -1 to 1
- routes: int32 [8192, 6], P(('dp', 'expert')), may hold values from 0 to 63, all different within a row; in each aligned block of 256 rows (0 to 255, 256 to 511, ...) at most 48 rows name the same one
- route_weight: float32 [8192, 6], P(('dp', 'expert')), may hold values from 0.05 to 0.35
- example_ids: int32 [16, 512], P('dp', 'expert'), may hold values from 0 to 7, never falling along the last dimension, each value on 1 to 128 neighbouring positions
- example_weight: float32 [16, 8], P('dp'), may hold values from 0.5 to 50
- hidden: bfloat16 [16, 2, 2, 48, 704], P('dp', 'expert'), may hold values from -6 to 6
Outputs:
- expert_grads: float32 [704, 2, 1024], P('dp', 'expert')
Inputs may be any that keep to these rules, and one draw needn't show every extreme that they name: `routes`: each row names 6 different experts; in the rows of one device no expert is named more than 48 times, a bound that some block reaches. `example_ids`: along a data group's tokens the numbers never fall; each of the 8 examples has from 1 to a quarter of 512 tokens, one exactly that many.
All inputs are finite; a program needn't handle non-finite values.
Results may differ from a plain program's by a relative error of at most 0.0011.
Values may be sent and summed in bfloat16 or wider, within the bound.
No kernel may reach another device: no remote copies, remote signals or barrier semaphores. Data moves between devices by JAX's collectives and lax.ppermute only.
A program may use at most 64 MiB of HBM per device.

v0:
```python
import jax
import jax.numpy as jnp
from jax import lax
from jax.experimental import pallas as pl
from jax.experimental.pallas import tpu as pltpu
from jax.sharding import PartitionSpec as P

EXAMPLES = 8
MATES = 4
LANES = 128
BF16 = jnp.bfloat16
F32 = jnp.float32


def iota(shape, axis):
    return lax.broadcasted_iota(jnp.int32, shape, axis)


def build(sources, cap, n_dp, pad, routes_at, weights_at, ids_at, loss_at, grad_at, hidden_at, *refs):
    blocks, parcels = refs[:sources], refs[sources : sources + MATES]
    routes, weights, ids, loss, grad, hidden, sems = refs[sources + MATES :]
    spare = grad_at.shape[1] + hidden_at.shape[2] // n_dp
    fetches = [
        pltpu.make_async_copy(source, target, sems.at[i])
        for i, (source, target) in enumerate(
            [
                (routes_at, routes),
                (ids_at, ids),
                (loss_at, loss),
                (weights_at, weights),
                (hidden_at, hidden),
                (grad_at, grad),
            ]
        )
    ]
    for fetch in fetches:
        fetch.start()
    me = lax.axis_index("expert")
    tokens, width = grad.shape
    before = (iota((tokens, tokens), 0) < iota((tokens, tokens), 1)).astype(F32).astype(BF16)
    slot = iota((cap, tokens), 0).astype(F32)
    fetches[0].wait()
    matches = [routes[...] == lax.rem(me + (sources - k), sources) for k in range(sources)]
    hits = [jnp.sum(jnp.where(m, 1.0, 0.0), axis=0, keepdims=True) for m in matches]
    blank = -(-sources // 8) * 8 - sources
    routed = jnp.concatenate(hits + [jnp.zeros((1, tokens), F32)] * blank, axis=0)
    ranking = jnp.dot(routed.astype(BF16), before, preferred_element_type=F32)
    for fetch in fetches[1:4]:
        fetch.wait()
    token_ids = ids[...]
    token_weight = jnp.zeros((1, tokens), F32)
    for x in range(EXAMPLES):
        token_weight = jnp.where(token_ids == x, loss[0, x], token_weight)
    token_code = (token_ids + 1).astype(F32)
    ready = []
    for k in range(sources):
        scale = jnp.sum(jnp.where(matches[k], weights[...], 0.0), axis=0, keepdims=True)
        scale = scale * token_weight
        placed = jnp.where(ranking[k : k + 1] == slot, hits[k], 0.0)
        slot_scale = jnp.sum(placed * scale, axis=1, keepdims=True)
        code = jnp.sum(placed * token_code, axis=1, keepdims=True)
        ready.append((placed.astype(BF16), slot_scale, code))
    fetches[4].wait()
    cut_hidden(sources, n_dp, pad, width, hidden, parcels)
    fetches[5].wait()
    for k in range(sources):
        placed, slot_scale, code = ready[k]
        rows = jnp.dot(placed, grad[...], preferred_element_type=F32)
        rows = (rows * slot_scale).astype(BF16)
        blocks[k][:, :width] = rows
        blocks[k][:, width:] = jnp.broadcast_to(code, (cap, LANES)).astype(BF16)
        if k == 0:
            parcels[2][:, :width] = rows
            parcels[2][:, spare : spare + 1] = code.astype(BF16)


def cut_hidden(sources, n_dp, pad, width, hidden, parcels):
    me, rank = lax.axis_index("expert"), lax.axis_index("dp")
    spread = n_dp // MATES
    cap, ff = hidden.shape[1:]
    rows = ff // n_dp
    high, low = rank // MATES, lax.rem(rank, MATES)
    column = iota((1, spread * pad), 1)
    wanted = jnp.full((1, spread * pad), -2 * ff, jnp.int32)
    for p in range(spread):
        inside = (column >= p * pad) & (column < p * pad + rows)
        wanted = jnp.where(inside, (high ^ p) * (MATES * rows) + column - p * pad, wanted)
    unit = iota((ff, spread * pad), 0)
    acts = [hidden[lax.rem(me + j, sources)] for j in range(sources)]
    acts = jnp.concatenate(acts, axis=0)
    for k in range(MATES):
        pick = jnp.where(unit == wanted + (low ^ k) * rows, 1.0, 0.0).astype(BF16)
        units = jnp.dot(acts, pick, preferred_element_type=F32).astype(BF16)
        first = width if k == 2 else 0
        for j in range(sources):
            at = slice(first + j * spread * pad, first + (j + 1) * spread * pad)
            parcels[k][:, at] = units[j * cap : (j + 1) * cap]


def stage(sources, block, hidden, own, left):
    me = lax.axis_index("expert")
    acts = jnp.concatenate([hidden[lax.rem(me + j, sources)] for j in range(sources)], axis=0)
    left[...] = lax.dot_general(
        acts, acts, (((1,), (1,)), ((), ())), preferred_element_type=F32
    )
    own[...] = block[...]


def chosen(codes):
    lane = iota(codes.shape, 1).astype(F32)
    return (codes == lane) & (codes > 0.0)


def norms(sources, left, own, *refs):
    takes, squares = refs[: sources - 1], refs[-1]
    width = own.shape[1] - LANES
    blocks = jnp.concatenate([own[...]] + [t[...] for t in takes], axis=0)
    cot = blocks[:, :width]
    member = jnp.where(chosen(blocks[:, width:].astype(F32)), 1.0, 0.0)
    last = (((1,), (1,)), ((), ()))
    right = lax.dot_general(cot, cot, last, preferred_element_type=F32)
    one_hot = member.astype(BF16)
    alike = lax.dot_general(one_hot, one_hot, last, preferred_element_type=F32)
    per_slot = jnp.sum(left[...] * right * alike, axis=1, keepdims=True)
    squares[...] = jnp.sum(per_slot * member, axis=0, keepdims=True)


def pass_on(across, *refs):
    takes, rest = refs[:-1], refs[-1]
    cap = takes[0].shape[0]
    for j, take in enumerate(takes):
        rest[j * cap : (j + 1) * cap] = take[...]


def pack(rows, own, rest, across, rest_across, clip, clip_across, out):
    cap, width = own.shape[0], own.shape[1] - LANES
    own_codes = own[:, width:].astype(F32)
    across_codes = across[:, width + rows : width + rows + 1].astype(F32)
    across_codes = jnp.broadcast_to(across_codes, (cap, LANES))
    at = 0
    for block, codes, factors in (
        (own, own_codes, clip),
        (rest, rest[:, width:].astype(F32), clip),
        (across, across_codes, clip_across),
        (rest_across, rest_across[:, width:].astype(F32), clip_across),
    ):
        weight = jnp.sum(jnp.where(chosen(codes), factors[...], 0.0), axis=1, keepdims=True)
        weight = weight / EXAMPLES
        scaled = (weight * block[:, :width].astype(F32)).astype(BF16)
        out[at : at + codes.shape[0]] = scaled
        at += codes.shape[0]


def multiply(cuts, cots, units):
    at, cap, across = 0, cuts[0].shape[0], units.shape[1]
    for cut in cuts:
        for j in range(cut.shape[1] // across):
            units[at : at + cap] = cut[:, j * across : (j + 1) * across]
            at += cap
    return lax.dot_general(
        units[...], cots[...], (((0,), (0,)), ((), ())), preferred_element_type=F32
    )


def near_product(cut, across, cots, out, units):
    out[...] = multiply([cut, across.at[:, cots.shape[1] :]], cots, units)


def product(rows, pad, start, cut, across, cots, keep, *refs):
    leave, units = refs[:-1], refs[-1]
    width = cots.shape[1]
    pieces = width // LANES
    part = start[...] + multiply([cut, across], cots, units)
    for p, out in enumerate([keep, *leave]):
        values = part[p * pad : p * pad + rows]
        if p:
            most = jnp.max(jnp.max(jnp.abs(values), axis=0, keepdims=True), axis=1, keepdims=True)
            exponent = jnp.ceil(jnp.log2(jnp.maximum(most, 2.0**-100)))
            values = values * jnp.exp2(-exponent)
            below = out.shape[0] - rows * pieces
            out[rows * pieces :] = jnp.broadcast_to(exponent, (below, LANES))
        for j in range(pieces):
            out[pl.ds(j, rows, stride=pieces), :] = values[:, j * LANES : (j + 1) * LANES]


def call(body, outs, args, fetched=(), scratch=(), limit=32, flops=1):
    vmem = pl.BlockSpec(memory_space=pltpu.VMEM)
    anywhere = pl.BlockSpec(memory_space=pl.ANY)
    return pl.pallas_call(
        body,
        out_shape=tuple(outs),
        in_specs=[anywhere if i in fetched else vmem for i in range(len(args))],
        out_specs=tuple([vmem] * len(outs)),
        scratch_shapes=list(scratch),
        compiler_params=pltpu.CompilerParams(vmem_limit_bytes=limit * 1024 * 1024),
        cost_estimate=pl.CostEstimate(flops=flops, bytes_accessed=1, transcendentals=0),
    )(*args)


def shards(grad_out, routes, route_weight, example_ids, example_weight, hidden):
    sources = lax.axis_size("expert")
    n_dp = lax.axis_size("dp")
    spread = n_dp // MATES
    tokens, width = grad_out.shape
    top = routes.shape[1]
    cap, ff = hidden.shape[3], hidden.shape[4]
    rows = ff // n_dp
    pad = -(-(rows + 1) // 16) * 16
    while spread * pad * sources % LANES:
        pad += 16
    across = spread * pad
    slots = sources * cap
    acts = hidden.reshape(sources, cap, ff)
    shape = jax.ShapeDtypeStruct

    def over_experts(array, k):
        return lax.ppermute(
            array, "expert", [(s, (s - k) % sources) for s in range(sources)]
        )

    def over_dp(array, k):
        return lax.ppermute(array, "dp", [(i, i ^ k) for i in range(n_dp)])

    made = call(
        lambda *refs: build(sources, cap, n_dp, pad, *refs),
        [shape((cap, width + LANES), BF16)] * sources
        + [
            shape((cap, sources * across + (width if k == 2 else 0)), BF16)
            for k in range(MATES)
        ],
        (routes.T, route_weight.T, example_ids, example_weight, grad_out, acts),
        fetched=range(6),
        limit=60,
        scratch=(
            pltpu.VMEM((top, tokens), jnp.int32),
            pltpu.VMEM((top, tokens), F32),
            pltpu.VMEM((1, tokens), jnp.int32),
            pltpu.SMEM((1, EXAMPLES), F32),
            pltpu.VMEM((tokens, width), BF16),
            pltpu.VMEM((sources, cap, ff), BF16),
            pltpu.SemaphoreType.DMA((6,)),
        ),
    )
    (block, *gives), (cut, *parcels) = made[:sources], made[sources:]
    takes = [over_experts(g, k + 1) for k, g in enumerate(gives)]
    parcels = [over_dp(parcel, k + 1) for k, parcel in enumerate(parcels)]
    own, left = call(
        lambda *refs: stage(sources, *refs),
        [shape((cap, width + LANES), BF16), shape((slots, slots), F32)],
        (block, acts),
        flops=1 << 32,
    )
    (rest,) = call(
        pass_on,
        [shape((slots - cap, width + LANES), BF16)],
        (parcels[1], *takes),
        fetched=(0,),
    )
    (squares,) = call(
        lambda *refs: norms(sources, *refs),
        [shape((1, LANES), F32)],
        (left, own, *takes),
        flops=1 << 32,
    )
    total = squares
    for k in range(1, sources):
        total = total + over_experts(squares, k)
    rest_across = over_dp(rest, 2)
    clip = 1.0 / jnp.maximum(jnp.sqrt(total / (ff * width)), 1.0)
    clip_across = over_dp(clip, 2)
    (cots,) = call(
        lambda *refs: pack(rows, *refs),
        [shape((2 * slots, width), BF16)],
        (own, rest, parcels[1], rest_across, clip, clip_across),
    )
    other_cots = over_dp(cots, 1)
    (start,) = call(
        near_product,
        [shape((across, width), F32)],
        (cut, parcels[1], cots),
        scratch=(pltpu.VMEM((2 * slots, across), BF16),),
        flops=1 << 32,
    )

    held = rows * (width // LANES)
    sent = -(-(held + 8) // 16) * 16
    part, *leave = call(
        lambda *refs: product(rows, pad, *refs),
        [shape((held if p == 0 else sent, LANES), F32) for p in range(spread)],
        (start, parcels[0], parcels[2], other_cots),
        scratch=(pltpu.VMEM((2 * slots, across), BF16),),
    )
    for p in range(1, spread):
        got = over_dp(leave[p - 1].astype(jnp.float16), p * MATES).astype(F32)
        part = part + got[:held] * jnp.exp2(got[held : held + 1])
    return part.reshape(rows, 1, width)


def solution(mesh):
    placed = (
        P(("dp", "expert"), None),
        P(("dp", "expert"), None),
        P(("dp", "expert"), None),
        P("dp", "expert"),
        P("dp", None),
        P("dp", "expert", None, None, None),
    )
    return jax.shard_map(
        shards, mesh=mesh, in_specs=placed, out_specs=P("dp", "expert", None), check_vma=False
    )
```

profile of v0, /device:TPU:0, one launch (start us, length us, event | category | flops | bytes accessed | tf_op | source)
XLA Modules:
  0.0 31.8 jit_solution(7385294493390011557)
XLA Ops:
  0.0 0.0 copy-start
  0.0 2.5 %shard_map.64 = (bf16[48,1152]{1,0:T(8,128)(2,1)}, bf16[48,1152]{1,0:T(8,128)(2,1)}, bf16[48,384]{1,0:T(8,128)(2,1)}, bf16[48,384]{1,0:T(8,128)(2,1)}, bf16[48,1...) custom-call(s32[6,256]{1,0:T(8,128)} %bitcast.12, f32[6,256]{1,0:T(8,128)} %bitcast.13, s32[1,256]{1,0:T(1,128)} %refs_2_.1, ...), custom_call_target="tpu_custom_call" | custom-call | flops 1 | bytes 1 | tf_op jit(solution)/shard_map/pallas_call | solution.py:189
  2.5 3.0 %collective-permute-start.1 = (bf16[48,1152]{1,0:T(8,128)(2,1)}, bf16[48,1152]{1,0:T(8,128)(2,1)S(1)}, u32[]{:S(2)}, u32[]{:S(2)}) collective-permute-start(bf16[48,1152]{1,0:T(8,128)(2,1)} %get-tuple-element.21), channel_id=1, source_target_pairs={{0,1},{1,0},{2,3},{3,2},{4,5},{5,4},{6,7},{7,6},{8,9},{9,8},{10,11... | collective-permute-start | bytes 331784 | tf_op jit(solution)/shard_map/ppermute | solution.py:217
  5.5 1.5 %collective-permute-start = (bf16[48,1408]{1,0:T(8,128)(2,1)}, bf16[48,1408]{1,0:T(8,128)(2,1)S(1)}, u32[]{:S(2)}, u32[]{:S(2)}) collective-permute-start(bf16[48,1408]{1,0:T(8,128)(2,1)} %get-tuple-element.18), channel_id=1, source_target_pairs={{0,4},{2,6},{4,0},{6,2},{8,12},{10,14},{12,8},{14,10},{16,20},{18,... | collective-permute-start | bytes 405512 | tf_op jit(solution)/shard_map/ppermute | solution.py:222
  7.0 0.0 copy-done
  7.0 0.0 copy-start.1
  7.0 0.9 %copy-done.1 = bf16[48,1152]{1,0:T(8,128)(2,1)S(1)} copy-done((bf16[48,1152]{1,0:T(8,128)(2,1)S(1)}, bf16[48,1152]{1,0:T(8,128)(2,1)}, u32[]{:S(2)}) %copy-start.1) | copy-done | bytes 110616
  7.9 0.2 shard_map.65
  8.1 0.7 %collective-permute-done.1.refs_0_.refs_2_ = bf16[48,1152]{1,0:T(8,128)(2,1)S(1)} collective-permute-done((bf16[48,1152]{1,0:T(8,128)(2,1)}, bf16[48,1152]{1,0:T(8,128)(2,1)S(1)}, u32[]{:S(2)}, u32[]{:S(2)}) %collective-permute-start.1) | collective-permute-done | bytes 110624 | tf_op jit(solution)/shard_map/ppermute | solution.py:217
  8.8 0.3 shard_map.67
  9.1 0.0 copy-start.4
  9.1 0.0 copy-start.3
  9.1 1.8 %collective-permute-start.3 = (f32[1,128]{1,0:T(1,128)S(1)}, f32[1,128]{1,0:T(1,128)S(1)}, u32[]{:S(2)}, u32[]{:S(2)}) collective-permute-start(f32[1,128]{1,0:T(1,128)S(1)} %shard_map.67), channel_id=1, source_target_pairs={{0,1},{1,0},{2,3},{3,2},{4,5},{5,4},{6,7},{7,6},{8,9},{9,8},{10,11... | collective-permute-start | bytes 1544 | tf_op jit(solution)/shard_map/ppermute | solution.py:217
  10.9 0.0 collective-permute-done.across.refs_2_
  10.9 1.6 %collective-permute-start.2 = (bf16[48,1152]{1,0:T(8,128)(2,1)S(1)}, bf16[48,1152]{1,0:T(8,128)(2,1)S(1)}, u32[]{:S(2)}, u32[]{:S(2)}) collective-permute-start(bf16[48,1152]{1,0:T(8,128)(2,1)S(1)} %shard_map.66.refs_1_), channel_id=1, source_target_pairs={{0,4},{2,6},{4,0},{6,2},{8,12},{10,14},{12,8},{14,10},{16,20},{18,... | collective-permute-start | bytes 331784 | tf_op jit(solution)/shard_map/ppermute | solution.py:222
  12.5 0.2 collective-permute-done.3
  12.7 1.8 %collective-permute-start.4 = (f32[1,128]{1,0:T(1,128)S(1)}, f32[1,128]{1,0:T(1,128)S(1)}, u32[]{:S(2)}, u32[]{:S(2)}) collective-permute-start(f32[1,128]{1,0:T(1,128)S(1)} %maximum_divide_fusion.refs_4_), channel_id=1, source_target_pairs={{0,4},{2,6},{4,0},{6,2},{8,12},{10,14},{12,8},{14,10},{16,20},{18,... | collective-permute-start | bytes 1544 | tf_op jit(solution)/shard_map/ppermute | solution.py:222
  14.5 0.0 copy-done.4
  14.5 0.0 collective-permute-start.5
  14.5 0.0 copy-done.3
  14.5 0.0 copy-start.2
  14.5 0.4 %collective-permute-start.6 = (bf16[48,384]{1,0:T(8,128)(2,1)S(1)}, bf16[48,384]{1,0:T(8,128)(2,1)S(1)}, u32[]{:S(2)}, u32[]{:S(2)}) collective-permute-start(bf16[48,384]{1,0:T(8,128)(2,1)S(1)} %copy-done.3), channel_id=1, source_target_pairs={{0,6},{2,4},{4,2},{6,0},{8,14},{10,12},{12,10},{14,8},{16,22},{18,... | collective-permute-start | bytes 110600 | tf_op jit(solution)/shard_map/ppermute | solution.py:222
  14.9 1.4 %collective-permute-done.4.refs_5_ = f32[1,128]{1,0:T(1,128)S(1)} collective-permute-done((f32[1,128]{1,0:T(1,128)S(1)}, f32[1,128]{1,0:T(1,128)S(1)}, u32[]{:S(2)}, u32[]{:S(2)}) %collective-permute-start.4) | collective-permute-done | bytes 544 | tf_op jit(solution)/shard_map/ppermute | solution.py:222
  16.3 0.0 collective-permute-done.2.refs_3_
  16.3 0.2 shard_map.68.cots
  16.5 0.1 collective-permute-start.7
  16.6 0.0 copy-done.2
  16.6 0.4 %shard_map.69.refs_0_ = f32[192,1024]{1,0:T(8,128)S(1)} custom-call(bf16[48,384]{1,0:T(8,128)(2,1)S(1)} %copy-done.2, bf16[48,1408]{1,0:T(8,128)(2,1)S(1)} %collective-permute-done.across.refs_2_, bf16[192,1024]{1,0:T(8,128)(2,1)S(1)} %shard_map.68.cots), custom_call_target="tpu_custom_call" | custom-call | flops 4294967296 | bytes 1 | tf_op jit(solution)/shard_map/pallas_call | solution.py:189
  17.0 0.0 collective-permute-done.5.refs_1_
  17.0 1.0 %collective-permute-done.6.refs_2_ = bf16[48,384]{1,0:T(8,128)(2,1)S(1)} collective-permute-done((bf16[48,384]{1,0:T(8,128)(2,1)S(1)}, bf16[48,384]{1,0:T(8,128)(2,1)S(1)}, u32[]{:S(2)}, u32[]{:S(2)}) %collective-permute-start.6) | collective-permute-done | bytes 36896 | tf_op jit(solution)/shard_map/ppermute | solution.py:222
  18.0 0.3 %collective-permute-done.7.refs_3_ = bf16[192,1024]{1,0:T(8,128)(2,1)S(1)} collective-permute-done((bf16[192,1024]{1,0:T(8,128)(2,1)S(1)}, bf16[192,1024]{1,0:T(8,128)(2,1)S(1)}, u32[]{:S(2)}, u32[]{:S(2)}) %collective-permute-start.7) | collective-permute-done | bytes 393248 | tf_op jit(solution)/shard_map/ppermute | solution.py:222
  18.3 0.6 %shard_map.70 = (f32[352,128]{1,0:T(8,128)S(1)}, f32[368,128]{1,0:T(8,128)S(1)}, f32[368,128]{1,0:T(8,128)S(1)}, f32[368,128]{1,0:T(8,128)S(1)}) custom-call(f32[192,1024]{1,0:T(8,128)S(1)} %shard_map.69.refs_0_, bf16[48,384]{1,0:T(8,128)(2,1)S(1)} %collective-permute-done.5.refs_1_, bf16[48,384]{1,0:T(8,128)(2,1)S(1)} %collective-permute-done.6.refs_2_, ...), custom_call_target="tpu_custom_call" | custom-call | flops 1 | bytes 1 | tf_op jit(solution)/shard_map/pallas_call | solution.py:189
  18.9 3.9 %collective-permute-start.10 = (f16[368,128]{1,0:T(8,128)(2,1)S(1)}, f16[368,128]{1,0:T(8,128)(2,1)S(1)}, u32[]{:S(2)}, u32[]{:S(2)}) collective-permute-start(f16[368,128]{1,0:T(8,128)(2,1)S(1)} %convert_element_type.22), channel_id=1, source_target_pairs={{0,24},{2,26},{4,28},{6,30},{8,16},{10,18},{12,20},{14,22},{16,8},... | collective-permute-start | bytes 282632 | tf_op jit(solution)/shard_map/ppermute | solution.py:222
  22.8 0.1 collective-permute-start.9
  22.9 0.6 %collective-permute-start.8 = (f16[368,128]{1,0:T(8,128)(2,1)S(1)}, f16[368,128]{1,0:T(8,128)(2,1)S(1)}, u32[]{:S(2)}, u32[]{:S(2)}) collective-permute-start(f16[368,128]{1,0:T(8,128)(2,1)S(1)} %convert_element_type.18), channel_id=1, source_target_pairs={{0,8},{2,10},{4,12},{6,14},{8,0},{10,2},{12,4},{14,6},{16,24},{18,... | collective-permute-start | bytes 282632 | tf_op jit(solution)/shard_map/ppermute | solution.py:222
  23.5 2.9 %collective-permute-done.10 = f16[368,128]{1,0:T(8,128)(2,1)S(1)} collective-permute-done((f16[368,128]{1,0:T(8,128)(2,1)S(1)}, f16[368,128]{1,0:T(8,128)(2,1)S(1)}, u32[]{:S(2)}, u32[]{:S(2)}) %collective-permute-start.10) | collective-permute-done | bytes 94240 | tf_op jit(solution)/shard_map/ppermute | solution.py:222
  26.4 4.6 %collective-permute-done.9 = f16[368,128]{1,0:T(8,128)(2,1)S(1)} collective-permute-done((f16[368,128]{1,0:T(8,128)(2,1)S(1)}, f16[368,128]{1,0:T(8,128)(2,1)S(1)}, u32[]{:S(2)}, u32[]{:S(2)}) %collective-permute-start.9) | collective-permute-done | bytes 94240 | tf_op jit(solution)/shard_map/ppermute | solution.py:222
  31.0 0.0 collective-permute-done.8
  31.1 0.7 %fusion = f32[352,128]{1,0:T(8,128)} fusion(f32[368,128]{1,0:T(8,128)S(1)} %convert_element_type.23, f32[368,128]{1,0:T(8,128)S(1)} %convert_element_type.21, f32[352,128]{1,0:T(8,128)S(1)} %get-tuple-element.25, f32[368,128]{1,0:T(8,128)S(1)} %convert_element_type.19, f32[128]{0:T(128)S(1)} %fusion.4, f32[128]{0:T(128)S(1)} %fusion.6, f32[128]{0:T(128)S(1)} %fusion.8), kind=kLoop, calls=%fused_computation.1 | loop fusion | flops 270336 | bytes 902656 | tf_op jit(solution)/shard_map/add | solution.py:295
  (11 shorter events, 0.1 us)
Async XLA Ops:
  0.0 7.0 %copy-start = (bf16[1,1,2,48,704]{4,3,2,1,0:T(8,128)(2,1)S(1)}, bf16[1,1,2,48,704]{4,3,2,1,0:T(8,128)(2,1)}, u32[]{:S(2)}) copy-start(bf16[1,1,2,48,704]{4,3,2,1,0:T(8,128)(2,1)} %param.11) | copy-start | bytes 405508
  2.5 6.3 %collective-permute-start.1 = (bf16[48,1152]{1,0:T(8,128)(2,1)}, bf16[48,1152]{1,0:T(8,128)(2,1)S(1)}, u32[]{:S(2)}, u32[]{:S(2)}) collective-permute-start(bf16[48,1152]{1,0:T(8,128)(2,1)} %get-tuple-element.21), channel_id=1, source_target_pairs={{0,1},{1,0},{2,3},{3,2},{4,5},{5,4},{6,7},{7,6},{8,9},{9,8},{10,11... | collective-permute-start | bytes 331784 | tf_op jit(solution)/shard_map/ppermute | solution.py:217
  5.5 5.4 %collective-permute-start = (bf16[48,1408]{1,0:T(8,128)(2,1)}, bf16[48,1408]{1,0:T(8,128)(2,1)S(1)}, u32[]{:S(2)}, u32[]{:S(2)}) collective-permute-start(bf16[48,1408]{1,0:T(8,128)(2,1)} %get-tuple-element.18), channel_id=1, source_target_pairs={{0,4},{2,6},{4,0},{6,2},{8,12},{10,14},{12,8},{14,10},{16,20},{18,... | collective-permute-start | bytes 405512 | tf_op jit(solution)/shard_map/ppermute | solution.py:222
  7.0 0.9 %copy-start.1 = (bf16[48,1152]{1,0:T(8,128)(2,1)S(1)}, bf16[48,1152]{1,0:T(8,128)(2,1)}, u32[]{:S(2)}) copy-start(bf16[48,1152]{1,0:T(8,128)(2,1)} %get-tuple-element.19.refs_0_) | copy-start | bytes 331780
  9.1 5.4 %copy-start.4 = (bf16[48,384]{1,0:T(8,128)(2,1)S(1)}, bf16[48,384]{1,0:T(8,128)(2,1)}, u32[]{:S(2)}) copy-start(bf16[48,384]{1,0:T(8,128)(2,1)} %get-tuple-element.23) | copy-start | bytes 110596
  9.1 5.4 %copy-start.3 = (bf16[48,384]{1,0:T(8,128)(2,1)S(1)}, bf16[48,384]{1,0:T(8,128)(2,1)}, u32[]{:S(2)}) copy-start(bf16[48,384]{1,0:T(8,128)(2,1)} %get-tuple-element.24) | copy-start | bytes 110596
  9.1 3.6 %collective-permute-start.3 = (f32[1,128]{1,0:T(1,128)S(1)}, f32[1,128]{1,0:T(1,128)S(1)}, u32[]{:S(2)}, u32[]{:S(2)}) collective-permute-start(f32[1,128]{1,0:T(1,128)S(1)} %shard_map.67), channel_id=1, source_target_pairs={{0,1},{1,0},{2,3},{3,2},{4,5},{5,4},{6,7},{7,6},{8,9},{9,8},{10,11... | collective-permute-start | bytes 1544 | tf_op jit(solution)/shard_map/ppermute | solution.py:217
  10.9 5.4 %collective-permute-start.2 = (bf16[48,1152]{1,0:T(8,128)(2,1)S(1)}, bf16[48,1152]{1,0:T(8,128)(2,1)S(1)}, u32[]{:S(2)}, u32[]{:S(2)}) collective-permute-start(bf16[48,1152]{1,0:T(8,128)(2,1)S(1)} %shard_map.66.refs_1_), channel_id=1, source_target_pairs={{0,4},{2,6},{4,0},{6,2},{8,12},{10,14},{12,8},{14,10},{16,20},{18,... | collective-permute-start | bytes 331784 | tf_op jit(solution)/shard_map/ppermute | solution.py:222
  12.7 3.6 %collective-permute-start.4 = (f32[1,128]{1,0:T(1,128)S(1)}, f32[1,128]{1,0:T(1,128)S(1)}, u32[]{:S(2)}, u32[]{:S(2)}) collective-permute-start(f32[1,128]{1,0:T(1,128)S(1)} %maximum_divide_fusion.refs_4_), channel_id=1, source_target_pairs={{0,4},{2,6},{4,0},{6,2},{8,12},{10,14},{12,8},{14,10},{16,20},{18,... | collective-permute-start | bytes 1544 | tf_op jit(solution)/shard_map/ppermute | solution.py:222
  14.5 2.5 %collective-permute-start.5 = (bf16[48,384]{1,0:T(8,128)(2,1)S(1)}, bf16[48,384]{1,0:T(8,128)(2,1)S(1)}, u32[]{:S(2)}, u32[]{:S(2)}) collective-permute-start(bf16[48,384]{1,0:T(8,128)(2,1)S(1)} %copy-done.4), channel_id=1, source_target_pairs={{0,2},{2,0},{4,6},{6,4},{8,10},{10,8},{12,14},{14,12},{16,18},{18,... | collective-permute-start | bytes 110600 | tf_op jit(solution)/shard_map/ppermute | solution.py:222
  14.5 2.1 %copy-start.2 = (bf16[48,384]{1,0:T(8,128)(2,1)S(1)}, bf16[48,384]{1,0:T(8,128)(2,1)}, u32[]{:S(2)}) copy-start(bf16[48,384]{1,0:T(8,128)(2,1)} %get-tuple-element.17.cut) | copy-start | bytes 110596
  14.5 3.4 %collective-permute-start.6 = (bf16[48,384]{1,0:T(8,128)(2,1)S(1)}, bf16[48,384]{1,0:T(8,128)(2,1)S(1)}, u32[]{:S(2)}, u32[]{:S(2)}) collective-permute-start(bf16[48,384]{1,0:T(8,128)(2,1)S(1)} %copy-done.3), channel_id=1, source_target_pairs={{0,6},{2,4},{4,2},{6,0},{8,14},{10,12},{12,10},{14,8},{16,22},{18,... | collective-permute-start | bytes 110600 | tf_op jit(solution)/shard_map/ppermute | solution.py:222
  16.5 1.8 %collective-permute-start.7 = (bf16[192,1024]{1,0:T(8,128)(2,1)S(1)}, bf16[192,1024]{1,0:T(8,128)(2,1)S(1)}, u32[]{:S(2)}, u32[]{:S(2)}) collective-permute-start(bf16[192,1024]{1,0:T(8,128)(2,1)S(1)} %shard_map.68.cots), channel_id=1, source_target_pairs={{0,2},{2,0},{4,6},{6,4},{8,10},{10,8},{12,14},{14,12},{16,18},{18,... | collective-permute-start | bytes 1179656 | tf_op jit(solution)/shard_map/ppermute | solution.py:222
  18.9 7.5 %collective-permute-start.10 = (f16[368,128]{1,0:T(8,128)(2,1)S(1)}, f16[368,128]{1,0:T(8,128)(2,1)S(1)}, u32[]{:S(2)}, u32[]{:S(2)}) collective-permute-start(f16[368,128]{1,0:T(8,128)(2,1)S(1)} %convert_element_type.22), channel_id=1, source_target_pairs={{0,24},{2,26},{4,28},{6,30},{8,16},{10,18},{12,20},{14,22},{16,8},... | collective-permute-start | bytes 282632 | tf_op jit(solution)/shard_map/ppermute | solution.py:222
  22.8 8.2 %collective-permute-start.9 = (f16[368,128]{1,0:T(8,128)(2,1)S(1)}, f16[368,128]{1,0:T(8,128)(2,1)S(1)}, u32[]{:S(2)}, u32[]{:S(2)}) collective-permute-start(f16[368,128]{1,0:T(8,128)(2,1)S(1)} %convert_element_type.20), channel_id=1, source_target_pairs={{0,16},{2,18},{4,20},{6,22},{8,24},{10,26},{12,28},{14,30},{16,0},... | collective-permute-start | bytes 282632 | tf_op jit(solution)/shard_map/ppermute | solution.py:222
  22.9 8.1 %collective-permute-start.8 = (f16[368,128]{1,0:T(8,128)(2,1)S(1)}, f16[368,128]{1,0:T(8,128)(2,1)S(1)}, u32[]{:S(2)}, u32[]{:S(2)}) collective-permute-start(f16[368,128]{1,0:T(8,128)(2,1)S(1)} %convert_element_type.18), channel_id=1, source_target_pairs={{0,8},{2,10},{4,12},{6,14},{8,0},{10,2},{12,4},{14,6},{16,24},{18,... | collective-permute-start | bytes 282632 | tf_op jit(solution)/shard_map/ppermute | solution.py:222
where the time goes:
time: 31.9 us; the launch traced here: 31.8 us
  starting transfers between devices  14.7 us (46%)
  waiting for transfers between devices  11.1 us (35%)
  Pallas kernels  4.05 us (13%)
  local copies, waits for them, and re-layouts  0.91 us (3%)
  other arithmetic  0.85 us (3%)
    ppermute x9, waiting for transfers between devices, over_dp(): return lax.ppermute(array, 'dp', [(i, i ^ k) for i in range(n_dp)])  10.2 us
    ppermute x9, starting transfers between devices, over_dp(): return lax.ppermute(array, 'dp', [(i, i ^ k) for i in range(n_dp)])  9.86 us
    ppermute x2, starting transfers between devices, over_experts(): lax.ppermute(array, 'expert', [(s, (s - k) % sources) for s in range(sour...  4.84 us
    pallas_call x7, Pallas kernels, call(): pl.pallas_call(body, out_shape=tuple(outs), in_specs=[anywhere if i in fe...  4.05 us
    unnamed x10, local copies, waits for them, and re-layouts  0.91 us
    ppermute x2, waiting for transfers between devices, over_experts(): lax.ppermute(array, 'expert', [(s, (s - k) % sources) for s in range(sour...  0.9 us
    add x1, other arithmetic, shards(): part = part + got[:held] * jnp.exp2(got[held:held + 1])  0.73 us
  transfers between devices with their start and end apart: 11, of which 7 were waited for; matrix products, arithmetic and copies ran while one was open for 0% of the time, Pallas kernels for 3%

commit v1 on v0

--- a/solution.py
+++ b/solution.py
@@ -16,10 +16,9 @@
     return lax.broadcasted_iota(jnp.int32, shape, axis)
 
 
-def build(sources, cap, n_dp, pad, routes_at, weights_at, ids_at, loss_at, grad_at, hidden_at, *refs):
-    blocks, parcels = refs[:sources], refs[sources : sources + MATES]
-    routes, weights, ids, loss, grad, hidden, sems = refs[sources + MATES :]
-    spare = grad_at.shape[1] + hidden_at.shape[2] // n_dp
+def build(sources, cap, routes_at, weights_at, ids_at, loss_at, grad_at, *refs):
+    blocks = refs[:sources]
+    routes, weights, ids, loss, grad, sems = refs[sources:]
     fetches = [
         pltpu.make_async_copy(source, target, sems.at[i])
         for i, (source, target) in enumerate(
@@ -28,7 +27,6 @@
                 (ids_at, ids),
                 (loss_at, loss),
                 (weights_at, weights),
-                (hidden_at, hidden),
                 (grad_at, grad),
             ]
         )
@@ -61,20 +59,16 @@
         code = jnp.sum(placed * token_code, axis=1, keepdims=True)
         ready.append((placed.astype(BF16), slot_scale, code))
     fetches[4].wait()
-    cut_hidden(sources, n_dp, pad, width, hidden, parcels)
-    fetches[5].wait()
     for k in range(sources):
         placed, slot_scale, code = ready[k]
         rows = jnp.dot(placed, grad[...], preferred_element_type=F32)
         rows = (rows * slot_scale).astype(BF16)
         blocks[k][:, :width] = rows
         blocks[k][:, width:] = jnp.broadcast_to(code, (cap, LANES)).astype(BF16)
-        if k == 0:
-            parcels[2][:, :width] = rows
-            parcels[2][:, spare : spare + 1] = code.astype(BF16)
-
-
-def cut_hidden(sources, n_dp, pad, width, hidden, parcels):
+
+
+def stage(sources, n_dp, pad, block, hidden, own, left, *cuts):
+    own[...] = block[...]
     me, rank = lax.axis_index("expert"), lax.axis_index("dp")
     spread = n_dp // MATES
     cap, ff = hidden.shape[1:]
@@ -88,25 +82,19 @@
     unit = iota((ff, spread * pad), 0)
     acts = [hidden[lax.rem(me + j, sources)] for j in range(sources)]
     acts = jnp.concatenate(acts, axis=0)
+    left[...] = lax.dot_general(
+        acts, acts, (((1,), (1,)), ((), ())), preferred_element_type=F32
+    )
     for k in range(MATES):
         pick = jnp.where(unit == wanted + (low ^ k) * rows, 1.0, 0.0).astype(BF16)
         units = jnp.dot(acts, pick, preferred_element_type=F32).astype(BF16)
-        first = width if k == 2 else 0
         for j in range(sources):
-            at = slice(first + j * spread * pad, first + (j + 1) * spread * pad)
-            parcels[k][:, at] = units[j * cap : (j + 1) * cap]
-
-
-def stage(sources, block, hidden, own, left):
-    me = lax.axis_index("expert")
-    acts = jnp.concatenate([hidden[lax.rem(me + j, sources)] for j in range(sources)], axis=0)
-    left[...] = lax.dot_general(
-        acts, acts, (((1,), (1,)), ((), ())), preferred_element_type=F32
-    )
-    own[...] = block[...]
+            at = slice(j * spread * pad, (j + 1) * spread * pad)
+            cuts[k][:, at] = units[j * cap : (j + 1) * cap]
 
 
 def chosen(codes):
+    codes = jnp.broadcast_to(codes.astype(F32), (codes.shape[0], LANES))
     lane = iota(codes.shape, 1).astype(F32)
     return (codes == lane) & (codes > 0.0)
 
@@ -116,7 +104,7 @@
     width = own.shape[1] - LANES
     blocks = jnp.concatenate([own[...]] + [t[...] for t in takes], axis=0)
     cot = blocks[:, :width]
-    member = jnp.where(chosen(blocks[:, width:].astype(F32)), 1.0, 0.0)
+    member = jnp.where(chosen(blocks[:, width : width + 1]), 1.0, 0.0)
     last = (((1,), (1,)), ((), ()))
     right = lax.dot_general(cot, cot, last, preferred_element_type=F32)
     one_hot = member.astype(BF16)
@@ -125,30 +113,42 @@
     squares[...] = jnp.sum(per_slot * member, axis=0, keepdims=True)
 
 
-def pass_on(across, *refs):
+def pass_on(across, squares, cut, *refs):
     takes, rest = refs[:-1], refs[-1]
-    cap = takes[0].shape[0]
+    cap, wide = takes[0].shape
+    half = LANES // 2
     for j, take in enumerate(takes):
-        rest[j * cap : (j + 1) * cap] = take[...]
-
-
-def pack(rows, own, rest, across, rest_across, clip, clip_across, out):
-    cap, width = own.shape[0], own.shape[1] - LANES
-    own_codes = own[:, width:].astype(F32)
-    across_codes = across[:, width + rows : width + rows + 1].astype(F32)
-    across_codes = jnp.broadcast_to(across_codes, (cap, LANES))
+        part = slice(j * cap, (j + 1) * cap)
+        rest[part, :wide] = take[...]
+        if j:
+            rest[part, wide:] = jnp.zeros((cap, rest.shape[1] - wide), BF16)
+    rest[:cap, wide:] = cut[...]
+    value = jnp.broadcast_to(squares[...], (cap, LANES))
+    high = value.astype(BF16).astype(F32)
+    middle = (value - high).astype(BF16).astype(F32)
+    low = value - high - middle
+    row = iota((cap, LANES), 0)
+    three = jnp.where(row == 0, high, jnp.where(row == 1, middle, low)).astype(BF16)
+    rest[:cap, wide - half : wide] = three[:, :half]
+
+
+def pack(sources, count, own, rest, across, rest_across, *refs):
+    near, far, out = refs[:sources], refs[sources:-1], refs[-1]
+    width = own.shape[1] - LANES
+    half = LANES // 2
+    three = rest_across[0:8, width + half : width + LANES].astype(F32)
+    three = three[0:1] + three[1:2] + three[2:3]
+    totals = [near[0][...], jnp.concatenate([three, jnp.zeros_like(three)], axis=1)]
+    for k in range(1, sources):
+        totals = [totals[0] + near[k][...], totals[1] + far[k - 1][...]]
+    clips = [1.0 / jnp.maximum(jnp.sqrt(total / count), 1.0) for total in totals]
     at = 0
-    for block, codes, factors in (
-        (own, own_codes, clip),
-        (rest, rest[:, width:].astype(F32), clip),
-        (across, across_codes, clip_across),
-        (rest_across, rest_across[:, width:].astype(F32), clip_across),
-    ):
-        weight = jnp.sum(jnp.where(chosen(codes), factors[...], 0.0), axis=1, keepdims=True)
-        weight = weight / EXAMPLES
+    for block, clip in ((own, clips[0]), (rest, clips[0]), (across, clips[1]), (rest_across, clips[1])):
+        mine = chosen(block[:, width : width + 1])
+        weight = jnp.sum(jnp.where(mine, clip, 0.0), axis=1, keepdims=True) / EXAMPLES
         scaled = (weight * block[:, :width].astype(F32)).astype(BF16)
-        out[at : at + codes.shape[0]] = scaled
-        at += codes.shape[0]
+        out[at : at + mine.shape[0]] = scaled
+        at += mine.shape[0]
 
 
 def multiply(cuts, cots, units):
@@ -162,8 +162,11 @@
     )
 
 
-def near_product(cut, across, cots, out, units):
-    out[...] = multiply([cut, across.at[:, cots.shape[1] :]], cots, units)
+def near_product(cut, rest_across, cots, out, units):
+    first = cots.shape[1] + LANES
+    cap = cut.shape[0]
+    across = rest_across.at[:cap, first : first + cut.shape[1]]
+    out[...] = multiply([cut, across], cots, units)
 
 
 def product(rows, pad, start, cut, across, cots, keep, *refs):
@@ -221,15 +224,18 @@
     def over_dp(array, k):
         return lax.ppermute(array, "dp", [(i, i ^ k) for i in range(n_dp)])
 
-    made = call(
-        lambda *refs: build(sources, cap, n_dp, pad, *refs),
-        [shape((cap, width + LANES), BF16)] * sources
-        + [
-            shape((cap, sources * across + (width if k == 2 else 0)), BF16)
-            for k in range(MATES)
-        ],
-        (routes.T, route_weight.T, example_ids, example_weight, grad_out, acts),
-        fetched=range(6),
+    def over_both(array, k):
+        where = [(i, e) for i in range(n_dp) for e in range(sources)]
+        pairs = [
+            (i * sources + e, (i ^ 2) * sources + (e - k) % sources) for i, e in where
+        ]
+        return lax.ppermute(array, ("dp", "expert"), pairs)
+
+    block, *gives = call(
+        lambda *refs: build(sources, cap, *refs),
+        [shape((cap, width + LANES), BF16)] * sources,
+        (routes.T, route_weight.T, example_ids, example_weight, grad_out),
+        fetched=range(5),
         limit=60,
         scratch=(
             pltpu.VMEM((top, tokens), jnp.int32),
@@ -237,24 +243,17 @@
             pltpu.VMEM((1, tokens), jnp.int32),
             pltpu.SMEM((1, EXAMPLES), F32),
             pltpu.VMEM((tokens, width), BF16),
-            pltpu.VMEM((sources, cap, ff), BF16),
-            pltpu.SemaphoreType.DMA((6,)),
+            pltpu.SemaphoreType.DMA((5,)),
         ),
     )
-    (block, *gives), (cut, *parcels) = made[:sources], made[sources:]
     takes = [over_experts(g, k + 1) for k, g in enumerate(gives)]
-    parcels = [over_dp(parcel, k + 1) for k, parcel in enumerate(parcels)]
-    own, left = call(
-        lambda *refs: stage(sources, *refs),
-        [shape((cap, width + LANES), BF16), shape((slots, slots), F32)],
+    block_across = over_dp(block, 2)
+    own, left, *cuts = call(
+        lambda *refs: stage(sources, n_dp, pad, *refs),
+        [shape((cap, width + LANES), BF16), shape((slots, slots), F32)]
+        + [shape((cap, sources * across), BF16)] * MATES,
         (block, acts),
         flops=1 << 32,
-    )
-    (rest,) = call(
-        pass_on,
-        [shape((slots - cap, width + LANES), BF16)],
-        (parcels[1], *takes),
-        fetched=(0,),
     )
     (squares,) = call(
         lambda *refs: norms(sources, *refs),
@@ -262,32 +261,35 @@
         (left, own, *takes),
         flops=1 << 32,
     )
-    total = squares
-    for k in range(1, sources):
-        total = total + over_experts(squares, k)
+    (rest,) = call(
+        pass_on,
+        [shape((slots - cap, width + LANES + sources * across), BF16)],
+        (block_across, squares, cuts[2], *takes),
+        fetched=(0,),
+    )
     rest_across = over_dp(rest, 2)
-    clip = 1.0 / jnp.maximum(jnp.sqrt(total / (ff * width)), 1.0)
-    clip_across = over_dp(clip, 2)
+    near_squares = [squares] + [over_experts(squares, k) for k in range(1, sources)]
+    far_squares = [over_both(squares, k) for k in range(1, sources)]
     (cots,) = call(
-        lambda *refs: pack(rows, *refs),
+        lambda *refs: pack(sources, ff * width, *refs),
         [shape((2 * slots, width), BF16)],
-        (own, rest, parcels[1], rest_across, clip, clip_across),
+        (own, rest, block_across, rest_across, *near_squares, *far_squares),
     )
     other_cots = over_dp(cots, 1)
     (start,) = call(
         near_product,
         [shape((across, width), F32)],
-        (cut, parcels[1], cots),
+        (cuts[0], rest_across, cots),
         scratch=(pltpu.VMEM((2 * slots, across), BF16),),
         flops=1 << 32,
     )
 
     held = rows * (width // LANES)
-    sent = -(-(held + 8) // 16) * 16
+    sent = held + 8
     part, *leave = call(
         lambda *refs: product(rows, pad, *refs),
         [shape((held if p == 0 else sent, LANES), F32) for p in range(spread)],
-        (start, parcels[0], parcels[2], other_cots),
+        (start, over_dp(cuts[1], 1), over_dp(cuts[3], 3), other_cots),
         scratch=(pltpu.VMEM((2 * slots, across), BF16),),
     )
     for p in range(1, spread):

time: 31.9 us -> 31.4 us (0.984)
  starting transfers between devices: 14.7 us -> 14.2 us
    ppermute x0 -> x1, waiting for transfers between devices: none -> 0.83 us  [over_both(): return lax.ppermute(array, ('dp', 'expert'), pairs)]
    ppermute x9 -> x8, starting transfers between devices: 9.86 us -> 9.18 us  [over_dp(): return lax.ppermute(array, 'dp', [(i, i ^ k) for i in range(n_dp)])]
    ppermute x2, waiting for transfers between devices: 0.9 us -> 0.28 us  [over_experts(): lax.ppermute(array, 'expert', [(s, (s - k) % sources) for s in range(sour...]
    ppermute x9 -> x8, waiting for transfers between devices: 10.2 us -> 9.81 us  [over_dp(): return lax.ppermute(array, 'dp', [(i, i ^ k) for i in range(n_dp)])]
    ppermute x0 -> x1, starting transfers between devices: none -> 0.37 us  [over_both(): return lax.ppermute(array, ('dp', 'expert'), pairs)]
    unnamed x10 -> x4, local copies, waits for them, and re-layouts: 0.91 us -> 0.93 us
  transfers between devices with their start and end apart: 11 -> 11, of which waited for: 7 -> 7; matrix products, arithmetic and copies ran while one was open for 0% -> 0% of each run, Pallas kernels for 3% -> 5%
where the time goes in v1:
time: 31.4 us; the launch traced here: 31.3 us
  starting transfers between devices  14.2 us (45%)
  waiting for transfers between devices  10.9 us (35%)
  Pallas kernels  4.24 us (14%)
  local copies, waits for them, and re-layouts  0.93 us (3%)
  other arithmetic  0.84 us (3%)
    ppermute x8, waiting for transfers between devices, over_dp(): return lax.ppermute(array, 'dp', [(i, i ^ k) for i in range(n_dp)])  9.81 us
    ppermute x8, starting transfers between devices, over_dp(): return lax.ppermute(array, 'dp', [(i, i ^ k) for i in range(n_dp)])  9.18 us
    ppermute x2, starting transfers between devices, over_experts(): lax.ppermute(array, 'expert', [(s, (s - k) % sources) for s in range(sour...  4.66 us
    pallas_call x7, Pallas kernels, call(): pl.pallas_call(body, out_shape=tuple(outs), in_specs=[anywhere if i in fe...  4.24 us
    unnamed x4, local copies, waits for them, and re-layouts  0.93 us
    ppermute x1, waiting for transfers between devices, over_both(): return lax.ppermute(array, ('dp', 'expert'), pairs)  0.83 us
    add x1, other arithmetic, shards(): part = part + got[:held] * jnp.exp2(got[held:held + 1])  0.73 us
  transfers between devices with their start and end apart: 11, of which 7 were waited for; matrix products, arithmetic and copies ran while one was open for 0% of the time, Pallas kernels for 5%

profile of v1, /device:TPU:0, one launch (start us, length us, event | category | flops | bytes accessed | tf_op | source)
XLA Modules:
  0.0 31.3 jit_solution(1619753196194524331)
XLA Ops:
  0.0 0.0 copy-start
  0.0 2.1 %shard_map.64 = (bf16[48,1152]{1,0:T(8,128)(2,1)}, bf16[48,1152]{1,0:T(8,128)(2,1)}) custom-call(s32[6,256]{1,0:T(8,128)} %bitcast.11, f32[6,256]{1,0:T(8,128)} %bitcast.12, s32[1,256]{1,0:T(1,128)} %refs_2_.1, f32[1,8]{1,0:T(1,128)} %refs_3_.1, bf16[256,1024]{1,0:T(8,128)(2,1)} %refs_4_.1), custom_call_target="tpu_custom_call" | custom-call | flops 1 | bytes 1 | tf_op jit(solution)/shard_map/pallas_call | solution.py:192
  2.2 3.0 %collective-permute-start.1 = (bf16[48,1152]{1,0:T(8,128)(2,1)}, bf16[48,1152]{1,0:T(8,128)(2,1)S(1)}, u32[]{:S(2)}, u32[]{:S(2)}) collective-permute-start(bf16[48,1152]{1,0:T(8,128)(2,1)} %get-tuple-element.21), channel_id=1, source_target_pairs={{0,1},{1,0},{2,3},{3,2},{4,5},{5,4},{6,7},{7,6},{8,9},{9,8},{10,11... | collective-permute-start | bytes 331784 | tf_op jit(solution)/shard_map/ppermute | solution.py:220
  5.2 1.5 %collective-permute-start = (bf16[48,1152]{1,0:T(8,128)(2,1)}, bf16[48,1152]{1,0:T(8,128)(2,1)S(1)}, u32[]{:S(2)}, u32[]{:S(2)}) collective-permute-start(bf16[48,1152]{1,0:T(8,128)(2,1)} %get-tuple-element.17.refs_0_), channel_id=1, source_target_pairs={{0,4},{2,6},{4,0},{6,2},{8,12},{10,14},{12,8},{14,10},{16,20},{18,... | collective-permute-start | bytes 331784 | tf_op jit(solution)/shard_map/ppermute | solution.py:225
  6.7 0.0 copy-done
  6.7 0.0 copy-start.1
  6.7 0.9 %copy-done.1 = bf16[48,1152]{1,0:T(8,128)(2,1)S(1)} copy-done((bf16[48,1152]{1,0:T(8,128)(2,1)S(1)}, bf16[48,1152]{1,0:T(8,128)(2,1)}, u32[]{:S(2)}) %copy-start.1) | copy-done | bytes 110616
  7.6 0.6 %shard_map.65 = (bf16[48,1152]{1,0:T(8,128)(2,1)S(1)}, f32[96,96]{1,0:T(8,128)S(1)}, bf16[48,384]{1,0:T(8,128)(2,1)S(1)}, bf16[48,384]{1,0:T(8,128)(2,1)S(1)}, b...) custom-call(bf16[48,1152]{1,0:T(8,128)(2,1)S(1)} %copy-done.1, bf16[2,48,704]{2,1,0:T(8,128)(2,1)S(1)} %bitcast.10), custom_call_target="tpu_custom_call" | custom-call | flops 4294967296 | bytes 1 | tf_op jit(solution)/shard_map/pallas_call | solution.py:192
  8.2 0.3 collective-permute-done.1.refs_2_.refs_0_
  8.5 0.3 %shard_map.66.squares.refs_4_ = f32[1,128]{1,0:T(1,128)S(1)} custom-call(f32[96,96]{1,0:T(8,128)S(1)} %get-tuple-element.19.refs_0_, bf16[48,1152]{1,0:T(8,128)(2,1)S(1)} %get-tuple-element.20.refs_1_.refs_0_, bf16[48,1152]{1,0:T(8,128)(2,1)S(1)} %collective-permute-done.1.refs_2_.refs_0_), custom_call_target="tpu_custom_call" | custom-call | flops 4294967296 | bytes 1 | tf_op jit(solution)/shard_map/pallas_call | solution.py:192
  8.8 1.4 %collective-permute-done.across.refs_2_ = bf16[48,1152]{1,0:T(8,128)(2,1)S(1)} collective-permute-done((bf16[48,1152]{1,0:T(8,128)(2,1)}, bf16[48,1152]{1,0:T(8,128)(2,1)S(1)}, u32[]{:S(2)}, u32[]{:S(2)}) %collective-permute-start) | collective-permute-done | bytes 110624 | tf_op jit(solution)/shard_map/ppermute | solution.py:225
  10.1 0.1 shard_map.67.refs_1_
  10.2 1.5 %collective-permute-start.2 = (bf16[48,1536]{1,0:T(8,128)(2,1)S(1)}, bf16[48,1536]{1,0:T(8,128)(2,1)S(1)}, u32[]{:S(2)}, u32[]{:S(2)}) collective-permute-start(bf16[48,1536]{1,0:T(8,128)(2,1)S(1)} %shard_map.67.refs_1_), channel_id=1, source_target_pairs={{0,4},{2,6},{4,0},{6,2},{8,12},{10,14},{12,8},{14,10},{16,20},{18,... | collective-permute-start | bytes 442376 | tf_op jit(solution)/shard_map/ppermute | solution.py:225
  11.7 0.4 %collective-permute-start.4 = (f32[1,128]{1,0:T(1,128)S(1)}, f32[1,128]{1,0:T(1,128)S(1)}, u32[]{:S(2)}, u32[]{:S(2)}) collective-permute-start(f32[1,128]{1,0:T(1,128)S(1)} %shard_map.66.squares.refs_4_), channel_id=1, source_target_pairs={{0,5},{1,4},{2,7},{3,6},{4,1},{5,0},{6,3},{7,2},{8,13},{9,12},{10,... | collective-permute-start | bytes 1544 | tf_op jit(solution)/shard_map/ppermute | solution.py:232
  12.1 1.6 %collective-permute-start.3 = (f32[1,128]{1,0:T(1,128)S(1)}, f32[1,128]{1,0:T(1,128)S(1)}, u32[]{:S(2)}, u32[]{:S(2)}) collective-permute-start(f32[1,128]{1,0:T(1,128)S(1)} %shard_map.66.squares.refs_4_), channel_id=1, source_target_pairs={{0,1},{1,0},{2,3},{3,2},{4,5},{5,4},{6,7},{7,6},{8,9},{9,8},{10,11... | collective-permute-start | bytes 1544 | tf_op jit(solution)/shard_map/ppermute | solution.py:220
  13.7 0.0 collective-permute-start.5
  13.7 1.6 %collective-permute-start.6 = (bf16[48,384]{1,0:T(8,128)(2,1)S(1)}, bf16[48,384]{1,0:T(8,128)(2,1)S(1)}, u32[]{:S(2)}, u32[]{:S(2)}) collective-permute-start(bf16[48,384]{1,0:T(8,128)(2,1)S(1)} %get-tuple-element.24), channel_id=1, source_target_pairs={{0,6},{2,4},{4,2},{6,0},{8,14},{10,12},{12,10},{14,8},{16,22},{18,... | collective-permute-start | bytes 110600 | tf_op jit(solution)/shard_map/ppermute | solution.py:225
  15.3 0.8 %collective-permute-done.4.refs_6_ = f32[1,128]{1,0:T(1,128)S(1)} collective-permute-done((f32[1,128]{1,0:T(1,128)S(1)}, f32[1,128]{1,0:T(1,128)S(1)}, u32[]{:S(2)}, u32[]{:S(2)}) %collective-permute-start.4) | collective-permute-done | bytes 544 | tf_op jit(solution)/shard_map/ppermute | solution.py:232
  16.2 0.0 collective-permute-done.3.refs_5_
  16.2 0.0 collective-permute-done.2.refs_3_.rest_across
  16.2 0.2 shard_map.68.cots
  16.4 0.1 collective-permute-start.7
  16.5 0.4 %shard_map.69.refs_0_ = f32[192,1024]{1,0:T(8,128)S(1)} custom-call(bf16[48,384]{1,0:T(8,128)(2,1)S(1)} %get-tuple-element.18.cut, bf16[48,1536]{1,0:T(8,128)(2,1)S(1)} %collective-permute-done.2.refs_3_.rest_across, bf16[192,1024]{1,0:T(8,128)(2,1)S(1)} %shard_map.68.cots), custom_call_target="tpu_custom_call" | custom-call | flops 4294967296 | bytes 1 | tf_op jit(solution)/shard_map/pallas_call | solution.py:192
  16.8 0.0 collective-permute-done.5.refs_1_
  16.9 0.3 collective-permute-done.6.refs_2_
  17.1 1.1 %collective-permute-done.7.refs_3_ = bf16[192,1024]{1,0:T(8,128)(2,1)S(1)} collective-permute-done((bf16[192,1024]{1,0:T(8,128)(2,1)S(1)}, bf16[192,1024]{1,0:T(8,128)(2,1)S(1)}, u32[]{:S(2)}, u32[]{:S(2)}) %collective-permute-start.7) | collective-permute-done | bytes 393248 | tf_op jit(solution)/shard_map/ppermute | solution.py:225
  18.2 0.6 %shard_map.70 = (f32[352,128]{1,0:T(8,128)S(1)}, f32[360,128]{1,0:T(8,128)S(1)}, f32[360,128]{1,0:T(8,128)S(1)}, f32[360,128]{1,0:T(8,128)S(1)}) custom-call(f32[192,1024]{1,0:T(8,128)S(1)} %shard_map.69.refs_0_, bf16[48,384]{1,0:T(8,128)(2,1)S(1)} %collective-permute-done.5.refs_1_, bf16[48,384]{1,0:T(8,128)(2,1)S(1)} %collective-permute-done.6.refs_2_, ...), custom_call_target="tpu_custom_call" | custom-call | flops 1 | bytes 1 | tf_op jit(solution)/shard_map/pallas_call | solution.py:192
  18.8 3.7 %collective-permute-start.10 = (f16[360,128]{1,0:T(8,128)(2,1)S(1)}, f16[360,128]{1,0:T(8,128)(2,1)S(1)}, u32[]{:S(2)}, u32[]{:S(2)}) collective-permute-start(f16[360,128]{1,0:T(8,128)(2,1)S(1)} %convert_element_type.22), channel_id=1, source_target_pairs={{0,24},{2,26},{4,28},{6,30},{8,16},{10,18},{12,20},{14,22},{16,8},... | collective-permute-start | bytes 276488 | tf_op jit(solution)/shard_map/ppermute | solution.py:225
  22.5 0.1 collective-permute-start.9
  22.6 0.8 %collective-permute-start.8 = (f16[360,128]{1,0:T(8,128)(2,1)S(1)}, f16[360,128]{1,0:T(8,128)(2,1)S(1)}, u32[]{:S(2)}, u32[]{:S(2)}) collective-permute-start(f16[360,128]{1,0:T(8,128)(2,1)S(1)} %convert_element_type.18), channel_id=1, source_target_pairs={{0,8},{2,10},{4,12},{6,14},{8,0},{10,2},{12,4},{14,6},{16,24},{18,... | collective-permute-start | bytes 276488 | tf_op jit(solution)/shard_map/ppermute | solution.py:225
  23.3 2.8 %collective-permute-done.10 = f16[360,128]{1,0:T(8,128)(2,1)S(1)} collective-permute-done((f16[360,128]{1,0:T(8,128)(2,1)S(1)}, f16[360,128]{1,0:T(8,128)(2,1)S(1)}, u32[]{:S(2)}, u32[]{:S(2)}) %collective-permute-start.10) | collective-permute-done | bytes 92192 | tf_op jit(solution)/shard_map/ppermute | solution.py:225
  26.2 4.3 %collective-permute-done.9 = f16[360,128]{1,0:T(8,128)(2,1)S(1)} collective-permute-done((f16[360,128]{1,0:T(8,128)(2,1)S(1)}, f16[360,128]{1,0:T(8,128)(2,1)S(1)}, u32[]{:S(2)}, u32[]{:S(2)}) %collective-permute-start.9) | collective-permute-done | bytes 92192 | tf_op jit(solution)/shard_map/ppermute | solution.py:225
  30.5 0.0 collective-permute-done.8
  30.6 0.7 %fusion = f32[352,128]{1,0:T(8,128)} fusion(f32[360,128]{1,0:T(8,128)S(1)} %convert_element_type.23, f32[360,128]{1,0:T(8,128)S(1)} %convert_element_type.21, f32[352,128]{1,0:T(8,128)S(1)} %get-tuple-element.25, f32[360,128]{1,0:T(8,128)S(1)} %convert_element_type.19, f32[128]{0:T(128)S(1)} %fusion.4, f32[128]{0:T(128)S(1)} %fusion.6, f32[128]{0:T(128)S(1)} %fusion.8), kind=kLoop, calls=%fused_computation.1 | loop fusion | flops 270336 | bytes 902656 | tf_op jit(solution)/shard_map/add | solution.py:297
  (9 shorter events, 0.1 us)
Async XLA Ops:
  0.0 6.7 %copy-start = (bf16[1,1,2,48,704]{4,3,2,1,0:T(8,128)(2,1)S(1)}, bf16[1,1,2,48,704]{4,3,2,1,0:T(8,128)(2,1)}, u32[]{:S(2)}) copy-start(bf16[1,1,2,48,704]{4,3,2,1,0:T(8,128)(2,1)} %param.11) | copy-start | bytes 405508
  2.2 6.3 %collective-permute-start.1 = (bf16[48,1152]{1,0:T(8,128)(2,1)}, bf16[48,1152]{1,0:T(8,128)(2,1)S(1)}, u32[]{:S(2)}, u32[]{:S(2)}) collective-permute-start(bf16[48,1152]{1,0:T(8,128)(2,1)} %get-tuple-element.21), channel_id=1, source_target_pairs={{0,1},{1,0},{2,3},{3,2},{4,5},{5,4},{6,7},{7,6},{8,9},{9,8},{10,11... | collective-permute-start | bytes 331784 | tf_op jit(solution)/shard_map/ppermute | solution.py:220
  5.2 5.0 %collective-permute-start = (bf16[48,1152]{1,0:T(8,128)(2,1)}, bf16[48,1152]{1,0:T(8,128)(2,1)S(1)}, u32[]{:S(2)}, u32[]{:S(2)}) collective-permute-start(bf16[48,1152]{1,0:T(8,128)(2,1)} %get-tuple-element.17.refs_0_), channel_id=1, source_target_pairs={{0,4},{2,6},{4,0},{6,2},{8,12},{10,14},{12,8},{14,10},{16,20},{18,... | collective-permute-start | bytes 331784 | tf_op jit(solution)/shard_map/ppermute | solution.py:225
  6.7 0.9 %copy-start.1 = (bf16[48,1152]{1,0:T(8,128)(2,1)S(1)}, bf16[48,1152]{1,0:T(8,128)(2,1)}, u32[]{:S(2)}) copy-start(bf16[48,1152]{1,0:T(8,128)(2,1)} %get-tuple-element.17.refs_0_) | copy-start | bytes 331780
  10.2 5.9 %collective-permute-start.2 = (bf16[48,1536]{1,0:T(8,128)(2,1)S(1)}, bf16[48,1536]{1,0:T(8,128)(2,1)S(1)}, u32[]{:S(2)}, u32[]{:S(2)}) collective-permute-start(bf16[48,1536]{1,0:T(8,128)(2,1)S(1)} %shard_map.67.refs_1_), channel_id=1, source_target_pairs={{0,4},{2,6},{4,0},{6,2},{8,12},{10,14},{12,8},{14,10},{16,20},{18,... | collective-permute-start | bytes 442376 | tf_op jit(solution)/shard_map/ppermute | solution.py:225
  11.7 4.4 %collective-permute-start.4 = (f32[1,128]{1,0:T(1,128)S(1)}, f32[1,128]{1,0:T(1,128)S(1)}, u32[]{:S(2)}, u32[]{:S(2)}) collective-permute-start(f32[1,128]{1,0:T(1,128)S(1)} %shard_map.66.squares.refs_4_), channel_id=1, source_target_pairs={{0,5},{1,4},{2,7},{3,6},{4,1},{5,0},{6,3},{7,2},{8,13},{9,12},{10,... | collective-permute-start | bytes 1544 | tf_op jit(solution)/shard_map/ppermute | solution.py:232
  12.1 4.1 %collective-permute-start.3 = (f32[1,128]{1,0:T(1,128)S(1)}, f32[1,128]{1,0:T(1,128)S(1)}, u32[]{:S(2)}, u32[]{:S(2)}) collective-permute-start(f32[1,128]{1,0:T(1,128)S(1)} %shard_map.66.squares.refs_4_), channel_id=1, source_target_pairs={{0,1},{1,0},{2,3},{3,2},{4,5},{5,4},{6,7},{7,6},{8,9},{9,8},{10,11... | collective-permute-start | bytes 1544 | tf_op jit(solution)/shard_map/ppermute | solution.py:220
  13.7 3.1 %collective-permute-start.5 = (bf16[48,384]{1,0:T(8,128)(2,1)S(1)}, bf16[48,384]{1,0:T(8,128)(2,1)S(1)}, u32[]{:S(2)}, u32[]{:S(2)}) collective-permute-start(bf16[48,384]{1,0:T(8,128)(2,1)S(1)} %get-tuple-element.23), channel_id=1, source_target_pairs={{0,2},{2,0},{4,6},{6,4},{8,10},{10,8},{12,14},{14,12},{16,18},{18,... | collective-permute-start | bytes 110600 | tf_op jit(solution)/shard_map/ppermute | solution.py:225
  13.7 3.4 %collective-permute-start.6 = (bf16[48,384]{1,0:T(8,128)(2,1)S(1)}, bf16[48,384]{1,0:T(8,128)(2,1)S(1)}, u32[]{:S(2)}, u32[]{:S(2)}) collective-permute-start(bf16[48,384]{1,0:T(8,128)(2,1)S(1)} %get-tuple-element.24), channel_id=1, source_target_pairs={{0,6},{2,4},{4,2},{6,0},{8,14},{10,12},{12,10},{14,8},{16,22},{18,... | collective-permute-start | bytes 110600 | tf_op jit(solution)/shard_map/ppermute | solution.py:225
  16.4 1.8 %collective-permute-start.7 = (bf16[192,1024]{1,0:T(8,128)(2,1)S(1)}, bf16[192,1024]{1,0:T(8,128)(2,1)S(1)}, u32[]{:S(2)}, u32[]{:S(2)}) collective-permute-start(bf16[192,1024]{1,0:T(8,128)(2,1)S(1)} %shard_map.68.cots), channel_id=1, source_target_pairs={{0,2},{2,0},{4,6},{6,4},{8,10},{10,8},{12,14},{14,12},{16,18},{18,... | collective-permute-start | bytes 1179656 | tf_op jit(solution)/shard_map/ppermute | solution.py:225
  18.8 7.4 %collective-permute-start.10 = (f16[360,128]{1,0:T(8,128)(2,1)S(1)}, f16[360,128]{1,0:T(8,128)(2,1)S(1)}, u32[]{:S(2)}, u32[]{:S(2)}) collective-permute-start(f16[360,128]{1,0:T(8,128)(2,1)S(1)} %convert_element_type.22), channel_id=1, source_target_pairs={{0,24},{2,26},{4,28},{6,30},{8,16},{10,18},{12,20},{14,22},{16,8},... | collective-permute-start | bytes 276488 | tf_op jit(solution)/shard_map/ppermute | solution.py:225
  22.5 8.0 %collective-permute-start.9 = (f16[360,128]{1,0:T(8,128)(2,1)S(1)}, f16[360,128]{1,0:T(8,128)(2,1)S(1)}, u32[]{:S(2)}, u32[]{:S(2)}) collective-permute-start(f16[360,128]{1,0:T(8,128)(2,1)S(1)} %convert_element_type.20), channel_id=1, source_target_pairs={{0,16},{2,18},{4,20},{6,22},{8,24},{10,26},{12,28},{14,30},{16,0},... | collective-permute-start | bytes 276488 | tf_op jit(solution)/shard_map/ppermute | solution.py:225
  22.6 8.0 %collective-permute-start.8 = (f16[360,128]{1,0:T(8,128)(2,1)S(1)}, f16[360,128]{1,0:T(8,128)(2,1)S(1)}, u32[]{:S(2)}, u32[]{:S(2)}) collective-permute-start(f16[360,128]{1,0:T(8,128)(2,1)S(1)} %convert_element_type.18), channel_id=1, source_target_pairs={{0,8},{2,10},{4,12},{6,14},{8,0},{10,2},{12,4},{14,6},{16,24},{18,... | collective-permute-start | bytes 276488 | tf_op jit(solution)/shard_map/ppermute | solution.py:225

commit v2 on v1

--- a/solution.py
+++ b/solution.py
@@ -16,9 +16,9 @@
     return lax.broadcasted_iota(jnp.int32, shape, axis)
 
 
-def build(sources, cap, routes_at, weights_at, ids_at, loss_at, grad_at, *refs):
+def build(sources, cap, n_dp, pad, routes_at, weights_at, ids_at, loss_at, grad_at, hidden_at, *refs):
     blocks = refs[:sources]
-    routes, weights, ids, loss, grad, sems = refs[sources:]
+    routes, weights, ids, loss, grad, hidden, sems = refs[sources:]
     fetches = [
         pltpu.make_async_copy(source, target, sems.at[i])
         for i, (source, target) in enumerate(
@@ -27,6 +27,7 @@
                 (ids_at, ids),
                 (loss_at, loss),
                 (weights_at, weights),
+                (hidden_at, hidden),
                 (grad_at, grad),
             ]
         )
@@ -59,16 +60,21 @@
         code = jnp.sum(placed * token_code, axis=1, keepdims=True)
         ready.append((placed.astype(BF16), slot_scale, code))
     fetches[4].wait()
+    at = width + LANES
+    for units in cuts_of(sources, n_dp, pad, hidden, (2, 3)):
+        for j in range(sources):
+            blocks[0][:, at : at + units.shape[1]] = units[j * cap : (j + 1) * cap]
+            at += units.shape[1]
+    fetches[5].wait()
     for k in range(sources):
         placed, slot_scale, code = ready[k]
         rows = jnp.dot(placed, grad[...], preferred_element_type=F32)
         rows = (rows * slot_scale).astype(BF16)
         blocks[k][:, :width] = rows
-        blocks[k][:, width:] = jnp.broadcast_to(code, (cap, LANES)).astype(BF16)
-
-
-def stage(sources, n_dp, pad, block, hidden, own, left, *cuts):
-    own[...] = block[...]
+        blocks[k][:, width : width + LANES] = jnp.broadcast_to(code, (cap, LANES)).astype(BF16)
+
+
+def cuts_of(sources, n_dp, pad, hidden, mates):
     me, rank = lax.axis_index("expert"), lax.axis_index("dp")
     spread = n_dp // MATES
     cap, ff = hidden.shape[1:]
@@ -82,15 +88,21 @@
     unit = iota((ff, spread * pad), 0)
     acts = [hidden[lax.rem(me + j, sources)] for j in range(sources)]
     acts = jnp.concatenate(acts, axis=0)
+    units = []
+    for k in mates:
+        pick = jnp.where(unit == wanted + (low ^ k) * rows, 1.0, 0.0).astype(BF16)
+        units.append(jnp.dot(acts, pick, preferred_element_type=F32).astype(BF16))
+    return units
+
+
+def stage(sources, n_dp, pad, block, hidden, own, left, cut, sibling_cut):
+    own[...] = block[:, : own.shape[1]]
+    me = lax.axis_index("expert")
+    acts = jnp.concatenate([hidden[lax.rem(me + j, sources)] for j in range(sources)], axis=0)
     left[...] = lax.dot_general(
         acts, acts, (((1,), (1,)), ((), ())), preferred_element_type=F32
     )
-    for k in range(MATES):
-        pick = jnp.where(unit == wanted + (low ^ k) * rows, 1.0, 0.0).astype(BF16)
-        units = jnp.dot(acts, pick, preferred_element_type=F32).astype(BF16)
-        for j in range(sources):
-            at = slice(j * spread * pad, (j + 1) * spread * pad)
-            cuts[k][:, at] = units[j * cap : (j + 1) * cap]
+    cut[...], sibling_cut[...] = cuts_of(sources, n_dp, pad, hidden, (0, 1))
 
 
 def chosen(codes):
@@ -113,16 +125,17 @@
     squares[...] = jnp.sum(per_slot * member, axis=0, keepdims=True)
 
 
-def pass_on(across, squares, cut, *refs):
+def after(across, squares, out):
+    out[...] = squares[...]
+
+
+def pass_on(squares, *refs):
     takes, rest = refs[:-1], refs[-1]
     cap, wide = takes[0].shape
     half = LANES // 2
     for j, take in enumerate(takes):
         part = slice(j * cap, (j + 1) * cap)
-        rest[part, :wide] = take[...]
-        if j:
-            rest[part, wide:] = jnp.zeros((cap, rest.shape[1] - wide), BF16)
-    rest[:cap, wide:] = cut[...]
+        rest[part] = take[...]
     value = jnp.broadcast_to(squares[...], (cap, LANES))
     high = value.astype(BF16).astype(F32)
     middle = (value - high).astype(BF16).astype(F32)
@@ -132,7 +145,7 @@
     rest[:cap, wide - half : wide] = three[:, :half]
 
 
-def pack(sources, count, own, rest, across, rest_across, *refs):
+def pack(sources, count, own, rest, across, rest_across, sibling_cut, *refs):
     near, far, out = refs[:sources], refs[sources:-1], refs[-1]
     width = own.shape[1] - LANES
     half = LANES // 2
@@ -147,33 +160,36 @@
         mine = chosen(block[:, width : width + 1])
         weight = jnp.sum(jnp.where(mine, clip, 0.0), axis=1, keepdims=True) / EXAMPLES
         scaled = (weight * block[:, :width].astype(F32)).astype(BF16)
-        out[at : at + mine.shape[0]] = scaled
+        out[at : at + mine.shape[0], :width] = scaled
         at += mine.shape[0]
-
-
-def multiply(cuts, cots, units):
-    at, cap, across = 0, cuts[0].shape[0], units.shape[1]
-    for cut in cuts:
-        for j in range(cut.shape[1] // across):
-            units[at : at + cap] = cut[:, j * across : (j + 1) * across]
-            at += cap
+    slots, lanes = sibling_cut.shape
+    cap = own.shape[0]
+    out[:slots, width:] = sibling_cut[...]
+    for j in range(sources):
+        first = width + LANES + (sources + j) * lanes
+        out[slots + j * cap : slots + (j + 1) * cap, width:] = across[:, first : first + lanes]
+
+
+def multiply(units, cots):
     return lax.dot_general(
-        units[...], cots[...], (((0,), (0,)), ((), ())), preferred_element_type=F32
-    )
-
-
-def near_product(cut, rest_across, cots, out, units):
-    first = cots.shape[1] + LANES
-    cap = cut.shape[0]
-    across = rest_across.at[:cap, first : first + cut.shape[1]]
-    out[...] = multiply([cut, across], cots, units)
-
-
-def product(rows, pad, start, cut, across, cots, keep, *refs):
-    leave, units = refs[:-1], refs[-1]
-    width = cots.shape[1]
+        units, cots, (((0,), (0,)), ((), ())), preferred_element_type=F32
+    )
+
+
+def near_product(sources, cut, across, cots, out):
+    lanes = cut.shape[1]
+    width = cots.shape[1] - lanes
+    first = width + LANES
+    units = [cut[...]] + [
+        across[:, first + j * lanes : first + (j + 1) * lanes] for j in range(sources)
+    ]
+    out[...] = multiply(jnp.concatenate(units, axis=0), cots[:, :width])
+
+
+def product(rows, pad, start, cots, keep, *leave):
+    width = start.shape[1]
     pieces = width // LANES
-    part = start[...] + multiply([cut, across], cots, units)
+    part = start[...] + multiply(cots[:, width:], cots[:, :width])
     for p, out in enumerate([keep, *leave]):
         values = part[p * pad : p * pad + rows]
         if p:
@@ -232,10 +248,11 @@
         return lax.ppermute(array, ("dp", "expert"), pairs)
 
     block, *gives = call(
-        lambda *refs: build(sources, cap, *refs),
-        [shape((cap, width + LANES), BF16)] * sources,
-        (routes.T, route_weight.T, example_ids, example_weight, grad_out),
-        fetched=range(5),
+        lambda *refs: build(sources, cap, n_dp, pad, *refs),
+        [shape((cap, width + LANES + 2 * sources * across), BF16)]
+        + [shape((cap, width + LANES), BF16)] * (sources - 1),
+        (routes.T, route_weight.T, example_ids, example_weight, grad_out, acts),
+        fetched=range(6),
         limit=60,
         scratch=(
             pltpu.VMEM((top, tokens), jnp.int32),
@@ -243,15 +260,16 @@
             pltpu.VMEM((1, tokens), jnp.int32),
             pltpu.SMEM((1, EXAMPLES), F32),
             pltpu.VMEM((tokens, width), BF16),
-            pltpu.SemaphoreType.DMA((5,)),
+            pltpu.VMEM((sources, cap, ff), BF16),
+            pltpu.SemaphoreType.DMA((6,)),
         ),
     )
     takes = [over_experts(g, k + 1) for k, g in enumerate(gives)]
     block_across = over_dp(block, 2)
-    own, left, *cuts = call(
+    own, left, cut, sibling_cut = call(
         lambda *refs: stage(sources, n_dp, pad, *refs),
         [shape((cap, width + LANES), BF16), shape((slots, slots), F32)]
-        + [shape((cap, sources * across), BF16)] * MATES,
+        + [shape((slots, across), BF16)] * 2,
         (block, acts),
         flops=1 << 32,
     )
@@ -263,24 +281,25 @@
     )
     (rest,) = call(
         pass_on,
-        [shape((slots - cap, width + LANES + sources * across), BF16)],
-        (block_across, squares, cuts[2], *takes),
-        fetched=(0,),
+        [shape((slots - cap, width + LANES), BF16)],
+        (squares, *takes),
+    )
+    (late_squares,) = call(
+        after, [shape((1, LANES), F32)], (block_across, squares), fetched=(0,)
     )
     rest_across = over_dp(rest, 2)
     near_squares = [squares] + [over_experts(squares, k) for k in range(1, sources)]
-    far_squares = [over_both(squares, k) for k in range(1, sources)]
+    far_squares = [over_both(late_squares, k) for k in range(1, sources)]
     (cots,) = call(
         lambda *refs: pack(sources, ff * width, *refs),
-        [shape((2 * slots, width), BF16)],
-        (own, rest, block_across, rest_across, *near_squares, *far_squares),
+        [shape((2 * slots, width + across), BF16)],
+        (own, rest, block_across, rest_across, sibling_cut, *near_squares, *far_squares),
     )
     other_cots = over_dp(cots, 1)
     (start,) = call(
-        near_product,
+        lambda *refs: near_product(sources, *refs),
         [shape((across, width), F32)],
-        (cuts[0], rest_across, cots),
-        scratch=(pltpu.VMEM((2 * slots, across), BF16),),
+        (cut, block_across, cots),
         flops=1 << 32,
     )
 
@@ -289,8 +308,7 @@
     part, *leave = call(
         lambda *refs: product(rows, pad, *refs),
         [shape((held if p == 0 else sent, LANES), F32) for p in range(spread)],
-        (start, over_dp(cuts[1], 1), over_dp(cuts[3], 3), other_cots),
-        scratch=(pltpu.VMEM((2 * slots, across), BF16),),
+        (start, other_cots),
     )
     for p in range(1, spread):
         got = over_dp(leave[p - 1].astype(jnp.float16), p * MATES).astype(F32)

time: 31.4 us -> 32.3 us (1.029)
  waiting for transfers between devices: 10.9 us -> 12.9 us
  starting transfers between devices: 14.2 us -> 13.1 us
    ppermute x1, waiting for transfers between devices: 0.83 us -> 2.48 us  [over_both(): return lax.ppermute(array, ('dp', 'expert'), pairs)]
    ppermute x2, waiting for transfers between devices: 0.28 us -> 1.7 us  [over_experts(): lax.ppermute(array, 'expert', [(s, (s - k) % sources) for s in range(sour...]
    ppermute x8 -> x6, starting transfers between devices: 9.18 us -> 7.8 us  [over_dp(): return lax.ppermute(array, 'dp', [(i, i ^ k) for i in range(n_dp)])]
    ppermute x8 -> x6, waiting for transfers between devices: 9.81 us -> 8.77 us  [over_dp(): return lax.ppermute(array, 'dp', [(i, i ^ k) for i in range(n_dp)])]
    ppermute x1, starting transfers between devices: 0.37 us -> 0.76 us  [over_both(): return lax.ppermute(array, ('dp', 'expert'), pairs)]
    pallas_call x7 -> x8, Pallas kernels: 4.24 us -> 4.16 us  [call(): pl.pallas_call(body, out_shape=tuple(outs), in_specs=[anywhere if i in fe...]
  transfers between devices with their start and end apart: 11 -> 9, of which waited for: 7 -> 7; matrix products, arithmetic and copies ran while one was open for 0% -> 0% of each run, Pallas kernels for 5% -> 3%
where the time goes in v2:
time: 32.3 us; the launch traced here: 32.2 us
  starting transfers between devices  13.1 us (41%)
  waiting for transfers between devices  12.9 us (40%)
  Pallas kernels  4.16 us (13%)
  local copies, waits for them, and re-layouts  0.96 us (3%)
  other arithmetic  0.84 us (3%)
    ppermute x6, waiting for transfers between devices, over_dp(): return lax.ppermute(array, 'dp', [(i, i ^ k) for i in range(n_dp)])  8.77 us
    ppermute x6, starting transfers between devices, over_dp(): return lax.ppermute(array, 'dp', [(i, i ^ k) for i in range(n_dp)])  7.8 us
    ppermute x2, starting transfers between devices, over_experts(): lax.ppermute(array, 'expert', [(s, (s - k) % sources) for s in range(sour...  4.56 us
    pallas_call x8, Pallas kernels, call(): pl.pallas_call(body, out_shape=tuple(outs), in_specs=[anywhere if i in fe...  4.16 us
    ppermute x1, waiting for transfers between devices, over_both(): return lax.ppermute(array, ('dp', 'expert'), pairs)  2.48 us
    ppermute x2, waiting for transfers between devices, over_experts(): lax.ppermute(array, 'expert', [(s, (s - k) % sources) for s in range(sour...  1.7 us
    unnamed x4, local copies, waits for them, and re-layouts  0.96 us
    ppermute x1, starting transfers between devices, over_both(): return lax.ppermute(array, ('dp', 'expert'), pairs)  0.76 us
  transfers between devices with their start and end apart: 9, of which 7 were waited for; matrix products, arithmetic and copies ran while one was open for 0% of the time, Pallas kernels for 3%

profile of v2, /device:TPU:0, one launch (start us, length us, event | category | flops | bytes accessed | tf_op | source)
XLA Modules:
  0.0 32.2 jit_solution(16690551043899085454)
XLA Ops:
  0.0 0.0 copy-start
  0.0 2.3 %shard_map.64 = (bf16[48,1920]{1,0:T(8,128)(2,1)}, bf16[48,1152]{1,0:T(8,128)(2,1)}) custom-call(s32[6,256]{1,0:T(8,128)} %bitcast.12, f32[6,256]{1,0:T(8,128)} %bitcast.13, s32[1,256]{1,0:T(1,128)} %refs_2_.1, f32[1,8]{1,0:T(1,128)} %refs_3_.1, bf16[256,1024]{1,0:T(8,128)(2,1)} %refs_4_.1, bf16[2,48,704]{2,1,0:T(8,128)(2,1)} %bitcast.10), custom_call_target="tpu_custom_call" | custom-call | flops 1 | bytes 1 | tf_op jit(solution)/shard_map/pallas_call | solution.py:208
  2.4 3.0 %collective-permute-start.1 = (bf16[48,1152]{1,0:T(8,128)(2,1)}, bf16[48,1152]{1,0:T(8,128)(2,1)S(1)}, u32[]{:S(2)}, u32[]{:S(2)}) collective-permute-start(bf16[48,1152]{1,0:T(8,128)(2,1)} %get-tuple-element.19), channel_id=1, source_target_pairs={{0,1},{1,0},{2,3},{3,2},{4,5},{5,4},{6,7},{7,6},{8,9},{9,8},{10,11... | collective-permute-start | bytes 331784 | tf_op jit(solution)/shard_map/ppermute | solution.py:236
  5.4 1.5 %collective-permute-start = (bf16[48,1920]{1,0:T(8,128)(2,1)}, bf16[48,1920]{1,0:T(8,128)(2,1)S(1)}, u32[]{:S(2)}, u32[]{:S(2)}) collective-permute-start(bf16[48,1920]{1,0:T(8,128)(2,1)} %get-tuple-element.15.refs_0_), channel_id=1, source_target_pairs={{0,4},{2,6},{4,0},{6,2},{8,12},{10,14},{12,8},{14,10},{16,20},{18,... | collective-permute-start | bytes 552968 | tf_op jit(solution)/shard_map/ppermute | solution.py:241
  6.9 0.0 copy-done
  6.9 0.0 copy-start.1
  6.9 1.0 %copy-done.1 = bf16[48,1920]{1,0:T(8,128)(2,1)S(1)} copy-done((bf16[48,1920]{1,0:T(8,128)(2,1)S(1)}, bf16[48,1920]{1,0:T(8,128)(2,1)}, u32[]{:S(2)}) %copy-start.1) | copy-done | bytes 184344
  7.8 0.3 shard_map.65
  8.2 0.5 %collective-permute-done.1.refs_2_.refs_0_ = bf16[48,1152]{1,0:T(8,128)(2,1)S(1)} collective-permute-done((bf16[48,1152]{1,0:T(8,128)(2,1)}, bf16[48,1152]{1,0:T(8,128)(2,1)S(1)}, u32[]{:S(2)}, u32[]{:S(2)}) %collective-permute-start.1) | collective-permute-done | bytes 110624 | tf_op jit(solution)/shard_map/ppermute | solution.py:236
  8.7 0.3 %shard_map.66.squares.refs_5_ = f32[1,128]{1,0:T(1,128)S(1)} custom-call(f32[96,96]{1,0:T(8,128)S(1)} %get-tuple-element.18.refs_0_, bf16[48,1152]{1,0:T(8,128)(2,1)S(1)} %get-tuple-element.17.refs_1_.refs_0_, bf16[48,1152]{1,0:T(8,128)(2,1)S(1)} %collective-permute-done.1.refs_2_.refs_0_), custom_call_target="tpu_custom_call" | custom-call | flops 4294967296 | bytes 1 | tf_op jit(solution)/shard_map/pallas_call | solution.py:208
  9.0 0.1 shard_map.67.refs_1_
  9.1 1.7 %collective-permute-start.2 = (bf16[48,1152]{1,0:T(8,128)(2,1)S(1)}, bf16[48,1152]{1,0:T(8,128)(2,1)S(1)}, u32[]{:S(2)}, u32[]{:S(2)}) collective-permute-start(bf16[48,1152]{1,0:T(8,128)(2,1)S(1)} %shard_map.67.refs_1_), channel_id=1, source_target_pairs={{0,4},{2,6},{4,0},{6,2},{8,12},{10,14},{12,8},{14,10},{16,20},{18,... | collective-permute-start | bytes 331784 | tf_op jit(solution)/shard_map/ppermute | solution.py:241
  10.8 1.5 %collective-permute-start.3 = (f32[1,128]{1,0:T(1,128)S(1)}, f32[1,128]{1,0:T(1,128)S(1)}, u32[]{:S(2)}, u32[]{:S(2)}) collective-permute-start(f32[1,128]{1,0:T(1,128)S(1)} %shard_map.66.squares.refs_5_), channel_id=1, source_target_pairs={{0,1},{1,0},{2,3},{3,2},{4,5},{5,4},{6,7},{7,6},{8,9},{9,8},{10,11... | collective-permute-start | bytes 1544 | tf_op jit(solution)/shard_map/ppermute | solution.py:236
  12.3 0.1 collective-permute-done.across.refs_2_.refs_1_
  12.4 0.8 %collective-permute-start.4 = (f32[1,128]{1,0:T(1,128)S(1)}, f32[1,128]{1,0:T(1,128)S(1)}, u32[]{:S(2)}, u32[]{:S(2)}) collective-permute-start(f32[1,128]{1,0:T(1,128)S(1)} %shard_map.68), channel_id=1, source_target_pairs={{0,5},{1,4},{2,7},{3,6},{4,1},{5,0},{6,3},{7,2},{8,13},{9,12},{10,... | collective-permute-start | bytes 1544 | tf_op jit(solution)/shard_map/ppermute | solution.py:248
  13.1 1.2 %collective-permute-done.3.refs_6_ = f32[1,128]{1,0:T(1,128)S(1)} collective-permute-done((f32[1,128]{1,0:T(1,128)S(1)}, f32[1,128]{1,0:T(1,128)S(1)}, u32[]{:S(2)}, u32[]{:S(2)}) %collective-permute-start.3) | collective-permute-done | bytes 544 | tf_op jit(solution)/shard_map/ppermute | solution.py:236
  14.3 2.5 %collective-permute-done.4.refs_7_ = f32[1,128]{1,0:T(1,128)S(1)} collective-permute-done((f32[1,128]{1,0:T(1,128)S(1)}, f32[1,128]{1,0:T(1,128)S(1)}, u32[]{:S(2)}, u32[]{:S(2)}) %collective-permute-start.4) | collective-permute-done | bytes 544 | tf_op jit(solution)/shard_map/ppermute | solution.py:248
  16.8 0.0 collective-permute-done.2.refs_3_
  16.8 0.3 shard_map.69.refs_2_
  17.1 0.1 collective-permute-start.5
  17.2 0.3 %shard_map.70.refs_0_ = f32[192,1024]{1,0:T(8,128)S(1)} custom-call(bf16[96,192]{1,0:T(8,128)(2,1)S(1)} %get-tuple-element.16.refs_0_, bf16[48,1920]{1,0:T(8,128)(2,1)S(1)} %collective-permute-done.across.refs_2_.refs_1_, bf16[192,1216]{1,0:T(8,128)(2,1)S(1)} %shard_map.69.refs_2_), custom_call_target="tpu_custom_call" | custom-call | flops 4294967296 | bytes 1 | tf_op jit(solution)/shard_map/pallas_call | solution.py:208
  17.5 1.5 %collective-permute-done.5.refs_1_ = bf16[192,1216]{1,0:T(8,128)(2,1)S(1)} collective-permute-done((bf16[192,1216]{1,0:T(8,128)(2,1)S(1)}, bf16[192,1216]{1,0:T(8,128)(2,1)S(1)}, u32[]{:S(2)}, u32[]{:S(2)}) %collective-permute-start.5) | collective-permute-done | bytes 466976 | tf_op jit(solution)/shard_map/ppermute | solution.py:241
  19.0 0.5 %shard_map.71 = (f32[352,128]{1,0:T(8,128)S(1)}, f32[360,128]{1,0:T(8,128)S(1)}, f32[360,128]{1,0:T(8,128)S(1)}, f32[360,128]{1,0:T(8,128)S(1)}) custom-call(f32[192,1024]{1,0:T(8,128)S(1)} %shard_map.70.refs_0_, bf16[192,1216]{1,0:T(8,128)(2,1)S(1)} %collective-permute-done.5.refs_1_), custom_call_target="tpu_custom_call" | custom-call | flops 1 | bytes 1 | tf_op jit(solution)/shard_map/pallas_call | solution.py:208
  19.5 3.8 %collective-permute-start.8 = (f16[360,128]{1,0:T(8,128)(2,1)S(1)}, f16[360,128]{1,0:T(8,128)(2,1)S(1)}, u32[]{:S(2)}, u32[]{:S(2)}) collective-permute-start(f16[360,128]{1,0:T(8,128)(2,1)S(1)} %convert_element_type.22), channel_id=1, source_target_pairs={{0,24},{2,26},{4,28},{6,30},{8,16},{10,18},{12,20},{14,22},{16,8},... | collective-permute-start | bytes 276488 | tf_op jit(solution)/shard_map/ppermute | solution.py:241
  23.4 0.1 collective-permute-start.7
  23.4 0.7 %collective-permute-start.6 = (f16[360,128]{1,0:T(8,128)(2,1)S(1)}, f16[360,128]{1,0:T(8,128)(2,1)S(1)}, u32[]{:S(2)}, u32[]{:S(2)}) collective-permute-start(f16[360,128]{1,0:T(8,128)(2,1)S(1)} %convert_element_type.18), channel_id=1, source_target_pairs={{0,8},{2,10},{4,12},{6,14},{8,0},{10,2},{12,4},{14,6},{16,24},{18,... | collective-permute-start | bytes 276488 | tf_op jit(solution)/shard_map/ppermute | solution.py:241
  24.1 2.9 %collective-permute-done.8 = f16[360,128]{1,0:T(8,128)(2,1)S(1)} collective-permute-done((f16[360,128]{1,0:T(8,128)(2,1)S(1)}, f16[360,128]{1,0:T(8,128)(2,1)S(1)}, u32[]{:S(2)}, u32[]{:S(2)}) %collective-permute-start.8) | collective-permute-done | bytes 92192 | tf_op jit(solution)/shard_map/ppermute | solution.py:241
  27.0 4.3 %collective-permute-done.7 = f16[360,128]{1,0:T(8,128)(2,1)S(1)} collective-permute-done((f16[360,128]{1,0:T(8,128)(2,1)S(1)}, f16[360,128]{1,0:T(8,128)(2,1)S(1)}, u32[]{:S(2)}, u32[]{:S(2)}) %collective-permute-start.7) | collective-permute-done | bytes 92192 | tf_op jit(solution)/shard_map/ppermute | solution.py:241
  31.4 0.0 collective-permute-done.6
  31.4 0.7 %fusion = f32[352,128]{1,0:T(8,128)} fusion(f32[360,128]{1,0:T(8,128)S(1)} %convert_element_type.23, f32[360,128]{1,0:T(8,128)S(1)} %convert_element_type.21, f32[352,128]{1,0:T(8,128)S(1)} %get-tuple-element.21, f32[360,128]{1,0:T(8,128)S(1)} %convert_element_type.19, f32[128]{0:T(128)S(1)} %fusion.4, f32[128]{0:T(128)S(1)} %fusion.6, f32[128]{0:T(128)S(1)} %fusion.8), kind=kLoop, calls=%fused_computation.1 | loop fusion | flops 270336 | bytes 902656 | tf_op jit(solution)/shard_map/add | solution.py:315
  (10 shorter events, 0.1 us)
Async XLA Ops:
  0.0 6.9 %copy-start = (bf16[1,1,2,48,704]{4,3,2,1,0:T(8,128)(2,1)S(1)}, bf16[1,1,2,48,704]{4,3,2,1,0:T(8,128)(2,1)}, u32[]{:S(2)}) copy-start(bf16[1,1,2,48,704]{4,3,2,1,0:T(8,128)(2,1)} %param.11) | copy-start | bytes 405508
  2.4 6.3 %collective-permute-start.1 = (bf16[48,1152]{1,0:T(8,128)(2,1)}, bf16[48,1152]{1,0:T(8,128)(2,1)S(1)}, u32[]{:S(2)}, u32[]{:S(2)}) collective-permute-start(bf16[48,1152]{1,0:T(8,128)(2,1)} %get-tuple-element.19), channel_id=1, source_target_pairs={{0,1},{1,0},{2,3},{3,2},{4,5},{5,4},{6,7},{7,6},{8,9},{9,8},{10,11... | collective-permute-start | bytes 331784 | tf_op jit(solution)/shard_map/ppermute | solution.py:236
  5.4 7.0 %collective-permute-start = (bf16[48,1920]{1,0:T(8,128)(2,1)}, bf16[48,1920]{1,0:T(8,128)(2,1)S(1)}, u32[]{:S(2)}, u32[]{:S(2)}) collective-permute-start(bf16[48,1920]{1,0:T(8,128)(2,1)} %get-tuple-element.15.refs_0_), channel_id=1, source_target_pairs={{0,4},{2,6},{4,0},{6,2},{8,12},{10,14},{12,8},{14,10},{16,20},{18,... | collective-permute-start | bytes 552968 | tf_op jit(solution)/shard_map/ppermute | solution.py:241
  6.9 1.0 %copy-start.1 = (bf16[48,1920]{1,0:T(8,128)(2,1)S(1)}, bf16[48,1920]{1,0:T(8,128)(2,1)}, u32[]{:S(2)}) copy-start(bf16[48,1920]{1,0:T(8,128)(2,1)} %get-tuple-element.15.refs_0_) | copy-start | bytes 552964
  9.1 7.7 %collective-permute-start.2 = (bf16[48,1152]{1,0:T(8,128)(2,1)S(1)}, bf16[48,1152]{1,0:T(8,128)(2,1)S(1)}, u32[]{:S(2)}, u32[]{:S(2)}) collective-permute-start(bf16[48,1152]{1,0:T(8,128)(2,1)S(1)} %shard_map.67.refs_1_), channel_id=1, source_target_pairs={{0,4},{2,6},{4,0},{6,2},{8,12},{10,14},{12,8},{14,10},{16,20},{18,... | collective-permute-start | bytes 331784 | tf_op jit(solution)/shard_map/ppermute | solution.py:241
  10.8 3.5 %collective-permute-start.3 = (f32[1,128]{1,0:T(1,128)S(1)}, f32[1,128]{1,0:T(1,128)S(1)}, u32[]{:S(2)}, u32[]{:S(2)}) collective-permute-start(f32[1,128]{1,0:T(1,128)S(1)} %shard_map.66.squares.refs_5_), channel_id=1, source_target_pairs={{0,1},{1,0},{2,3},{3,2},{4,5},{5,4},{6,7},{7,6},{8,9},{9,8},{10,11... | collective-permute-start | bytes 1544 | tf_op jit(solution)/shard_map/ppermute | solution.py:236
  12.4 4.4 %collective-permute-start.4 = (f32[1,128]{1,0:T(1,128)S(1)}, f32[1,128]{1,0:T(1,128)S(1)}, u32[]{:S(2)}, u32[]{:S(2)}) collective-permute-start(f32[1,128]{1,0:T(1,128)S(1)} %shard_map.68), channel_id=1, source_target_pairs={{0,5},{1,4},{2,7},{3,6},{4,1},{5,0},{6,3},{7,2},{8,13},{9,12},{10,... | collective-permute-start | bytes 1544 | tf_op jit(solution)/shard_map/ppermute | solution.py:248
  17.1 1.9 %collective-permute-start.5 = (bf16[192,1216]{1,0:T(8,128)(2,1)S(1)}, bf16[192,1216]{1,0:T(8,128)(2,1)S(1)}, u32[]{:S(2)}, u32[]{:S(2)}) collective-permute-start(bf16[192,1216]{1,0:T(8,128)(2,1)S(1)} %shard_map.69.refs_2_), channel_id=1, source_target_pairs={{0,2},{2,0},{4,6},{6,4},{8,10},{10,8},{12,14},{14,12},{16,18},{18,... | collective-permute-start | bytes 1400840 | tf_op jit(solution)/shard_map/ppermute | solution.py:241
  19.5 7.4 %collective-permute-start.8 = (f16[360,128]{1,0:T(8,128)(2,1)S(1)}, f16[360,128]{1,0:T(8,128)(2,1)S(1)}, u32[]{:S(2)}, u32[]{:S(2)}) collective-permute-start(f16[360,128]{1,0:T(8,128)(2,1)S(1)} %convert_element_type.22), channel_id=1, source_target_pairs={{0,24},{2,26},{4,28},{6,30},{8,16},{10,18},{12,20},{14,22},{16,8},... | collective-permute-start | bytes 276488 | tf_op jit(solution)/shard_map/ppermute | solution.py:241
  23.4 8.0 %collective-permute-start.7 = (f16[360,128]{1,0:T(8,128)(2,1)S(1)}, f16[360,128]{1,0:T(8,128)(2,1)S(1)}, u32[]{:S(2)}, u32[]{:S(2)}) collective-permute-start(f16[360,128]{1,0:T(8,128)(2,1)S(1)} %convert_element_type.20), channel_id=1, source_target_pairs={{0,16},{2,18},{4,20},{6,22},{8,24},{10,26},{12,28},{14,30},{16,0},... | collective-permute-start | bytes 276488 | tf_op jit(solution)/shard_map/ppermute | solution.py:241
  23.4 7.9 %collective-permute-start.6 = (f16[360,128]{1,0:T(8,128)(2,1)S(1)}, f16[360,128]{1,0:T(8,128)(2,1)S(1)}, u32[]{:S(2)}, u32[]{:S(2)}) collective-permute-start(f16[360,128]{1,0:T(8,128)(2,1)S(1)} %convert_element_type.18), channel_id=1, source_target_pairs={{0,8},{2,10},{4,12},{6,14},{8,0},{10,2},{12,4},{14,6},{16,24},{18,... | collective-permute-start | bytes 276488 | tf_op jit(solution)/shard_map/ppermute | solution.py:241

commit v3 on v1

--- a/solution.py
+++ b/solution.py
@@ -17,8 +17,8 @@
 
 
 def build(sources, cap, routes_at, weights_at, ids_at, loss_at, grad_at, *refs):
-    blocks = refs[:sources]
-    routes, weights, ids, loss, grad, sems = refs[sources:]
+    alone, blocks = refs[0], refs[1 : sources + 1]
+    routes, weights, ids, loss, grad, sems = refs[sources + 1 :]
     fetches = [
         pltpu.make_async_copy(source, target, sems.at[i])
         for i, (source, target) in enumerate(
@@ -64,6 +64,8 @@
         rows = jnp.dot(placed, grad[...], preferred_element_type=F32)
         rows = (rows * slot_scale).astype(BF16)
         blocks[k][:, :width] = rows
+        if k == 0:
+            alone[...] = rows
         blocks[k][:, width:] = jnp.broadcast_to(code, (cap, LANES)).astype(BF16)
 
 
@@ -113,38 +115,52 @@
     squares[...] = jnp.sum(per_slot * member, axis=0, keepdims=True)
 
 
-def pass_on(across, squares, cut, *refs):
+def diagonal(cap):
+    return iota((cap, LANES), 0) == iota((cap, LANES), 1)
+
+
+def pass_on(rows, pad, across, own, squares, cut, *refs):
     takes, rest = refs[:-1], refs[-1]
-    cap, wide = takes[0].shape
-    half = LANES // 2
+    cap, width = own.shape[0], own.shape[1] - LANES
+    value = jnp.where(diagonal(cap), squares[...], 0.0)
+    value = jnp.sum(value, axis=1, keepdims=True)
+    high = value.astype(BF16).astype(F32)
+    middle = (value - high).astype(BF16).astype(F32)
+    lane = iota(cut.shape, 1)
+    tail = cut[...].astype(F32)
+    for at, column in (
+        (pad + rows, own[:, width : width + 1].astype(F32)),
+        (rows + 1, high),
+        (rows + 2, middle),
+        (rows + 3, value - high - middle),
+    ):
+        tail = jnp.where(lane == at, column, tail)
     for j, take in enumerate(takes):
         part = slice(j * cap, (j + 1) * cap)
-        rest[part, :wide] = take[...]
-        if j:
-            rest[part, wide:] = jnp.zeros((cap, rest.shape[1] - wide), BF16)
-    rest[:cap, wide:] = cut[...]
-    value = jnp.broadcast_to(squares[...], (cap, LANES))
-    high = value.astype(BF16).astype(F32)
-    middle = (value - high).astype(BF16).astype(F32)
-    low = value - high - middle
-    row = iota((cap, LANES), 0)
-    three = jnp.where(row == 0, high, jnp.where(row == 1, middle, low)).astype(BF16)
-    rest[:cap, wide - half : wide] = three[:, :half]
-
-
-def pack(sources, count, own, rest, across, rest_across, *refs):
+        rest[part, :width] = take[:, :width]
+        code = take[:, width : width + 1].astype(F32)
+        rest[part, width:] = jnp.where(lane == rows, code, 0.0 if j else tail).astype(BF16)
+
+
+def pack(sources, count, rows, pad, own, rest, across, rest_across, *refs):
     near, far, out = refs[:sources], refs[sources:-1], refs[-1]
-    width = own.shape[1] - LANES
-    half = LANES // 2
-    three = rest_across[0:8, width + half : width + LANES].astype(F32)
-    three = three[0:1] + three[1:2] + three[2:3]
-    totals = [near[0][...], jnp.concatenate([three, jnp.zeros_like(three)], axis=1)]
+    cap, width = own.shape[0], own.shape[1] - LANES
+    first = width + rows
+    three = rest_across[:cap, first + 1 : first + 4].astype(F32)
+    three = three[:, 0:1] + three[:, 1:2] + three[:, 2:3]
+    three = jnp.where(diagonal(cap), three, 0.0)
+    totals = [near[0][...], jnp.sum(three, axis=0, keepdims=True)]
     for k in range(1, sources):
         totals = [totals[0] + near[k][...], totals[1] + far[k - 1][...]]
     clips = [1.0 / jnp.maximum(jnp.sqrt(total / count), 1.0) for total in totals]
     at = 0
-    for block, clip in ((own, clips[0]), (rest, clips[0]), (across, clips[1]), (rest_across, clips[1])):
-        mine = chosen(block[:, width : width + 1])
+    for block, codes, clip in (
+        (own, own[:, width : width + 1], clips[0]),
+        (rest, rest[:, first : first + 1], clips[0]),
+        (across, rest_across[:cap, first + pad : first + pad + 1], clips[1]),
+        (rest_across, rest_across[:, first : first + 1], clips[1]),
+    ):
+        mine = chosen(codes)
         weight = jnp.sum(jnp.where(mine, clip, 0.0), axis=1, keepdims=True) / EXAMPLES
         scaled = (weight * block[:, :width].astype(F32)).astype(BF16)
         out[at : at + mine.shape[0]] = scaled
@@ -163,9 +179,7 @@
 
 
 def near_product(cut, rest_across, cots, out, units):
-    first = cots.shape[1] + LANES
-    cap = cut.shape[0]
-    across = rest_across.at[:cap, first : first + cut.shape[1]]
+    across = rest_across.at[: cut.shape[0], cots.shape[1] :]
     out[...] = multiply([cut, across], cots, units)
 
 
@@ -208,7 +222,7 @@
     top = routes.shape[1]
     cap, ff = hidden.shape[3], hidden.shape[4]
     rows = ff // n_dp
-    pad = -(-(rows + 1) // 16) * 16
+    pad = -(-(rows + 4) // 16) * 16
     while spread * pad * sources % LANES:
         pad += 16
     across = spread * pad
@@ -231,9 +245,9 @@
         ]
         return lax.ppermute(array, ("dp", "expert"), pairs)
 
-    block, *gives = call(
+    alone, block, *gives = call(
         lambda *refs: build(sources, cap, *refs),
-        [shape((cap, width + LANES), BF16)] * sources,
+        [shape((cap, width), BF16)] + [shape((cap, width + LANES), BF16)] * sources,
         (routes.T, route_weight.T, example_ids, example_weight, grad_out),
         fetched=range(5),
         limit=60,
@@ -247,13 +261,13 @@
         ),
     )
     takes = [over_experts(g, k + 1) for k, g in enumerate(gives)]
-    block_across = over_dp(block, 2)
+    block_across = over_dp(alone, 2)
     own, left, *cuts = call(
         lambda *refs: stage(sources, n_dp, pad, *refs),
         [shape((cap, width + LANES), BF16), shape((slots, slots), F32)]
         + [shape((cap, sources * across), BF16)] * MATES,
         (block, acts),
-        flops=1 << 32,
+        flops=1,
     )
     (squares,) = call(
         lambda *refs: norms(sources, *refs),
@@ -262,16 +276,16 @@
         flops=1 << 32,
     )
     (rest,) = call(
-        pass_on,
-        [shape((slots - cap, width + LANES + sources * across), BF16)],
-        (block_across, squares, cuts[2], *takes),
+        lambda *refs: pass_on(rows, pad, *refs),
+        [shape((slots - cap, width + sources * across), BF16)],
+        (block_across, own, squares, cuts[2], *takes),
         fetched=(0,),
     )
     rest_across = over_dp(rest, 2)
     near_squares = [squares] + [over_experts(squares, k) for k in range(1, sources)]
     far_squares = [over_both(squares, k) for k in range(1, sources)]
     (cots,) = call(
-        lambda *refs: pack(sources, ff * width, *refs),
+        lambda *refs: pack(sources, ff * width, rows, pad, *refs),
         [shape((2 * slots, width), BF16)],
         (own, rest, block_across, rest_across, *near_squares, *far_squares),
     )

time: 31.4 us -> 31.6 us (level)
  no operation moved by 1% of the time
where the time goes in v3:
time: 31.6 us; the launch traced here: 31.4 us
  starting transfers between devices  14.3 us (45%)
  waiting for transfers between devices  10.8 us (34%)
  Pallas kernels  4.42 us (14%)
  local copies, waits for them, and re-layouts  0.9 us (3%)
  other arithmetic  0.84 us (3%)
    ppermute x8, waiting for transfers between devices, over_dp(): return lax.ppermute(array, 'dp', [(i, i ^ k) for i in range(n_dp)])  9.69 us
    ppermute x8, starting transfers between devices, over_dp(): return lax.ppermute(array, 'dp', [(i, i ^ k) for i in range(n_dp)])  9.24 us
    ppermute x2, starting transfers between devices, over_experts(): lax.ppermute(array, 'expert', [(s, (s - k) % sources) for s in range(sour...  4.53 us
    pallas_call x7, Pallas kernels, call(): pl.pallas_call(body, out_shape=tuple(outs), in_specs=[anywhere if i in fe...  4.42 us
    unnamed x4, local copies, waits for them, and re-layouts  0.9 us
    ppermute x1, waiting for transfers between devices, over_both(): return lax.ppermute(array, ('dp', 'expert'), pairs)  0.83 us
    add x1, other arithmetic, shards(): part = part + got[:held] * jnp.exp2(got[held:held + 1])  0.73 us
  transfers between devices with their start and end apart: 11, of which 7 were waited for; matrix products, arithmetic and copies ran while one was open for 0% of the time, Pallas kernels for 5%

profile of v3, /device:TPU:0, one launch (start us, length us, event | category | flops | bytes accessed | tf_op | source)
XLA Modules:
  0.0 31.4 jit_solution(17504305084276552112)
XLA Ops:
  0.0 0.0 copy-start
  0.0 2.1 %shard_map.64 = (bf16[48,1024]{1,0:T(8,128)(2,1)}, bf16[48,1152]{1,0:T(8,128)(2,1)}, bf16[48,1152]{1,0:T(8,128)(2,1)}) custom-call(s32[6,256]{1,0:T(8,128)} %bitcast.11, f32[6,256]{1,0:T(8,128)} %bitcast.12, s32[1,256]{1,0:T(1,128)} %refs_2_.1, f32[1,8]{1,0:T(1,128)} %refs_3_.1, bf16[256,1024]{1,0:T(8,128)(2,1)} %refs_4_.1), custom_call_target="tpu_custom_call" | custom-call | flops 1 | bytes 1 | tf_op jit(solution)/shard_map/pallas_call | solution.py:206
  2.2 3.0 %collective-permute-start.1 = (bf16[48,1152]{1,0:T(8,128)(2,1)}, bf16[48,1152]{1,0:T(8,128)(2,1)S(1)}, u32[]{:S(2)}, u32[]{:S(2)}) collective-permute-start(bf16[48,1152]{1,0:T(8,128)(2,1)} %get-tuple-element.23), channel_id=1, source_target_pairs={{0,1},{1,0},{2,3},{3,2},{4,5},{5,4},{6,7},{7,6},{8,9},{9,8},{10,11... | collective-permute-start | bytes 331784 | tf_op jit(solution)/shard_map/ppermute | solution.py:234
  5.2 1.5 %collective-permute-start = (bf16[48,1024]{1,0:T(8,128)(2,1)}, bf16[48,1024]{1,0:T(8,128)(2,1)S(1)}, u32[]{:S(2)}, u32[]{:S(2)}) collective-permute-start(bf16[48,1024]{1,0:T(8,128)(2,1)} %get-tuple-element.20), channel_id=1, source_target_pairs={{0,4},{2,6},{4,0},{6,2},{8,12},{10,14},{12,8},{14,10},{16,20},{18,... | collective-permute-start | bytes 294920 | tf_op jit(solution)/shard_map/ppermute | solution.py:239
  6.7 0.0 copy-done
  6.7 0.0 copy-start.1
  6.7 0.9 %copy-done.1 = bf16[48,1152]{1,0:T(8,128)(2,1)S(1)} copy-done((bf16[48,1152]{1,0:T(8,128)(2,1)S(1)}, bf16[48,1152]{1,0:T(8,128)(2,1)}, u32[]{:S(2)}) %copy-start.1) | copy-done | bytes 110616
  7.6 0.6 %shard_map.65 = (bf16[48,1152]{1,0:T(8,128)(2,1)S(1)}, f32[96,96]{1,0:T(8,128)S(1)}, bf16[48,384]{1,0:T(8,128)(2,1)S(1)}, bf16[48,384]{1,0:T(8,128)(2,1)S(1)}, b...) custom-call(bf16[48,1152]{1,0:T(8,128)(2,1)S(1)} %copy-done.1, bf16[2,48,704]{2,1,0:T(8,128)(2,1)S(1)} %bitcast.10), custom_call_target="tpu_custom_call" | custom-call | flops 1 | bytes 1 | tf_op jit(solution)/shard_map/pallas_call | solution.py:206
  8.1 0.3 collective-permute-done.1.refs_2_.refs_4_
  8.5 0.3 %shard_map.66.refs_2_.refs_4_ = f32[1,128]{1,0:T(1,128)S(1)} custom-call(f32[96,96]{1,0:T(8,128)S(1)} %get-tuple-element.22.refs_0_, bf16[48,1152]{1,0:T(8,128)(2,1)S(1)} %get-tuple-element.21.refs_1_.refs_0_, bf16[48,1152]{1,0:T(8,128)(2,1)S(1)} %collective-permute-done.1.refs_2_.refs_4_), custom_call_target="tpu_custom_call" | custom-call | flops 4294967296 | bytes 1 | tf_op jit(solution)/shard_map/pallas_call | solution.py:206
  8.8 1.2 %collective-permute-done.refs_0_.refs_2_ = bf16[48,1024]{1,0:T(8,128)(2,1)S(1)} collective-permute-done((bf16[48,1024]{1,0:T(8,128)(2,1)}, bf16[48,1024]{1,0:T(8,128)(2,1)S(1)}, u32[]{:S(2)}, u32[]{:S(2)}) %collective-permute-start) | collective-permute-done | bytes 98336 | tf_op jit(solution)/shard_map/ppermute | solution.py:239
  10.0 0.1 shard_map.67.refs_1_
  10.1 1.6 %collective-permute-start.2 = (bf16[48,1408]{1,0:T(8,128)(2,1)S(1)}, bf16[48,1408]{1,0:T(8,128)(2,1)S(1)}, u32[]{:S(2)}, u32[]{:S(2)}) collective-permute-start(bf16[48,1408]{1,0:T(8,128)(2,1)S(1)} %shard_map.67.refs_1_), channel_id=1, source_target_pairs={{0,4},{2,6},{4,0},{6,2},{8,12},{10,14},{12,8},{14,10},{16,20},{18,... | collective-permute-start | bytes 405512 | tf_op jit(solution)/shard_map/ppermute | solution.py:239
  11.7 0.5 %collective-permute-start.4 = (f32[1,128]{1,0:T(1,128)S(1)}, f32[1,128]{1,0:T(1,128)S(1)}, u32[]{:S(2)}, u32[]{:S(2)}) collective-permute-start(f32[1,128]{1,0:T(1,128)S(1)} %shard_map.66.refs_2_.refs_4_), channel_id=1, source_target_pairs={{0,5},{1,4},{2,7},{3,6},{4,1},{5,0},{6,3},{7,2},{8,13},{9,12},{10,... | collective-permute-start | bytes 1544 | tf_op jit(solution)/shard_map/ppermute | solution.py:246
  12.2 1.5 %collective-permute-start.3 = (f32[1,128]{1,0:T(1,128)S(1)}, f32[1,128]{1,0:T(1,128)S(1)}, u32[]{:S(2)}, u32[]{:S(2)}) collective-permute-start(f32[1,128]{1,0:T(1,128)S(1)} %shard_map.66.refs_2_.refs_4_), channel_id=1, source_target_pairs={{0,1},{1,0},{2,3},{3,2},{4,5},{5,4},{6,7},{7,6},{8,9},{9,8},{10,11... | collective-permute-start | bytes 1544 | tf_op jit(solution)/shard_map/ppermute | solution.py:234
  13.7 0.0 collective-permute-start.5
  13.7 1.6 %collective-permute-start.6 = (bf16[48,384]{1,0:T(8,128)(2,1)S(1)}, bf16[48,384]{1,0:T(8,128)(2,1)S(1)}, u32[]{:S(2)}, u32[]{:S(2)}) collective-permute-start(bf16[48,384]{1,0:T(8,128)(2,1)S(1)} %get-tuple-element.26), channel_id=1, source_target_pairs={{0,6},{2,4},{4,2},{6,0},{8,14},{10,12},{12,10},{14,8},{16,22},{18,... | collective-permute-start | bytes 110600 | tf_op jit(solution)/shard_map/ppermute | solution.py:239
  15.3 0.8 %collective-permute-done.4.refs_6_ = f32[1,128]{1,0:T(1,128)S(1)} collective-permute-done((f32[1,128]{1,0:T(1,128)S(1)}, f32[1,128]{1,0:T(1,128)S(1)}, u32[]{:S(2)}, u32[]{:S(2)}) %collective-permute-start.4) | collective-permute-done | bytes 544 | tf_op jit(solution)/shard_map/ppermute | solution.py:246
  16.1 0.0 collective-permute-done.3.refs_5_
  16.1 0.0 collective-permute-done.2.refs_3_.rest_across
  16.1 0.4 %shard_map.68.cots = bf16[192,1024]{1,0:T(8,128)(2,1)S(1)} custom-call(bf16[48,1152]{1,0:T(8,128)(2,1)S(1)} %get-tuple-element.21.refs_1_.refs_0_, bf16[48,1408]{1,0:T(8,128)(2,1)S(1)} %shard_map.67.refs_1_, bf16[48,1024]{1,0:T(8,128)(2,1)S(1)} %collective-permute-done.refs_0_.refs_2_, bf16[48,1408]{1,0:T(8,128)(2,1)S(1)} %collective-permute-done.2.refs_3_.rest_across, ...), custom_call_target="tpu_custom_call" | custom-call | flops 1 | bytes 1 | tf_op jit(solution)/shard_map/pallas_call | solution.py:206
  16.5 0.1 collective-permute-start.7
  16.6 0.4 %shard_map.69.refs_0_ = f32[192,1024]{1,0:T(8,128)S(1)} custom-call(bf16[48,384]{1,0:T(8,128)(2,1)S(1)} %get-tuple-element.19.cut, bf16[48,1408]{1,0:T(8,128)(2,1)S(1)} %collective-permute-done.2.refs_3_.rest_across, bf16[192,1024]{1,0:T(8,128)(2,1)S(1)} %shard_map.68.cots), custom_call_target="tpu_custom_call" | custom-call | flops 4294967296 | bytes 1 | tf_op jit(solution)/shard_map/pallas_call | solution.py:206
  17.0 0.0 collective-permute-done.5.refs_1_
  17.0 0.1 collective-permute-done.6.refs_2_
  17.1 1.2 %collective-permute-done.7.refs_3_ = bf16[192,1024]{1,0:T(8,128)(2,1)S(1)} collective-permute-done((bf16[192,1024]{1,0:T(8,128)(2,1)S(1)}, bf16[192,1024]{1,0:T(8,128)(2,1)S(1)}, u32[]{:S(2)}, u32[]{:S(2)}) %collective-permute-start.7) | collective-permute-done | bytes 393248 | tf_op jit(solution)/shard_map/ppermute | solution.py:239
  18.3 0.6 %shard_map.70 = (f32[352,128]{1,0:T(8,128)S(1)}, f32[360,128]{1,0:T(8,128)S(1)}, f32[360,128]{1,0:T(8,128)S(1)}, f32[360,128]{1,0:T(8,128)S(1)}) custom-call(f32[192,1024]{1,0:T(8,128)S(1)} %shard_map.69.refs_0_, bf16[48,384]{1,0:T(8,128)(2,1)S(1)} %collective-permute-done.5.refs_1_, bf16[48,384]{1,0:T(8,128)(2,1)S(1)} %collective-permute-done.6.refs_2_, ...), custom_call_target="tpu_custom_call" | custom-call | flops 1 | bytes 1 | tf_op jit(solution)/shard_map/pallas_call | solution.py:206
  18.9 3.7 %collective-permute-start.10 = (f16[360,128]{1,0:T(8,128)(2,1)S(1)}, f16[360,128]{1,0:T(8,128)(2,1)S(1)}, u32[]{:S(2)}, u32[]{:S(2)}) collective-permute-start(f16[360,128]{1,0:T(8,128)(2,1)S(1)} %convert_element_type.22), channel_id=1, source_target_pairs={{0,24},{2,26},{4,28},{6,30},{8,16},{10,18},{12,20},{14,22},{16,8},... | collective-permute-start | bytes 276488 | tf_op jit(solution)/shard_map/ppermute | solution.py:239
  22.6 0.1 collective-permute-start.9
  22.7 0.8 %collective-permute-start.8 = (f16[360,128]{1,0:T(8,128)(2,1)S(1)}, f16[360,128]{1,0:T(8,128)(2,1)S(1)}, u32[]{:S(2)}, u32[]{:S(2)}) collective-permute-start(f16[360,128]{1,0:T(8,128)(2,1)S(1)} %convert_element_type.18), channel_id=1, source_target_pairs={{0,8},{2,10},{4,12},{6,14},{8,0},{10,2},{12,4},{14,6},{16,24},{18,... | collective-permute-start | bytes 276488 | tf_op jit(solution)/shard_map/ppermute | solution.py:239
  23.5 2.8 %collective-permute-done.10 = f16[360,128]{1,0:T(8,128)(2,1)S(1)} collective-permute-done((f16[360,128]{1,0:T(8,128)(2,1)S(1)}, f16[360,128]{1,0:T(8,128)(2,1)S(1)}, u32[]{:S(2)}, u32[]{:S(2)}) %collective-permute-start.10) | collective-permute-done | bytes 92192 | tf_op jit(solution)/shard_map/ppermute | solution.py:239
  26.3 4.3 %collective-permute-done.9 = f16[360,128]{1,0:T(8,128)(2,1)S(1)} collective-permute-done((f16[360,128]{1,0:T(8,128)(2,1)S(1)}, f16[360,128]{1,0:T(8,128)(2,1)S(1)}, u32[]{:S(2)}, u32[]{:S(2)}) %collective-permute-start.9) | collective-permute-done | bytes 92192 | tf_op jit(solution)/shard_map/ppermute | solution.py:239
  30.6 0.0 collective-permute-done.8
  30.7 0.7 %fusion = f32[352,128]{1,0:T(8,128)} fusion(f32[360,128]{1,0:T(8,128)S(1)} %convert_element_type.23, f32[360,128]{1,0:T(8,128)S(1)} %convert_element_type.21, f32[352,128]{1,0:T(8,128)S(1)} %get-tuple-element.27, f32[360,128]{1,0:T(8,128)S(1)} %convert_element_type.19, f32[128]{0:T(128)S(1)} %fusion.4, f32[128]{0:T(128)S(1)} %fusion.6, f32[128]{0:T(128)S(1)} %fusion.8), kind=kLoop, calls=%fused_computation.1 | loop fusion | flops 270336 | bytes 902656 | tf_op jit(solution)/shard_map/add | solution.py:311
  (9 shorter events, 0.1 us)
Async XLA Ops:
  0.0 6.7 %copy-start = (bf16[1,1,2,48,704]{4,3,2,1,0:T(8,128)(2,1)S(1)}, bf16[1,1,2,48,704]{4,3,2,1,0:T(8,128)(2,1)}, u32[]{:S(2)}) copy-start(bf16[1,1,2,48,704]{4,3,2,1,0:T(8,128)(2,1)} %param.11) | copy-start | bytes 405508
  2.2 6.3 %collective-permute-start.1 = (bf16[48,1152]{1,0:T(8,128)(2,1)}, bf16[48,1152]{1,0:T(8,128)(2,1)S(1)}, u32[]{:S(2)}, u32[]{:S(2)}) collective-permute-start(bf16[48,1152]{1,0:T(8,128)(2,1)} %get-tuple-element.23), channel_id=1, source_target_pairs={{0,1},{1,0},{2,3},{3,2},{4,5},{5,4},{6,7},{7,6},{8,9},{9,8},{10,11... | collective-permute-start | bytes 331784 | tf_op jit(solution)/shard_map/ppermute | solution.py:234
  5.2 4.8 %collective-permute-start = (bf16[48,1024]{1,0:T(8,128)(2,1)}, bf16[48,1024]{1,0:T(8,128)(2,1)S(1)}, u32[]{:S(2)}, u32[]{:S(2)}) collective-permute-start(bf16[48,1024]{1,0:T(8,128)(2,1)} %get-tuple-element.20), channel_id=1, source_target_pairs={{0,4},{2,6},{4,0},{6,2},{8,12},{10,14},{12,8},{14,10},{16,20},{18,... | collective-permute-start | bytes 294920 | tf_op jit(solution)/shard_map/ppermute | solution.py:239
  6.7 0.9 %copy-start.1 = (bf16[48,1152]{1,0:T(8,128)(2,1)S(1)}, bf16[48,1152]{1,0:T(8,128)(2,1)}, u32[]{:S(2)}) copy-start(bf16[48,1152]{1,0:T(8,128)(2,1)} %get-tuple-element.18.refs_0_) | copy-start | bytes 331780
  10.1 6.0 %collective-permute-start.2 = (bf16[48,1408]{1,0:T(8,128)(2,1)S(1)}, bf16[48,1408]{1,0:T(8,128)(2,1)S(1)}, u32[]{:S(2)}, u32[]{:S(2)}) collective-permute-start(bf16[48,1408]{1,0:T(8,128)(2,1)S(1)} %shard_map.67.refs_1_), channel_id=1, source_target_pairs={{0,4},{2,6},{4,0},{6,2},{8,12},{10,14},{12,8},{14,10},{16,20},{18,... | collective-permute-start | bytes 405512 | tf_op jit(solution)/shard_map/ppermute | solution.py:239
  11.7 4.4 %collective-permute-start.4 = (f32[1,128]{1,0:T(1,128)S(1)}, f32[1,128]{1,0:T(1,128)S(1)}, u32[]{:S(2)}, u32[]{:S(2)}) collective-permute-start(f32[1,128]{1,0:T(1,128)S(1)} %shard_map.66.refs_2_.refs_4_), channel_id=1, source_target_pairs={{0,5},{1,4},{2,7},{3,6},{4,1},{5,0},{6,3},{7,2},{8,13},{9,12},{10,... | collective-permute-start | bytes 1544 | tf_op jit(solution)/shard_map/ppermute | solution.py:246
  12.2 3.9 %collective-permute-start.3 = (f32[1,128]{1,0:T(1,128)S(1)}, f32[1,128]{1,0:T(1,128)S(1)}, u32[]{:S(2)}, u32[]{:S(2)}) collective-permute-start(f32[1,128]{1,0:T(1,128)S(1)} %shard_map.66.refs_2_.refs_4_), channel_id=1, source_target_pairs={{0,1},{1,0},{2,3},{3,2},{4,5},{5,4},{6,7},{7,6},{8,9},{9,8},{10,11... | collective-permute-start | bytes 1544 | tf_op jit(solution)/shard_map/ppermute | solution.py:234
  13.7 3.3 %collective-permute-start.5 = (bf16[48,384]{1,0:T(8,128)(2,1)S(1)}, bf16[48,384]{1,0:T(8,128)(2,1)S(1)}, u32[]{:S(2)}, u32[]{:S(2)}) collective-permute-start(bf16[48,384]{1,0:T(8,128)(2,1)S(1)} %get-tuple-element.25), channel_id=1, source_target_pairs={{0,2},{2,0},{4,6},{6,4},{8,10},{10,8},{12,14},{14,12},{16,18},{18,... | collective-permute-start | bytes 110600 | tf_op jit(solution)/shard_map/ppermute | solution.py:239
  13.7 3.4 %collective-permute-start.6 = (bf16[48,384]{1,0:T(8,128)(2,1)S(1)}, bf16[48,384]{1,0:T(8,128)(2,1)S(1)}, u32[]{:S(2)}, u32[]{:S(2)}) collective-permute-start(bf16[48,384]{1,0:T(8,128)(2,1)S(1)} %get-tuple-element.26), channel_id=1, source_target_pairs={{0,6},{2,4},{4,2},{6,0},{8,14},{10,12},{12,10},{14,8},{16,22},{18,... | collective-permute-start | bytes 110600 | tf_op jit(solution)/shard_map/ppermute | solution.py:239
  16.5 1.8 %collective-permute-start.7 = (bf16[192,1024]{1,0:T(8,128)(2,1)S(1)}, bf16[192,1024]{1,0:T(8,128)(2,1)S(1)}, u32[]{:S(2)}, u32[]{:S(2)}) collective-permute-start(bf16[192,1024]{1,0:T(8,128)(2,1)S(1)} %shard_map.68.cots), channel_id=1, source_target_pairs={{0,2},{2,0},{4,6},{6,4},{8,10},{10,8},{12,14},{14,12},{16,18},{18,... | collective-permute-start | bytes 1179656 | tf_op jit(solution)/shard_map/ppermute | solution.py:239
  18.9 7.3 %collective-permute-start.10 = (f16[360,128]{1,0:T(8,128)(2,1)S(1)}, f16[360,128]{1,0:T(8,128)(2,1)S(1)}, u32[]{:S(2)}, u32[]{:S(2)}) collective-permute-start(f16[360,128]{1,0:T(8,128)(2,1)S(1)} %convert_element_type.22), channel_id=1, source_target_pairs={{0,24},{2,26},{4,28},{6,30},{8,16},{10,18},{12,20},{14,22},{16,8},... | collective-permute-start | bytes 276488 | tf_op jit(solution)/shard_map/ppermute | solution.py:239
  22.6 8.0 %collective-permute-start.9 = (f16[360,128]{1,0:T(8,128)(2,1)S(1)}, f16[360,128]{1,0:T(8,128)(2,1)S(1)}, u32[]{:S(2)}, u32[]{:S(2)}) collective-permute-start(f16[360,128]{1,0:T(8,128)(2,1)S(1)} %convert_element_type.20), channel_id=1, source_target_pairs={{0,16},{2,18},{4,20},{6,22},{8,24},{10,26},{12,28},{14,30},{16,0},... | collective-permute-start | bytes 276488 | tf_op jit(solution)/shard_map/ppermute | solution.py:239
  22.7 8.0 %collective-permute-start.8 = (f16[360,128]{1,0:T(8,128)(2,1)S(1)}, f16[360,128]{1,0:T(8,128)(2,1)S(1)}, u32[]{:S(2)}, u32[]{:S(2)}) collective-permute-start(f16[360,128]{1,0:T(8,128)(2,1)S(1)} %convert_element_type.18), channel_id=1, source_target_pairs={{0,8},{2,10},{4,12},{6,14},{8,0},{10,2},{12,4},{14,6},{16,24},{18,... | collective-permute-start | bytes 276488 | tf_op jit(solution)/shard_map/ppermute | solution.py:239

commit v4 on v1

--- a/solution.py
+++ b/solution.py
@@ -174,16 +174,24 @@
     width = cots.shape[1]
     pieces = width // LANES
     part = start[...] + multiply([cut, across], cots, units)
-    for p, out in enumerate([keep, *leave]):
+    leave = list(leave)
+    for p in range(part.shape[0] // pad):
         values = part[p * pad : p * pad + rows]
         if p:
             most = jnp.max(jnp.max(jnp.abs(values), axis=0, keepdims=True), axis=1, keepdims=True)
             exponent = jnp.ceil(jnp.log2(jnp.maximum(most, 2.0**-100)))
             values = values * jnp.exp2(-exponent)
-            below = out.shape[0] - rows * pieces
-            out[rows * pieces :] = jnp.broadcast_to(exponent, (below, LANES))
-        for j in range(pieces):
-            out[pl.ds(j, rows, stride=pieces), :] = values[:, j * LANES : (j + 1) * LANES]
+        done = 0
+        for out in [keep] if p == 0 else [leave.pop(0) for _ in range(1 if p == 1 else 2)]:
+            held = out.shape[0] if p == 0 else out.shape[0] - 8
+            count = held // pieces
+            for j in range(pieces):
+                out[pl.ds(j, count, stride=pieces), :] = values[
+                    done : done + count, j * LANES : (j + 1) * LANES
+                ]
+            if p:
+                out[held:] = jnp.broadcast_to(exponent, (8, LANES))
+            done += count
 
 
 def call(body, outs, args, fetched=(), scratch=(), limit=32, flops=1):
@@ -285,16 +293,35 @@
     )
 
     held = rows * (width // LANES)
-    sent = held + 8
+    pieces = width // LANES
+    upper = rows // 2 * pieces
+    lower = held - upper
+    sizes = [held, held + 8] + [upper + 8, lower + 8] * (spread - 2)
     part, *leave = call(
         lambda *refs: product(rows, pad, *refs),
-        [shape((held if p == 0 else sent, LANES), F32) for p in range(spread)],
+        [shape((size, LANES), F32) for size in sizes],
         (start, over_dp(cuts[1], 1), over_dp(cuts[3], 3), other_cots),
         scratch=(pltpu.VMEM((2 * slots, across), BF16),),
     )
-    for p in range(1, spread):
-        got = over_dp(leave[p - 1].astype(jnp.float16), p * MATES).astype(F32)
-        part = part + got[:held] * jnp.exp2(got[held : held + 1])
+    uppers, lowers = [None, None] + leave[1::2], [None, None] + leave[2::2]
+
+    def over_spread(array, p):
+        return over_dp(array.astype(jnp.float16), p * MATES).astype(F32)
+
+    def value(array):
+        return array[:-8] * jnp.exp2(array[-8:-7])
+
+    sums = {}
+    for p in range(2, spread, 2):
+        got = over_spread(lowers[p + 1], 1)
+        top = jnp.maximum(got[-8:-7], lowers[p][-8:-7])
+        added = got[:-8] * jnp.exp2(got[-8:-7] - top)
+        added = added + lowers[p][:-8] * jnp.exp2(lowers[p][-8:-7] - top)
+        sums[p] = jnp.concatenate([added, jnp.broadcast_to(top, (8, LANES))], axis=0)
+    come = sum(value(over_spread(uppers[p], p)) for p in range(spread - 1, 1, -1))
+    come_lower = sum(value(over_spread(sums[p], p)) for p in sums)
+    come = jnp.concatenate([come, come_lower], axis=0)
+    part = part + value(over_spread(leave[0], 1)) + come
     return part.reshape(rows, 1, width)
 
 

time: 31.4 us -> 31 us (0.987)
  waiting for transfers between devices: 10.9 us -> 6.04 us
  starting transfers between devices: 14.2 us -> 18.5 us
    ppermute x8 -> x10, waiting for transfers between devices: 9.81 us -> 4.92 us  [over_dp(): return lax.ppermute(array, 'dp', [(i, i ^ k) for i in range(n_dp)])]
    ppermute x8 -> x10, starting transfers between devices: 9.18 us -> 13.5 us  [over_dp(): return lax.ppermute(array, 'dp', [(i, i ^ k) for i in range(n_dp)])]
    add x1 -> x2, other arithmetic: 0.73 us -> 0.74 us  [the longest x1 0.72 us: shards(): part = part + value(over_spread(leave[0], 1)) + come]
  transfers between devices with their start and end apart: 11 -> 13, of which waited for: 7 -> 7; matrix products, arithmetic and copies ran while one was open for 0% -> 1% of each run, Pallas kernels for 5% -> 5%
where the time goes in v4:
time: 31 us; the launch traced here: 30.9 us
  starting transfers between devices  18.5 us (60%)
  waiting for transfers between devices  6.04 us (19%)
  Pallas kernels  4.28 us (14%)
  local copies, waits for them, and re-layouts  0.94 us (3%)
  other arithmetic  0.92 us (3%)
    ppermute x10, starting transfers between devices, over_dp(): return lax.ppermute(array, 'dp', [(i, i ^ k) for i in range(n_dp)])  13.5 us
    ppermute x10, waiting for transfers between devices, over_dp(): return lax.ppermute(array, 'dp', [(i, i ^ k) for i in range(n_dp)])  4.92 us
    ppermute x2, starting transfers between devices, over_experts(): lax.ppermute(array, 'expert', [(s, (s - k) % sources) for s in range(sour...  4.66 us
    pallas_call x7, Pallas kernels, call(): pl.pallas_call(body, out_shape=tuple(outs), in_specs=[anywhere if i in fe...  4.28 us
    unnamed x4, local copies, waits for them, and re-layouts  0.93 us
    ppermute x1, waiting for transfers between devices, over_both(): return lax.ppermute(array, ('dp', 'expert'), pairs)  0.83 us
    add x1, other arithmetic, shards(): part = part + value(over_spread(leave[0], 1)) + come  0.72 us
  transfers between devices with their start and end apart: 13, of which 7 were waited for; matrix products, arithmetic and copies ran while one was open for 1% of the time, Pallas kernels for 5%

profile of v4, /device:TPU:0, one launch (start us, length us, event | category | flops | bytes accessed | tf_op | source)
XLA Modules:
  0.0 30.9 jit_solution(7980813392834530235)
XLA Ops:
  0.0 0.0 copy-start
  0.0 2.2 %shard_map.64 = (bf16[48,1152]{1,0:T(8,128)(2,1)}, bf16[48,1152]{1,0:T(8,128)(2,1)}) custom-call(s32[6,256]{1,0:T(8,128)} %bitcast.19, f32[6,256]{1,0:T(8,128)} %bitcast.20, s32[1,256]{1,0:T(1,128)} %refs_2_.1, f32[1,8]{1,0:T(1,128)} %refs_3_.1, bf16[256,1024]{1,0:T(8,128)(2,1)} %refs_4_.1), custom_call_target="tpu_custom_call" | custom-call | flops 1 | bytes 1 | tf_op jit(solution)/shard_map/pallas_call | solution.py:200
  2.2 3.0 %collective-permute-start.1 = (bf16[48,1152]{1,0:T(8,128)(2,1)}, bf16[48,1152]{1,0:T(8,128)(2,1)S(1)}, u32[]{:S(2)}, u32[]{:S(2)}) collective-permute-start(bf16[48,1152]{1,0:T(8,128)(2,1)} %get-tuple-element.23), channel_id=1, source_target_pairs={{0,1},{1,0},{2,3},{3,2},{4,5},{5,4},{6,7},{7,6},{8,9},{9,8},{10,11... | collective-permute-start | bytes 331784 | tf_op jit(solution)/shard_map/ppermute | solution.py:228
  5.2 1.5 %collective-permute-start = (bf16[48,1152]{1,0:T(8,128)(2,1)}, bf16[48,1152]{1,0:T(8,128)(2,1)S(1)}, u32[]{:S(2)}, u32[]{:S(2)}) collective-permute-start(bf16[48,1152]{1,0:T(8,128)(2,1)} %get-tuple-element.19.refs_0_), channel_id=1, source_target_pairs={{0,4},{2,6},{4,0},{6,2},{8,12},{10,14},{12,8},{14,10},{16,20},{18,... | collective-permute-start | bytes 331784 | tf_op jit(solution)/shard_map/ppermute | solution.py:233
  6.7 0.0 copy-done
  6.7 0.0 copy-start.1
  6.7 0.9 %copy-done.1 = bf16[48,1152]{1,0:T(8,128)(2,1)S(1)} copy-done((bf16[48,1152]{1,0:T(8,128)(2,1)S(1)}, bf16[48,1152]{1,0:T(8,128)(2,1)}, u32[]{:S(2)}) %copy-start.1) | copy-done | bytes 110616
  7.6 0.6 %shard_map.65 = (bf16[48,1152]{1,0:T(8,128)(2,1)S(1)}, f32[96,96]{1,0:T(8,128)S(1)}, bf16[48,384]{1,0:T(8,128)(2,1)S(1)}, bf16[48,384]{1,0:T(8,128)(2,1)S(1)}, b...) custom-call(bf16[48,1152]{1,0:T(8,128)(2,1)S(1)} %copy-done.1, bf16[2,48,704]{2,1,0:T(8,128)(2,1)S(1)} %bitcast.18), custom_call_target="tpu_custom_call" | custom-call | flops 4294967296 | bytes 1 | tf_op jit(solution)/shard_map/pallas_call | solution.py:200
  8.2 0.3 collective-permute-done.1.refs_2_.refs_0_
  8.5 0.3 %shard_map.66.squares.refs_4_ = f32[1,128]{1,0:T(1,128)S(1)} custom-call(f32[96,96]{1,0:T(8,128)S(1)} %get-tuple-element.21.refs_0_, bf16[48,1152]{1,0:T(8,128)(2,1)S(1)} %get-tuple-element.22.refs_1_.refs_0_, bf16[48,1152]{1,0:T(8,128)(2,1)S(1)} %collective-permute-done.1.refs_2_.refs_0_), custom_call_target="tpu_custom_call" | custom-call | flops 4294967296 | bytes 1 | tf_op jit(solution)/shard_map/pallas_call | solution.py:200
  8.8 1.4 %collective-permute-done.across.refs_2_ = bf16[48,1152]{1,0:T(8,128)(2,1)S(1)} collective-permute-done((bf16[48,1152]{1,0:T(8,128)(2,1)}, bf16[48,1152]{1,0:T(8,128)(2,1)S(1)}, u32[]{:S(2)}, u32[]{:S(2)}) %collective-permute-start) | collective-permute-done | bytes 110624 | tf_op jit(solution)/shard_map/ppermute | solution.py:233
  10.2 0.1 shard_map.67.refs_1_
  10.2 1.5 %collective-permute-start.2 = (bf16[48,1536]{1,0:T(8,128)(2,1)S(1)}, bf16[48,1536]{1,0:T(8,128)(2,1)S(1)}, u32[]{:S(2)}, u32[]{:S(2)}) collective-permute-start(bf16[48,1536]{1,0:T(8,128)(2,1)S(1)} %shard_map.67.refs_1_), channel_id=1, source_target_pairs={{0,4},{2,6},{4,0},{6,2},{8,12},{10,14},{12,8},{14,10},{16,20},{18,... | collective-permute-start | bytes 442376 | tf_op jit(solution)/shard_map/ppermute | solution.py:233
  11.7 0.4 %collective-permute-start.4 = (f32[1,128]{1,0:T(1,128)S(1)}, f32[1,128]{1,0:T(1,128)S(1)}, u32[]{:S(2)}, u32[]{:S(2)}) collective-permute-start(f32[1,128]{1,0:T(1,128)S(1)} %shard_map.66.squares.refs_4_), channel_id=1, source_target_pairs={{0,5},{1,4},{2,7},{3,6},{4,1},{5,0},{6,3},{7,2},{8,13},{9,12},{10,... | collective-permute-start | bytes 1544 | tf_op jit(solution)/shard_map/ppermute | solution.py:240
  12.1 1.6 %collective-permute-start.3 = (f32[1,128]{1,0:T(1,128)S(1)}, f32[1,128]{1,0:T(1,128)S(1)}, u32[]{:S(2)}, u32[]{:S(2)}) collective-permute-start(f32[1,128]{1,0:T(1,128)S(1)} %shard_map.66.squares.refs_4_), channel_id=1, source_target_pairs={{0,1},{1,0},{2,3},{3,2},{4,5},{5,4},{6,7},{7,6},{8,9},{9,8},{10,11... | collective-permute-start | bytes 1544 | tf_op jit(solution)/shard_map/ppermute | solution.py:228
  13.7 0.0 collective-permute-start.5
  13.7 1.6 %collective-permute-start.6 = (bf16[48,384]{1,0:T(8,128)(2,1)S(1)}, bf16[48,384]{1,0:T(8,128)(2,1)S(1)}, u32[]{:S(2)}, u32[]{:S(2)}) collective-permute-start(bf16[48,384]{1,0:T(8,128)(2,1)S(1)} %get-tuple-element.26), channel_id=1, source_target_pairs={{0,6},{2,4},{4,2},{6,0},{8,14},{10,12},{12,10},{14,8},{16,22},{18,... | collective-permute-start | bytes 110600 | tf_op jit(solution)/shard_map/ppermute | solution.py:233
  15.3 0.8 %collective-permute-done.4.refs_6_ = f32[1,128]{1,0:T(1,128)S(1)} collective-permute-done((f32[1,128]{1,0:T(1,128)S(1)}, f32[1,128]{1,0:T(1,128)S(1)}, u32[]{:S(2)}, u32[]{:S(2)}) %collective-permute-start.4) | collective-permute-done | bytes 544 | tf_op jit(solution)/shard_map/ppermute | solution.py:240
  16.2 0.0 collective-permute-done.3.refs_5_
  16.2 0.0 collective-permute-done.2.refs_3_.rest_across
  16.2 0.2 shard_map.68.cots
  16.4 0.1 collective-permute-start.7
  16.5 0.4 %shard_map.69.refs_0_ = f32[192,1024]{1,0:T(8,128)S(1)} custom-call(bf16[48,384]{1,0:T(8,128)(2,1)S(1)} %get-tuple-element.20.cut, bf16[48,1536]{1,0:T(8,128)(2,1)S(1)} %collective-permute-done.2.refs_3_.rest_across, bf16[192,1024]{1,0:T(8,128)(2,1)S(1)} %shard_map.68.cots), custom_call_target="tpu_custom_call" | custom-call | flops 4294967296 | bytes 1 | tf_op jit(solution)/shard_map/pallas_call | solution.py:200
  16.9 0.0 collective-permute-done.5.refs_1_
  16.9 0.3 collective-permute-done.6.refs_2_
  17.1 1.1 %collective-permute-done.7.refs_3_ = bf16[192,1024]{1,0:T(8,128)(2,1)S(1)} collective-permute-done((bf16[192,1024]{1,0:T(8,128)(2,1)S(1)}, bf16[192,1024]{1,0:T(8,128)(2,1)S(1)}, u32[]{:S(2)}, u32[]{:S(2)}) %collective-permute-start.7) | collective-permute-done | bytes 393248 | tf_op jit(solution)/shard_map/ppermute | solution.py:233
  18.2 0.6 %shard_map.70 = (f32[352,128]{1,0:T(8,128)S(1)}, f32[360,128]{1,0:T(8,128)S(1)}, f32[184,128]{1,0:T(8,128)S(1)}, f32[184,128]{1,0:T(8,128)S(1)}, f32[184,128]{1,0:T(8,128)S(1)}, /*index=5*/f32[184,128]{1,0:T(8,128)S(1)}) custom-call(f32[192,1024]{1,0:T(8,128)S(1)} %shard_map.69.refs_0_, bf16[48,384]{1,0:T(8,128)(2,1)S(1)} %collective-permute-done.5.refs_1_, ...), custom_call_target="tpu_custom_call" | custom-call | flops 1 | bytes 1 | tf_op jit(solution)/shard_map/pallas_call | solution.py:200
  18.8 1.6 %collective-permute-start.11 = (f16[184,128]{1,0:T(8,128)(2,1)S(1)}, f16[184,128]{1,0:T(8,128)(2,1)S(1)}, u32[]{:S(2)}, u32[]{:S(2)}) collective-permute-start(f16[184,128]{1,0:T(8,128)(2,1)S(1)} %convert_element_type.34), channel_id=1, source_target_pairs={{0,8},{2,10},{4,12},{6,14},{8,0},{10,2},{12,4},{14,6},{16,24},{18,... | collective-permute-start | bytes 141320 | tf_op jit(solution)/shard_map/ppermute | solution.py:233
  20.5 2.6 %collective-permute-start.10 = (f16[184,128]{1,0:T(8,128)(2,1)S(1)}, f16[184,128]{1,0:T(8,128)(2,1)S(1)}, u32[]{:S(2)}, u32[]{:S(2)}) collective-permute-start(f16[184,128]{1,0:T(8,128)(2,1)S(1)} %convert_element_type.32), channel_id=1, source_target_pairs={{0,16},{2,18},{4,20},{6,22},{8,24},{10,26},{12,28},{14,30},{16,0},... | collective-permute-start | bytes 141320 | tf_op jit(solution)/shard_map/ppermute | solution.py:233
  23.1 0.2 collective-permute-start.9
  23.4 0.7 %collective-permute-start.8 = (f16[360,128]{1,0:T(8,128)(2,1)S(1)}, f16[360,128]{1,0:T(8,128)(2,1)S(1)}, u32[]{:S(2)}, u32[]{:S(2)}) collective-permute-start(f16[360,128]{1,0:T(8,128)(2,1)S(1)} %convert_element_type.28), channel_id=1, source_target_pairs={{0,8},{2,10},{4,12},{6,14},{8,0},{10,2},{12,4},{14,6},{16,24},{18,... | collective-permute-start | bytes 276488 | tf_op jit(solution)/shard_map/ppermute | solution.py:233
  24.1 0.0 collective-permute-done.11
  24.2 3.5 %collective-permute-start.12 = (f16[184,128]{1,0:T(8,128)(2,1)S(1)}, f16[184,128]{1,0:T(8,128)(2,1)S(1)}, u32[]{:S(2)}, u32[]{:S(2)}) collective-permute-start(f16[184,128]{1,0:T(8,128)(2,1)S(1)} %pad_maximum_fusion), channel_id=1, source_target_pairs={{0,16},{2,18},{4,20},{6,22},{8,24},{10,26},{12,28},{14,30},{16,0},... | collective-permute-start | bytes 141320 | tf_op jit(solution)/shard_map/ppermute | solution.py:233
  27.8 0.0 collective-permute-done.10
  27.8 1.8 %collective-permute-done.9 = f16[184,128]{1,0:T(8,128)(2,1)S(1)} collective-permute-done((f16[184,128]{1,0:T(8,128)(2,1)S(1)}, f16[184,128]{1,0:T(8,128)(2,1)S(1)}, u32[]{:S(2)}, u32[]{:S(2)}) %collective-permute-start.9) | collective-permute-done | bytes 47136 | tf_op jit(solution)/shard_map/ppermute | solution.py:233
  29.6 0.0 collective-permute-done.8
  29.7 0.4 %collective-permute-done.12 = f16[184,128]{1,0:T(8,128)(2,1)S(1)} collective-permute-done((f16[184,128]{1,0:T(8,128)(2,1)S(1)}, f16[184,128]{1,0:T(8,128)(2,1)S(1)}, u32[]{:S(2)}, u32[]{:S(2)}) %collective-permute-start.12) | collective-permute-done | bytes 47136 | tf_op jit(solution)/shard_map/ppermute | solution.py:233
  30.1 0.7 %fusion.1 = f32[352,128]{1,0:T(8,128)} fusion(f32[352,128]{1,0:T(8,128)S(1)} %get-tuple-element.27, f32[360,128]{1,0:T(8,128)S(1)} %convert_element_type.29, f32[176,128]{1,0:T(8,128)S(1)} %slice_multiply_fusion.1, f32[176,128]{1,0:T(8,128)S(1)} %fusion.4, f32[128]{0:T(128)S(1)} %fusion.12), kind=kLoop, calls=%fused_computation.2 | loop fusion | flops 180224 | bytes 721408 | tf_op jit(solution)/shard_map/add | solution.py:324
  (19 shorter events, 0.2 us)
Async XLA Ops:
  0.0 6.7 %copy-start = (bf16[1,1,2,48,704]{4,3,2,1,0:T(8,128)(2,1)S(1)}, bf16[1,1,2,48,704]{4,3,2,1,0:T(8,128)(2,1)}, u32[]{:S(2)}) copy-start(bf16[1,1,2,48,704]{4,3,2,1,0:T(8,128)(2,1)} %param.11) | copy-start | bytes 405508
  2.2 6.3 %collective-permute-start.1 = (bf16[48,1152]{1,0:T(8,128)(2,1)}, bf16[48,1152]{1,0:T(8,128)(2,1)S(1)}, u32[]{:S(2)}, u32[]{:S(2)}) collective-permute-start(bf16[48,1152]{1,0:T(8,128)(2,1)} %get-tuple-element.23), channel_id=1, source_target_pairs={{0,1},{1,0},{2,3},{3,2},{4,5},{5,4},{6,7},{7,6},{8,9},{9,8},{10,11... | collective-permute-start | bytes 331784 | tf_op jit(solution)/shard_map/ppermute | solution.py:228
  5.2 5.0 %collective-permute-start = (bf16[48,1152]{1,0:T(8,128)(2,1)}, bf16[48,1152]{1,0:T(8,128)(2,1)S(1)}, u32[]{:S(2)}, u32[]{:S(2)}) collective-permute-start(bf16[48,1152]{1,0:T(8,128)(2,1)} %get-tuple-element.19.refs_0_), channel_id=1, source_target_pairs={{0,4},{2,6},{4,0},{6,2},{8,12},{10,14},{12,8},{14,10},{16,20},{18,... | collective-permute-start | bytes 331784 | tf_op jit(solution)/shard_map/ppermute | solution.py:233
  6.7 0.9 %copy-start.1 = (bf16[48,1152]{1,0:T(8,128)(2,1)S(1)}, bf16[48,1152]{1,0:T(8,128)(2,1)}, u32[]{:S(2)}) copy-start(bf16[48,1152]{1,0:T(8,128)(2,1)} %get-tuple-element.19.refs_0_) | copy-start | bytes 331780
  10.2 5.9 %collective-permute-start.2 = (bf16[48,1536]{1,0:T(8,128)(2,1)S(1)}, bf16[48,1536]{1,0:T(8,128)(2,1)S(1)}, u32[]{:S(2)}, u32[]{:S(2)}) collective-permute-start(bf16[48,1536]{1,0:T(8,128)(2,1)S(1)} %shard_map.67.refs_1_), channel_id=1, source_target_pairs={{0,4},{2,6},{4,0},{6,2},{8,12},{10,14},{12,8},{14,10},{16,20},{18,... | collective-permute-start | bytes 442376 | tf_op jit(solution)/shard_map/ppermute | solution.py:233
  11.7 4.4 %collective-permute-start.4 = (f32[1,128]{1,0:T(1,128)S(1)}, f32[1,128]{1,0:T(1,128)S(1)}, u32[]{:S(2)}, u32[]{:S(2)}) collective-permute-start(f32[1,128]{1,0:T(1,128)S(1)} %shard_map.66.squares.refs_4_), channel_id=1, source_target_pairs={{0,5},{1,4},{2,7},{3,6},{4,1},{5,0},{6,3},{7,2},{8,13},{9,12},{10,... | collective-permute-start | bytes 1544 | tf_op jit(solution)/shard_map/ppermute | solution.py:240
  12.1 4.1 %collective-permute-start.3 = (f32[1,128]{1,0:T(1,128)S(1)}, f32[1,128]{1,0:T(1,128)S(1)}, u32[]{:S(2)}, u32[]{:S(2)}) collective-permute-start(f32[1,128]{1,0:T(1,128)S(1)} %shard_map.66.squares.refs_4_), channel_id=1, source_target_pairs={{0,1},{1,0},{2,3},{3,2},{4,5},{5,4},{6,7},{7,6},{8,9},{9,8},{10,11... | collective-permute-start | bytes 1544 | tf_op jit(solution)/shard_map/ppermute | solution.py:228
  13.7 3.1 %collective-permute-start.5 = (bf16[48,384]{1,0:T(8,128)(2,1)S(1)}, bf16[48,384]{1,0:T(8,128)(2,1)S(1)}, u32[]{:S(2)}, u32[]{:S(2)}) collective-permute-start(bf16[48,384]{1,0:T(8,128)(2,1)S(1)} %get-tuple-element.25), channel_id=1, source_target_pairs={{0,2},{2,0},{4,6},{6,4},{8,10},{10,8},{12,14},{14,12},{16,18},{18,... | collective-permute-start | bytes 110600 | tf_op jit(solution)/shard_map/ppermute | solution.py:233
  13.7 3.4 %collective-permute-start.6 = (bf16[48,384]{1,0:T(8,128)(2,1)S(1)}, bf16[48,384]{1,0:T(8,128)(2,1)S(1)}, u32[]{:S(2)}, u32[]{:S(2)}) collective-permute-start(bf16[48,384]{1,0:T(8,128)(2,1)S(1)} %get-tuple-element.26), channel_id=1, source_target_pairs={{0,6},{2,4},{4,2},{6,0},{8,14},{10,12},{12,10},{14,8},{16,22},{18,... | collective-permute-start | bytes 110600 | tf_op jit(solution)/shard_map/ppermute | solution.py:233
  16.4 1.8 %collective-permute-start.7 = (bf16[192,1024]{1,0:T(8,128)(2,1)S(1)}, bf16[192,1024]{1,0:T(8,128)(2,1)S(1)}, u32[]{:S(2)}, u32[]{:S(2)}) collective-permute-start(bf16[192,1024]{1,0:T(8,128)(2,1)S(1)} %shard_map.68.cots), channel_id=1, source_target_pairs={{0,2},{2,0},{4,6},{6,4},{8,10},{10,8},{12,14},{14,12},{16,18},{18,... | collective-permute-start | bytes 1179656 | tf_op jit(solution)/shard_map/ppermute | solution.py:233
  18.8 5.3 %collective-permute-start.11 = (f16[184,128]{1,0:T(8,128)(2,1)S(1)}, f16[184,128]{1,0:T(8,128)(2,1)S(1)}, u32[]{:S(2)}, u32[]{:S(2)}) collective-permute-start(f16[184,128]{1,0:T(8,128)(2,1)S(1)} %convert_element_type.34), channel_id=1, source_target_pairs={{0,8},{2,10},{4,12},{6,14},{8,0},{10,2},{12,4},{14,6},{16,24},{18,... | collective-permute-start | bytes 141320 | tf_op jit(solution)/shard_map/ppermute | solution.py:233
  20.5 7.3 %collective-permute-start.10 = (f16[184,128]{1,0:T(8,128)(2,1)S(1)}, f16[184,128]{1,0:T(8,128)(2,1)S(1)}, u32[]{:S(2)}, u32[]{:S(2)}) collective-permute-start(f16[184,128]{1,0:T(8,128)(2,1)S(1)} %convert_element_type.32), channel_id=1, source_target_pairs={{0,16},{2,18},{4,20},{6,22},{8,24},{10,26},{12,28},{14,30},{16,0},... | collective-permute-start | bytes 141320 | tf_op jit(solution)/shard_map/ppermute | solution.py:233
  23.1 6.4 %collective-permute-start.9 = (f16[184,128]{1,0:T(8,128)(2,1)S(1)}, f16[184,128]{1,0:T(8,128)(2,1)S(1)}, u32[]{:S(2)}, u32[]{:S(2)}) collective-permute-start(f16[184,128]{1,0:T(8,128)(2,1)S(1)} %convert_element_type.30), channel_id=1, source_target_pairs={{0,24},{2,26},{4,28},{6,30},{8,16},{10,18},{12,20},{14,22},{16,8},... | collective-permute-start | bytes 141320 | tf_op jit(solution)/shard_map/ppermute | solution.py:233
  23.4 6.2 %collective-permute-start.8 = (f16[360,128]{1,0:T(8,128)(2,1)S(1)}, f16[360,128]{1,0:T(8,128)(2,1)S(1)}, u32[]{:S(2)}, u32[]{:S(2)}) collective-permute-start(f16[360,128]{1,0:T(8,128)(2,1)S(1)} %convert_element_type.28), channel_id=1, source_target_pairs={{0,8},{2,10},{4,12},{6,14},{8,0},{10,2},{12,4},{14,6},{16,24},{18,... | collective-permute-start | bytes 276488 | tf_op jit(solution)/shard_map/ppermute | solution.py:233
  24.2 5.9 %collective-permute-start.12 = (f16[184,128]{1,0:T(8,128)(2,1)S(1)}, f16[184,128]{1,0:T(8,128)(2,1)S(1)}, u32[]{:S(2)}, u32[]{:S(2)}) collective-permute-start(f16[184,128]{1,0:T(8,128)(2,1)S(1)} %pad_maximum_fusion), channel_id=1, source_target_pairs={{0,16},{2,18},{4,20},{6,22},{8,24},{10,26},{12,28},{14,30},{16,0},... | collective-permute-start | bytes 141320 | tf_op jit(solution)/shard_map/ppermute | solution.py:233

commit v5 on v4

--- a/solution.py
+++ b/solution.py
@@ -169,29 +169,37 @@
     out[...] = multiply([cut, across], cots, units)
 
 
-def product(rows, pad, start, cut, across, cots, keep, *refs):
-    leave, units = refs[:-1], refs[-1]
-    width = cots.shape[1]
-    pieces = width // LANES
+def store(out, first, values, exponent=None):
+    pieces = values.shape[1] // LANES
+    for j in range(pieces):
+        out[pl.ds(first + j, values.shape[0], stride=pieces), :] = values[
+            :, j * LANES : (j + 1) * LANES
+        ]
+    if exponent is not None:
+        end = first + values.shape[0] * pieces
+        out[end : end + 8] = jnp.broadcast_to(exponent, (8, LANES))
+
+
+def product(rows, pad, start, cut, across, cots, keep, joint, *refs):
+    leave, units = list(refs[:-1]), refs[-1]
+    pieces = start.shape[1] // LANES
+    upper = rows // 2
     part = start[...] + multiply([cut, across], cots, units)
-    leave = list(leave)
-    for p in range(part.shape[0] // pad):
+    store(keep, 0, part[:rows])
+    at = 0
+    for p in range(1, part.shape[0] // pad):
         values = part[p * pad : p * pad + rows]
-        if p:
-            most = jnp.max(jnp.max(jnp.abs(values), axis=0, keepdims=True), axis=1, keepdims=True)
-            exponent = jnp.ceil(jnp.log2(jnp.maximum(most, 2.0**-100)))
-            values = values * jnp.exp2(-exponent)
-        done = 0
-        for out in [keep] if p == 0 else [leave.pop(0) for _ in range(1 if p == 1 else 2)]:
-            held = out.shape[0] if p == 0 else out.shape[0] - 8
-            count = held // pieces
-            for j in range(pieces):
-                out[pl.ds(j, count, stride=pieces), :] = values[
-                    done : done + count, j * LANES : (j + 1) * LANES
-                ]
-            if p:
-                out[held:] = jnp.broadcast_to(exponent, (8, LANES))
-            done += count
+        most = jnp.max(jnp.max(jnp.abs(values), axis=0, keepdims=True), axis=1, keepdims=True)
+        exponent = jnp.ceil(jnp.log2(jnp.maximum(most, 2.0**-100)))
+        values = values * jnp.exp2(-exponent)
+        if p > 1:
+            store(leave.pop(0), 0, values[:upper], exponent)
+            values = values[upper:]
+        if p % 2:
+            store(joint, at, values, exponent)
+            at += values.shape[0] * pieces + 8
+        else:
+            store(leave.pop(0), 0, values, exponent)
 
 
 def call(body, outs, args, fetched=(), scratch=(), limit=32, flops=1):
@@ -296,32 +304,36 @@
     pieces = width // LANES
     upper = rows // 2 * pieces
     lower = held - upper
-    sizes = [held, held + 8] + [upper + 8, lower + 8] * (spread - 2)
-    part, *leave = call(
+    pairs = spread // 2 - 1
+    sizes = [held, held + 8 + pairs * (lower + 8)] + [upper + 8, lower + 8, upper + 8] * pairs
+    part, joint, *leave = call(
         lambda *refs: product(rows, pad, *refs),
         [shape((size, LANES), F32) for size in sizes],
         (start, over_dp(cuts[1], 1), over_dp(cuts[3], 3), other_cots),
         scratch=(pltpu.VMEM((2 * slots, across), BF16),),
     )
-    uppers, lowers = [None, None] + leave[1::2], [None, None] + leave[2::2]
+    uppers = {p: leave[p // 2 * 3 - 3 + p % 2 * 2] for p in range(2, spread)}
+    lowers = {p: leave[p // 2 * 3 - 2] for p in range(2, spread, 2)}
 
     def over_spread(array, p):
-        return over_dp(array.astype(jnp.float16), p * MATES).astype(F32)
+        return over_dp(array.astype(jnp.float16), p * MATES)
 
     def value(array):
         return array[:-8] * jnp.exp2(array[-8:-7])
 
+    near = over_spread(joint, 1).astype(F32)
     sums = {}
     for p in range(2, spread, 2):
-        got = over_spread(lowers[p + 1], 1)
+        got = near[held + 8 :][(p // 2 - 1) * (lower + 8) : p // 2 * (lower + 8)]
         top = jnp.maximum(got[-8:-7], lowers[p][-8:-7])
         added = got[:-8] * jnp.exp2(got[-8:-7] - top)
         added = added + lowers[p][:-8] * jnp.exp2(lowers[p][-8:-7] - top)
         sums[p] = jnp.concatenate([added, jnp.broadcast_to(top, (8, LANES))], axis=0)
-    come = sum(value(over_spread(uppers[p], p)) for p in range(spread - 1, 1, -1))
-    come_lower = sum(value(over_spread(sums[p], p)) for p in sums)
-    come = jnp.concatenate([come, come_lower], axis=0)
-    part = part + value(over_spread(leave[0], 1)) + come
+    come = [over_spread(sums[p], p) for p in sums]
+    come += [over_spread(uppers[p], p) for p in range(spread - 1, 1, -1)]
+    halves = [value(array.astype(F32)) for array in lax.optimization_barrier(come)]
+    lower_sum, upper_sum = sum(halves[: len(sums)]), sum(halves[len(sums) :])
+    part = part + value(near[: held + 8]) + jnp.concatenate([upper_sum, lower_sum], axis=0)
     return part.reshape(rows, 1, width)
 
 

time: 31 us -> 31.4 us (1.013)
  waiting for transfers between devices: 6.04 us -> 8.01 us
  starting transfers between devices: 18.5 us -> 17 us
    ppermute x10 -> x9, waiting for transfers between devices: 4.92 us -> 6.89 us  [over_dp(): return lax.ppermute(array, 'dp', [(i, i ^ k) for i in range(n_dp)])]
    ppermute x10 -> x9, starting transfers between devices: 13.5 us -> 12 us  [over_dp(): return lax.ppermute(array, 'dp', [(i, i ^ k) for i in range(n_dp)])]
  transfers between devices with their start and end apart: 13 -> 12, of which waited for: 7 -> 8; matrix products, arithmetic and copies ran while one was open for 1% -> 0% of each run, Pallas kernels for 5% -> 5%
where the time goes in v5:
time: 31.4 us; the launch traced here: 31.3 us
  starting transfers between devices  17 us (54%)
  waiting for transfers between devices  8.01 us (26%)
  Pallas kernels  4.28 us (14%)
  local copies, waits for them, and re-layouts  0.94 us (3%)
  other arithmetic  0.9 us (3%)
    ppermute x9, starting transfers between devices, over_dp(): return lax.ppermute(array, 'dp', [(i, i ^ k) for i in range(n_dp)])  12 us
    ppermute x9, waiting for transfers between devices, over_dp(): return lax.ppermute(array, 'dp', [(i, i ^ k) for i in range(n_dp)])  6.89 us
    ppermute x2, starting transfers between devices, over_experts(): lax.ppermute(array, 'expert', [(s, (s - k) % sources) for s in range(sour...  4.66 us
    pallas_call x7, Pallas kernels, call(): pl.pallas_call(body, out_shape=tuple(outs), in_specs=[anywhere if i in fe...  4.28 us
    unnamed x4, local copies, waits for them, and re-layouts  0.93 us
    ppermute x1, waiting for transfers between devices, over_both(): return lax.ppermute(array, ('dp', 'expert'), pairs)  0.83 us
    add x1, other arithmetic, shards(): part + value(near[:held + 8])  0.72 us
  transfers between devices with their start and end apart: 12, of which 8 were waited for; matrix products, arithmetic and copies ran while one was open for 0% of the time, Pallas kernels for 5%

profile of v5, /device:TPU:0, one launch (start us, length us, event | category | flops | bytes accessed | tf_op | source)
XLA Modules:
  0.0 31.3 jit_solution(11873422525211443291)
XLA Ops:
  0.0 0.0 copy-start
  0.0 2.2 %shard_map.64 = (bf16[48,1152]{1,0:T(8,128)(2,1)}, bf16[48,1152]{1,0:T(8,128)(2,1)}) custom-call(s32[6,256]{1,0:T(8,128)} %bitcast.19, f32[6,256]{1,0:T(8,128)} %bitcast.20, s32[1,256]{1,0:T(1,128)} %refs_2_.1, f32[1,8]{1,0:T(1,128)} %refs_3_.1, bf16[256,1024]{1,0:T(8,128)(2,1)} %refs_4_.1), custom_call_target="tpu_custom_call" | custom-call | flops 1 | bytes 1 | tf_op jit(solution)/shard_map/pallas_call | solution.py:208
  2.2 3.0 %collective-permute-start.1 = (bf16[48,1152]{1,0:T(8,128)(2,1)}, bf16[48,1152]{1,0:T(8,128)(2,1)S(1)}, u32[]{:S(2)}, u32[]{:S(2)}) collective-permute-start(bf16[48,1152]{1,0:T(8,128)(2,1)} %get-tuple-element.25), channel_id=1, source_target_pairs={{0,1},{1,0},{2,3},{3,2},{4,5},{5,4},{6,7},{7,6},{8,9},{9,8},{10,11... | collective-permute-start | bytes 331784 | tf_op jit(solution)/shard_map/ppermute | solution.py:236
  5.2 1.5 %collective-permute-start = (bf16[48,1152]{1,0:T(8,128)(2,1)}, bf16[48,1152]{1,0:T(8,128)(2,1)S(1)}, u32[]{:S(2)}, u32[]{:S(2)}) collective-permute-start(bf16[48,1152]{1,0:T(8,128)(2,1)} %get-tuple-element.21.refs_0_), channel_id=1, source_target_pairs={{0,4},{2,6},{4,0},{6,2},{8,12},{10,14},{12,8},{14,10},{16,20},{18,... | collective-permute-start | bytes 331784 | tf_op jit(solution)/shard_map/ppermute | solution.py:241
  6.7 0.0 copy-done
  6.7 0.0 copy-start.1
  6.7 0.9 %copy-done.1 = bf16[48,1152]{1,0:T(8,128)(2,1)S(1)} copy-done((bf16[48,1152]{1,0:T(8,128)(2,1)S(1)}, bf16[48,1152]{1,0:T(8,128)(2,1)}, u32[]{:S(2)}) %copy-start.1) | copy-done | bytes 110616
  7.6 0.6 %shard_map.65 = (bf16[48,1152]{1,0:T(8,128)(2,1)S(1)}, f32[96,96]{1,0:T(8,128)S(1)}, bf16[48,384]{1,0:T(8,128)(2,1)S(1)}, bf16[48,384]{1,0:T(8,128)(2,1)S(1)}, b...) custom-call(bf16[48,1152]{1,0:T(8,128)(2,1)S(1)} %copy-done.1, bf16[2,48,704]{2,1,0:T(8,128)(2,1)S(1)} %bitcast.18), custom_call_target="tpu_custom_call" | custom-call | flops 4294967296 | bytes 1 | tf_op jit(solution)/shard_map/pallas_call | solution.py:208
  8.2 0.3 collective-permute-done.1.refs_2_.refs_0_
  8.5 0.3 %shard_map.66.squares.refs_4_ = f32[1,128]{1,0:T(1,128)S(1)} custom-call(f32[96,96]{1,0:T(8,128)S(1)} %get-tuple-element.23.refs_0_, bf16[48,1152]{1,0:T(8,128)(2,1)S(1)} %get-tuple-element.24.refs_1_.refs_0_, bf16[48,1152]{1,0:T(8,128)(2,1)S(1)} %collective-permute-done.1.refs_2_.refs_0_), custom_call_target="tpu_custom_call" | custom-call | flops 4294967296 | bytes 1 | tf_op jit(solution)/shard_map/pallas_call | solution.py:208
  8.8 1.4 %collective-permute-done.across.refs_2_ = bf16[48,1152]{1,0:T(8,128)(2,1)S(1)} collective-permute-done((bf16[48,1152]{1,0:T(8,128)(2,1)}, bf16[48,1152]{1,0:T(8,128)(2,1)S(1)}, u32[]{:S(2)}, u32[]{:S(2)}) %collective-permute-start) | collective-permute-done | bytes 110624 | tf_op jit(solution)/shard_map/ppermute | solution.py:241
  10.2 0.1 shard_map.67.refs_1_
  10.2 1.5 %collective-permute-start.2 = (bf16[48,1536]{1,0:T(8,128)(2,1)S(1)}, bf16[48,1536]{1,0:T(8,128)(2,1)S(1)}, u32[]{:S(2)}, u32[]{:S(2)}) collective-permute-start(bf16[48,1536]{1,0:T(8,128)(2,1)S(1)} %shard_map.67.refs_1_), channel_id=1, source_target_pairs={{0,4},{2,6},{4,0},{6,2},{8,12},{10,14},{12,8},{14,10},{16,20},{18,... | collective-permute-start | bytes 442376 | tf_op jit(solution)/shard_map/ppermute | solution.py:241
  11.7 0.4 %collective-permute-start.4 = (f32[1,128]{1,0:T(1,128)S(1)}, f32[1,128]{1,0:T(1,128)S(1)}, u32[]{:S(2)}, u32[]{:S(2)}) collective-permute-start(f32[1,128]{1,0:T(1,128)S(1)} %shard_map.66.squares.refs_4_), channel_id=1, source_target_pairs={{0,5},{1,4},{2,7},{3,6},{4,1},{5,0},{6,3},{7,2},{8,13},{9,12},{10,... | collective-permute-start | bytes 1544 | tf_op jit(solution)/shard_map/ppermute | solution.py:248
  12.1 1.6 %collective-permute-start.3 = (f32[1,128]{1,0:T(1,128)S(1)}, f32[1,128]{1,0:T(1,128)S(1)}, u32[]{:S(2)}, u32[]{:S(2)}) collective-permute-start(f32[1,128]{1,0:T(1,128)S(1)} %shard_map.66.squares.refs_4_), channel_id=1, source_target_pairs={{0,1},{1,0},{2,3},{3,2},{4,5},{5,4},{6,7},{7,6},{8,9},{9,8},{10,11... | collective-permute-start | bytes 1544 | tf_op jit(solution)/shard_map/ppermute | solution.py:236
  13.7 0.0 collective-permute-start.5
  13.7 1.6 %collective-permute-start.6 = (bf16[48,384]{1,0:T(8,128)(2,1)S(1)}, bf16[48,384]{1,0:T(8,128)(2,1)S(1)}, u32[]{:S(2)}, u32[]{:S(2)}) collective-permute-start(bf16[48,384]{1,0:T(8,128)(2,1)S(1)} %get-tuple-element.28), channel_id=1, source_target_pairs={{0,6},{2,4},{4,2},{6,0},{8,14},{10,12},{12,10},{14,8},{16,22},{18,... | collective-permute-start | bytes 110600 | tf_op jit(solution)/shard_map/ppermute | solution.py:241
  15.3 0.8 %collective-permute-done.4.refs_6_ = f32[1,128]{1,0:T(1,128)S(1)} collective-permute-done((f32[1,128]{1,0:T(1,128)S(1)}, f32[1,128]{1,0:T(1,128)S(1)}, u32[]{:S(2)}, u32[]{:S(2)}) %collective-permute-start.4) | collective-permute-done | bytes 544 | tf_op jit(solution)/shard_map/ppermute | solution.py:248
  16.2 0.0 collective-permute-done.3.refs_5_
  16.2 0.0 collective-permute-done.2.refs_3_.rest_across
  16.2 0.2 shard_map.68.cots
  16.4 0.1 collective-permute-start.7
  16.5 0.4 %shard_map.69.refs_0_ = f32[192,1024]{1,0:T(8,128)S(1)} custom-call(bf16[48,384]{1,0:T(8,128)(2,1)S(1)} %get-tuple-element.22.cut, bf16[48,1536]{1,0:T(8,128)(2,1)S(1)} %collective-permute-done.2.refs_3_.rest_across, bf16[192,1024]{1,0:T(8,128)(2,1)S(1)} %shard_map.68.cots), custom_call_target="tpu_custom_call" | custom-call | flops 4294967296 | bytes 1 | tf_op jit(solution)/shard_map/pallas_call | solution.py:208
  16.9 0.0 collective-permute-done.5.refs_1_
  16.9 0.3 collective-permute-done.6.refs_2_
  17.1 1.1 %collective-permute-done.7.refs_3_ = bf16[192,1024]{1,0:T(8,128)(2,1)S(1)} collective-permute-done((bf16[192,1024]{1,0:T(8,128)(2,1)S(1)}, bf16[192,1024]{1,0:T(8,128)(2,1)S(1)}, u32[]{:S(2)}, u32[]{:S(2)}) %collective-permute-start.7) | collective-permute-done | bytes 393248 | tf_op jit(solution)/shard_map/ppermute | solution.py:241
  18.2 0.6 %shard_map.70 = (f32[352,128]{1,0:T(8,128)S(1)}, f32[544,128]{1,0:T(8,128)S(1)}, f32[184,128]{1,0:T(8,128)S(1)}, f32[184,128]{1,0:T(8,128)S(1)}, f32[184,128]{1,0:T(8,128)S(1)}) custom-call(f32[192,1024]{1,0:T(8,128)S(1)} %shard_map.69.refs_0_, bf16[48,384]{1,0:T(8,128)(2,1)S(1)} %collective-permute-done.5.refs_1_, ...), custom_call_target="tpu_custom_call" | custom-call | flops 1 | bytes 1 | tf_op jit(solution)/shard_map/pallas_call | solution.py:208
  18.8 1.6 %collective-permute-start.8 = (f16[544,128]{1,0:T(8,128)(2,1)S(1)}, f16[544,128]{1,0:T(8,128)(2,1)S(1)}, u32[]{:S(2)}, u32[]{:S(2)}) collective-permute-start(f16[544,128]{1,0:T(8,128)(2,1)S(1)} %convert_element_type.22), channel_id=1, source_target_pairs={{0,8},{2,10},{4,12},{6,14},{8,0},{10,2},{12,4},{14,6},{16,24},{18,... | collective-permute-start | bytes 417800 | tf_op jit(solution)/shard_map/ppermute | solution.py:241
  20.5 2.6 %collective-permute-start.11 = (f16[184,128]{1,0:T(8,128)(2,1)S(1)}, f16[184,128]{1,0:T(8,128)(2,1)S(1)}, u32[]{:S(2)}, u32[]{:S(2)}) collective-permute-start(f16[184,128]{1,0:T(8,128)(2,1)S(1)} %convert_element_type.25), channel_id=1, source_target_pairs={{0,16},{2,18},{4,20},{6,22},{8,24},{10,26},{12,28},{14,30},{16,0},... | collective-permute-start | bytes 141320 | tf_op jit(solution)/shard_map/ppermute | solution.py:241
  23.1 0.2 collective-permute-start.10
  23.4 1.7 %collective-permute-done.8 = f16[544,128]{1,0:T(8,128)(2,1)S(1)} collective-permute-done((f16[544,128]{1,0:T(8,128)(2,1)S(1)}, f16[544,128]{1,0:T(8,128)(2,1)S(1)}, u32[]{:S(2)}, u32[]{:S(2)}) %collective-permute-start.8) | collective-permute-done | bytes 139296 | tf_op jit(solution)/shard_map/ppermute | solution.py:241
  25.2 2.8 %collective-permute-start.9 = (f16[184,128]{1,0:T(8,128)(2,1)S(1)}, f16[184,128]{1,0:T(8,128)(2,1)S(1)}, u32[]{:S(2)}, u32[]{:S(2)}) collective-permute-start(f16[184,128]{1,0:T(8,128)(2,1)S(1)} %pad_maximum_fusion), channel_id=1, source_target_pairs={{0,16},{2,18},{4,20},{6,22},{8,24},{10,26},{12,28},{14,30},{16,0},... | collective-permute-start | bytes 141320 | tf_op jit(solution)/shard_map/ppermute | solution.py:241
  28.0 0.0 collective-permute-done.11
  28.0 1.0 %collective-permute-done.10 = f16[184,128]{1,0:T(8,128)(2,1)S(1)} collective-permute-done((f16[184,128]{1,0:T(8,128)(2,1)S(1)}, f16[184,128]{1,0:T(8,128)(2,1)S(1)}, u32[]{:S(2)}, u32[]{:S(2)}) %collective-permute-start.10) | collective-permute-done | bytes 47136 | tf_op jit(solution)/shard_map/ppermute | solution.py:241
  29.0 1.4 %collective-permute-done.9 = f16[184,128]{1,0:T(8,128)(2,1)S(1)} collective-permute-done((f16[184,128]{1,0:T(8,128)(2,1)S(1)}, f16[184,128]{1,0:T(8,128)(2,1)S(1)}, u32[]{:S(2)}, u32[]{:S(2)}) %collective-permute-start.9) | collective-permute-done | bytes 47136 | tf_op jit(solution)/shard_map/ppermute | solution.py:241
  30.6 0.7 %fusion.1 = f32[352,128]{1,0:T(8,128)} fusion(f32[352,128]{1,0:T(8,128)S(1)} %get-tuple-element.29, f32[544,128]{1,0:T(8,128)S(1)} %convert_element_type.23, f32[176,128]{1,0:T(8,128)S(1)} %slice_multiply_fusion.1, f32[176,128]{1,0:T(8,128)S(1)} %fusion.2, f32[128]{0:T(128)S(1)} %get-tuple-element.40), kind=kLoop, calls=%fused_computation.2 | loop fusion | flops 180224 | bytes 721408 | tf_op jit(solution)/shard_map/add | solution.py:336
  (15 shorter events, 0.2 us)
Async XLA Ops:
  0.0 6.7 %copy-start = (bf16[1,1,2,48,704]{4,3,2,1,0:T(8,128)(2,1)S(1)}, bf16[1,1,2,48,704]{4,3,2,1,0:T(8,128)(2,1)}, u32[]{:S(2)}) copy-start(bf16[1,1,2,48,704]{4,3,2,1,0:T(8,128)(2,1)} %param.11) | copy-start | bytes 405508
  2.2 6.3 %collective-permute-start.1 = (bf16[48,1152]{1,0:T(8,128)(2,1)}, bf16[48,1152]{1,0:T(8,128)(2,1)S(1)}, u32[]{:S(2)}, u32[]{:S(2)}) collective-permute-start(bf16[48,1152]{1,0:T(8,128)(2,1)} %get-tuple-element.25), channel_id=1, source_target_pairs={{0,1},{1,0},{2,3},{3,2},{4,5},{5,4},{6,7},{7,6},{8,9},{9,8},{10,11... | collective-permute-start | bytes 331784 | tf_op jit(solution)/shard_map/ppermute | solution.py:236
  5.2 5.0 %collective-permute-start = (bf16[48,1152]{1,0:T(8,128)(2,1)}, bf16[48,1152]{1,0:T(8,128)(2,1)S(1)}, u32[]{:S(2)}, u32[]{:S(2)}) collective-permute-start(bf16[48,1152]{1,0:T(8,128)(2,1)} %get-tuple-element.21.refs_0_), channel_id=1, source_target_pairs={{0,4},{2,6},{4,0},{6,2},{8,12},{10,14},{12,8},{14,10},{16,20},{18,... | collective-permute-start | bytes 331784 | tf_op jit(solution)/shard_map/ppermute | solution.py:241
  6.7 0.9 %copy-start.1 = (bf16[48,1152]{1,0:T(8,128)(2,1)S(1)}, bf16[48,1152]{1,0:T(8,128)(2,1)}, u32[]{:S(2)}) copy-start(bf16[48,1152]{1,0:T(8,128)(2,1)} %get-tuple-element.21.refs_0_) | copy-start | bytes 331780
  10.2 5.9 %collective-permute-start.2 = (bf16[48,1536]{1,0:T(8,128)(2,1)S(1)}, bf16[48,1536]{1,0:T(8,128)(2,1)S(1)}, u32[]{:S(2)}, u32[]{:S(2)}) collective-permute-start(bf16[48,1536]{1,0:T(8,128)(2,1)S(1)} %shard_map.67.refs_1_), channel_id=1, source_target_pairs={{0,4},{2,6},{4,0},{6,2},{8,12},{10,14},{12,8},{14,10},{16,20},{18,... | collective-permute-start | bytes 442376 | tf_op jit(solution)/shard_map/ppermute | solution.py:241
  11.7 4.4 %collective-permute-start.4 = (f32[1,128]{1,0:T(1,128)S(1)}, f32[1,128]{1,0:T(1,128)S(1)}, u32[]{:S(2)}, u32[]{:S(2)}) collective-permute-start(f32[1,128]{1,0:T(1,128)S(1)} %shard_map.66.squares.refs_4_), channel_id=1, source_target_pairs={{0,5},{1,4},{2,7},{3,6},{4,1},{5,0},{6,3},{7,2},{8,13},{9,12},{10,... | collective-permute-start | bytes 1544 | tf_op jit(solution)/shard_map/ppermute | solution.py:248
  12.1 4.1 %collective-permute-start.3 = (f32[1,128]{1,0:T(1,128)S(1)}, f32[1,128]{1,0:T(1,128)S(1)}, u32[]{:S(2)}, u32[]{:S(2)}) collective-permute-start(f32[1,128]{1,0:T(1,128)S(1)} %shard_map.66.squares.refs_4_), channel_id=1, source_target_pairs={{0,1},{1,0},{2,3},{3,2},{4,5},{5,4},{6,7},{7,6},{8,9},{9,8},{10,11... | collective-permute-start | bytes 1544 | tf_op jit(solution)/shard_map/ppermute | solution.py:236
  13.7 3.1 %collective-permute-start.5 = (bf16[48,384]{1,0:T(8,128)(2,1)S(1)}, bf16[48,384]{1,0:T(8,128)(2,1)S(1)}, u32[]{:S(2)}, u32[]{:S(2)}) collective-permute-start(bf16[48,384]{1,0:T(8,128)(2,1)S(1)} %get-tuple-element.27), channel_id=1, source_target_pairs={{0,2},{2,0},{4,6},{6,4},{8,10},{10,8},{12,14},{14,12},{16,18},{18,... | collective-permute-start | bytes 110600 | tf_op jit(solution)/shard_map/ppermute | solution.py:241
  13.7 3.4 %collective-permute-start.6 = (bf16[48,384]{1,0:T(8,128)(2,1)S(1)}, bf16[48,384]{1,0:T(8,128)(2,1)S(1)}, u32[]{:S(2)}, u32[]{:S(2)}) collective-permute-start(bf16[48,384]{1,0:T(8,128)(2,1)S(1)} %get-tuple-element.28), channel_id=1, source_target_pairs={{0,6},{2,4},{4,2},{6,0},{8,14},{10,12},{12,10},{14,8},{16,22},{18,... | collective-permute-start | bytes 110600 | tf_op jit(solution)/shard_map/ppermute | solution.py:241
  16.4 1.8 %collective-permute-start.7 = (bf16[192,1024]{1,0:T(8,128)(2,1)S(1)}, bf16[192,1024]{1,0:T(8,128)(2,1)S(1)}, u32[]{:S(2)}, u32[]{:S(2)}) collective-permute-start(bf16[192,1024]{1,0:T(8,128)(2,1)S(1)} %shard_map.68.cots), channel_id=1, source_target_pairs={{0,2},{2,0},{4,6},{6,4},{8,10},{10,8},{12,14},{14,12},{16,18},{18,... | collective-permute-start | bytes 1179656 | tf_op jit(solution)/shard_map/ppermute | solution.py:241
  18.8 6.3 %collective-permute-start.8 = (f16[544,128]{1,0:T(8,128)(2,1)S(1)}, f16[544,128]{1,0:T(8,128)(2,1)S(1)}, u32[]{:S(2)}, u32[]{:S(2)}) collective-permute-start(f16[544,128]{1,0:T(8,128)(2,1)S(1)} %convert_element_type.22), channel_id=1, source_target_pairs={{0,8},{2,10},{4,12},{6,14},{8,0},{10,2},{12,4},{14,6},{16,24},{18,... | collective-permute-start | bytes 417800 | tf_op jit(solution)/shard_map/ppermute | solution.py:241
  20.5 7.5 %collective-permute-start.11 = (f16[184,128]{1,0:T(8,128)(2,1)S(1)}, f16[184,128]{1,0:T(8,128)(2,1)S(1)}, u32[]{:S(2)}, u32[]{:S(2)}) collective-permute-start(f16[184,128]{1,0:T(8,128)(2,1)S(1)} %convert_element_type.25), channel_id=1, source_target_pairs={{0,16},{2,18},{4,20},{6,22},{8,24},{10,26},{12,28},{14,30},{16,0},... | collective-permute-start | bytes 141320 | tf_op jit(solution)/shard_map/ppermute | solution.py:241
  23.1 5.9 %collective-permute-start.10 = (f16[184,128]{1,0:T(8,128)(2,1)S(1)}, f16[184,128]{1,0:T(8,128)(2,1)S(1)}, u32[]{:S(2)}, u32[]{:S(2)}) collective-permute-start(f16[184,128]{1,0:T(8,128)(2,1)S(1)} %convert_element_type.24), channel_id=1, source_target_pairs={{0,24},{2,26},{4,28},{6,30},{8,16},{10,18},{12,20},{14,22},{16,8},... | collective-permute-start | bytes 141320 | tf_op jit(solution)/shard_map/ppermute | solution.py:241
  25.2 5.2 %collective-permute-start.9 = (f16[184,128]{1,0:T(8,128)(2,1)S(1)}, f16[184,128]{1,0:T(8,128)(2,1)S(1)}, u32[]{:S(2)}, u32[]{:S(2)}) collective-permute-start(f16[184,128]{1,0:T(8,128)(2,1)S(1)} %pad_maximum_fusion), channel_id=1, source_target_pairs={{0,16},{2,18},{4,20},{6,22},{8,24},{10,26},{12,28},{14,30},{16,0},... | collective-permute-start | bytes 141320 | tf_op jit(solution)/shard_map/ppermute | solution.py:241

commit v6 on v4

--- a/solution.py
+++ b/solution.py
@@ -294,7 +294,7 @@
 
     held = rows * (width // LANES)
     pieces = width // LANES
-    upper = rows // 2 * pieces
+    upper = (rows - rows // 3) * pieces
     lower = held - upper
     sizes = [held, held + 8] + [upper + 8, lower + 8] * (spread - 2)
     part, *leave = call(

time: 31 us -> 35.1 us (1.13)
  waiting for transfers between devices: 6.04 us -> 10.5 us
  starting transfers between devices: 18.5 us -> 18.1 us
    ppermute x10, waiting for transfers between devices: 4.92 us -> 9.4 us  [over_dp(): return lax.ppermute(array, 'dp', [(i, i ^ k) for i in range(n_dp)])]
    ppermute x10, starting transfers between devices: 13.5 us -> 13 us  [over_dp(): return lax.ppermute(array, 'dp', [(i, i ^ k) for i in range(n_dp)])]
  transfers between devices with their start and end apart: 13 -> 13, of which waited for: 7 -> 8; matrix products, arithmetic and copies ran while one was open for 1% -> 0% of each run, Pallas kernels for 5% -> 4%
where the time goes in v6:
time: 35.1 us; the launch traced here: 34.9 us
  starting transfers between devices  18.1 us (52%)
  waiting for transfers between devices  10.5 us (30%)
  Pallas kernels  4.27 us (12%)
  local copies, waits for them, and re-layouts  0.94 us (3%)
  other arithmetic  0.92 us (3%)
    ppermute x10, starting transfers between devices, over_dp(): return lax.ppermute(array, 'dp', [(i, i ^ k) for i in range(n_dp)])  13 us
    ppermute x10, waiting for transfers between devices, over_dp(): return lax.ppermute(array, 'dp', [(i, i ^ k) for i in range(n_dp)])  9.4 us
    ppermute x2, starting transfers between devices, over_experts(): lax.ppermute(array, 'expert', [(s, (s - k) % sources) for s in range(sour...  4.66 us
    pallas_call x7, Pallas kernels, call(): pl.pallas_call(body, out_shape=tuple(outs), in_specs=[anywhere if i in fe...  4.27 us
    unnamed x4, local copies, waits for them, and re-layouts  0.93 us
    ppermute x1, waiting for transfers between devices, over_both(): return lax.ppermute(array, ('dp', 'expert'), pairs)  0.83 us
    add x1, other arithmetic, shards(): part = part + value(over_spread(leave[0], 1)) + come  0.72 us
  transfers between devices with their start and end apart: 13, of which 8 were waited for; matrix products, arithmetic and copies ran while one was open for 0% of the time, Pallas kernels for 4%

profile of v6, /device:TPU:0, one launch (start us, length us, event | category | flops | bytes accessed | tf_op | source)
XLA Modules:
  0.0 34.9 jit_solution(8938052201395224973)
XLA Ops:
  0.0 0.0 copy-start
  0.0 2.2 %shard_map.64 = (bf16[48,1152]{1,0:T(8,128)(2,1)}, bf16[48,1152]{1,0:T(8,128)(2,1)}) custom-call(s32[6,256]{1,0:T(8,128)} %bitcast.19, f32[6,256]{1,0:T(8,128)} %bitcast.20, s32[1,256]{1,0:T(1,128)} %refs_2_.1, f32[1,8]{1,0:T(1,128)} %refs_3_.1, bf16[256,1024]{1,0:T(8,128)(2,1)} %refs_4_.1), custom_call_target="tpu_custom_call" | custom-call | flops 1 | bytes 1 | tf_op jit(solution)/shard_map/pallas_call | solution.py:200
  2.2 3.0 %collective-permute-start.1 = (bf16[48,1152]{1,0:T(8,128)(2,1)}, bf16[48,1152]{1,0:T(8,128)(2,1)S(1)}, u32[]{:S(2)}, u32[]{:S(2)}) collective-permute-start(bf16[48,1152]{1,0:T(8,128)(2,1)} %get-tuple-element.23), channel_id=1, source_target_pairs={{0,1},{1,0},{2,3},{3,2},{4,5},{5,4},{6,7},{7,6},{8,9},{9,8},{10,11... | collective-permute-start | bytes 331784 | tf_op jit(solution)/shard_map/ppermute | solution.py:228
  5.2 1.5 %collective-permute-start = (bf16[48,1152]{1,0:T(8,128)(2,1)}, bf16[48,1152]{1,0:T(8,128)(2,1)S(1)}, u32[]{:S(2)}, u32[]{:S(2)}) collective-permute-start(bf16[48,1152]{1,0:T(8,128)(2,1)} %get-tuple-element.19.refs_0_), channel_id=1, source_target_pairs={{0,4},{2,6},{4,0},{6,2},{8,12},{10,14},{12,8},{14,10},{16,20},{18,... | collective-permute-start | bytes 331784 | tf_op jit(solution)/shard_map/ppermute | solution.py:233
  6.7 0.0 copy-done
  6.7 0.0 copy-start.1
  6.7 0.9 %copy-done.1 = bf16[48,1152]{1,0:T(8,128)(2,1)S(1)} copy-done((bf16[48,1152]{1,0:T(8,128)(2,1)S(1)}, bf16[48,1152]{1,0:T(8,128)(2,1)}, u32[]{:S(2)}) %copy-start.1) | copy-done | bytes 110616
  7.6 0.6 %shard_map.65 = (bf16[48,1152]{1,0:T(8,128)(2,1)S(1)}, f32[96,96]{1,0:T(8,128)S(1)}, bf16[48,384]{1,0:T(8,128)(2,1)S(1)}, bf16[48,384]{1,0:T(8,128)(2,1)S(1)}, b...) custom-call(bf16[48,1152]{1,0:T(8,128)(2,1)S(1)} %copy-done.1, bf16[2,48,704]{2,1,0:T(8,128)(2,1)S(1)} %bitcast.18), custom_call_target="tpu_custom_call" | custom-call | flops 4294967296 | bytes 1 | tf_op jit(solution)/shard_map/pallas_call | solution.py:200
  8.2 0.3 collective-permute-done.1.refs_2_.refs_0_
  8.5 0.3 shard_map.66.squares.refs_4_
  8.8 1.4 %collective-permute-done.across.refs_2_ = bf16[48,1152]{1,0:T(8,128)(2,1)S(1)} collective-permute-done((bf16[48,1152]{1,0:T(8,128)(2,1)}, bf16[48,1152]{1,0:T(8,128)(2,1)S(1)}, u32[]{:S(2)}, u32[]{:S(2)}) %collective-permute-start) | collective-permute-done | bytes 110624 | tf_op jit(solution)/shard_map/ppermute | solution.py:233
  10.2 0.1 shard_map.67.refs_1_
  10.2 1.5 %collective-permute-start.2 = (bf16[48,1536]{1,0:T(8,128)(2,1)S(1)}, bf16[48,1536]{1,0:T(8,128)(2,1)S(1)}, u32[]{:S(2)}, u32[]{:S(2)}) collective-permute-start(bf16[48,1536]{1,0:T(8,128)(2,1)S(1)} %shard_map.67.refs_1_), channel_id=1, source_target_pairs={{0,4},{2,6},{4,0},{6,2},{8,12},{10,14},{12,8},{14,10},{16,20},{18,... | collective-permute-start | bytes 442376 | tf_op jit(solution)/shard_map/ppermute | solution.py:233
  11.7 0.4 %collective-permute-start.4 = (f32[1,128]{1,0:T(1,128)S(1)}, f32[1,128]{1,0:T(1,128)S(1)}, u32[]{:S(2)}, u32[]{:S(2)}) collective-permute-start(f32[1,128]{1,0:T(1,128)S(1)} %shard_map.66.squares.refs_4_), channel_id=1, source_target_pairs={{0,5},{1,4},{2,7},{3,6},{4,1},{5,0},{6,3},{7,2},{8,13},{9,12},{10,... | collective-permute-start | bytes 1544 | tf_op jit(solution)/shard_map/ppermute | solution.py:240
  12.1 1.6 %collective-permute-start.3 = (f32[1,128]{1,0:T(1,128)S(1)}, f32[1,128]{1,0:T(1,128)S(1)}, u32[]{:S(2)}, u32[]{:S(2)}) collective-permute-start(f32[1,128]{1,0:T(1,128)S(1)} %shard_map.66.squares.refs_4_), channel_id=1, source_target_pairs={{0,1},{1,0},{2,3},{3,2},{4,5},{5,4},{6,7},{7,6},{8,9},{9,8},{10,11... | collective-permute-start | bytes 1544 | tf_op jit(solution)/shard_map/ppermute | solution.py:228
  13.7 0.0 collective-permute-start.5
  13.7 1.6 %collective-permute-start.6 = (bf16[48,384]{1,0:T(8,128)(2,1)S(1)}, bf16[48,384]{1,0:T(8,128)(2,1)S(1)}, u32[]{:S(2)}, u32[]{:S(2)}) collective-permute-start(bf16[48,384]{1,0:T(8,128)(2,1)S(1)} %get-tuple-element.26), channel_id=1, source_target_pairs={{0,6},{2,4},{4,2},{6,0},{8,14},{10,12},{12,10},{14,8},{16,22},{18,... | collective-permute-start | bytes 110600 | tf_op jit(solution)/shard_map/ppermute | solution.py:233
  15.3 0.8 %collective-permute-done.4.refs_6_ = f32[1,128]{1,0:T(1,128)S(1)} collective-permute-done((f32[1,128]{1,0:T(1,128)S(1)}, f32[1,128]{1,0:T(1,128)S(1)}, u32[]{:S(2)}, u32[]{:S(2)}) %collective-permute-start.4) | collective-permute-done | bytes 544 | tf_op jit(solution)/shard_map/ppermute | solution.py:240
  16.2 0.0 collective-permute-done.3.refs_5_
  16.2 0.0 collective-permute-done.2.refs_3_.rest_across
  16.2 0.2 shard_map.68.cots
  16.4 0.1 collective-permute-start.7
  16.5 0.4 %shard_map.69.refs_0_ = f32[192,1024]{1,0:T(8,128)S(1)} custom-call(bf16[48,384]{1,0:T(8,128)(2,1)S(1)} %get-tuple-element.20.cut, bf16[48,1536]{1,0:T(8,128)(2,1)S(1)} %collective-permute-done.2.refs_3_.rest_across, bf16[192,1024]{1,0:T(8,128)(2,1)S(1)} %shard_map.68.cots), custom_call_target="tpu_custom_call" | custom-call | flops 4294967296 | bytes 1 | tf_op jit(solution)/shard_map/pallas_call | solution.py:200
  16.9 0.0 collective-permute-done.5.refs_1_
  16.9 0.3 collective-permute-done.6.refs_2_
  17.1 1.1 %collective-permute-done.7.refs_3_ = bf16[192,1024]{1,0:T(8,128)(2,1)S(1)} collective-permute-done((bf16[192,1024]{1,0:T(8,128)(2,1)S(1)}, bf16[192,1024]{1,0:T(8,128)(2,1)S(1)}, u32[]{:S(2)}, u32[]{:S(2)}) %collective-permute-start.7) | collective-permute-done | bytes 393248 | tf_op jit(solution)/shard_map/ppermute | solution.py:233
  18.2 0.6 %shard_map.70 = (f32[352,128]{1,0:T(8,128)S(1)}, f32[360,128]{1,0:T(8,128)S(1)}, f32[248,128]{1,0:T(8,128)S(1)}, f32[120,128]{1,0:T(8,128)S(1)}, f32[248,128]{1,0:T(8,128)S(1)}, /*index=5*/f32[120,128]{1,0:T(8,128)S(1)}) custom-call(f32[192,1024]{1,0:T(8,128)S(1)} %shard_map.69.refs_0_, bf16[48,384]{1,0:T(8,128)(2,1)S(1)} %collective-permute-done.5.refs_1_, ...), custom_call_target="tpu_custom_call" | custom-call | flops 1 | bytes 1 | tf_op jit(solution)/shard_map/pallas_call | solution.py:200
  18.8 1.6 %collective-permute-start.11 = (f16[120,128]{1,0:T(8,128)(2,1)S(1)}, f16[120,128]{1,0:T(8,128)(2,1)S(1)}, u32[]{:S(2)}, u32[]{:S(2)}) collective-permute-start(f16[120,128]{1,0:T(8,128)(2,1)S(1)} %convert_element_type.34), channel_id=1, source_target_pairs={{0,8},{2,10},{4,12},{6,14},{8,0},{10,2},{12,4},{14,6},{16,24},{18,... | collective-permute-start | bytes 92168 | tf_op jit(solution)/shard_map/ppermute | solution.py:233
  20.4 2.3 %collective-permute-done.11 = f16[120,128]{1,0:T(8,128)(2,1)S(1)} collective-permute-done((f16[120,128]{1,0:T(8,128)(2,1)S(1)}, f16[120,128]{1,0:T(8,128)(2,1)S(1)}, u32[]{:S(2)}, u32[]{:S(2)}) %collective-permute-start.11) | collective-permute-done | bytes 30752 | tf_op jit(solution)/shard_map/ppermute | solution.py:233
  22.8 2.6 %collective-permute-start.12 = (f16[120,128]{1,0:T(8,128)(2,1)S(1)}, f16[120,128]{1,0:T(8,128)(2,1)S(1)}, u32[]{:S(2)}, u32[]{:S(2)}) collective-permute-start(f16[120,128]{1,0:T(8,128)(2,1)S(1)} %pad_maximum_fusion), channel_id=1, source_target_pairs={{0,16},{2,18},{4,20},{6,22},{8,24},{10,26},{12,28},{14,30},{16,0},... | collective-permute-start | bytes 92168 | tf_op jit(solution)/shard_map/ppermute | solution.py:233
  25.5 0.4 %collective-permute-start.10 = (f16[248,128]{1,0:T(8,128)(2,1)S(1)}, f16[248,128]{1,0:T(8,128)(2,1)S(1)}, u32[]{:S(2)}, u32[]{:S(2)}) collective-permute-start(f16[248,128]{1,0:T(8,128)(2,1)S(1)} %convert_element_type.32), channel_id=1, source_target_pairs={{0,16},{2,18},{4,20},{6,22},{8,24},{10,26},{12,28},{14,30},{16,0},... | collective-permute-start | bytes 190472 | tf_op jit(solution)/shard_map/ppermute | solution.py:233
  25.9 3.6 %collective-permute-start.9 = (f16[248,128]{1,0:T(8,128)(2,1)S(1)}, f16[248,128]{1,0:T(8,128)(2,1)S(1)}, u32[]{:S(2)}, u32[]{:S(2)}) collective-permute-start(f16[248,128]{1,0:T(8,128)(2,1)S(1)} %convert_element_type.30), channel_id=1, source_target_pairs={{0,24},{2,26},{4,28},{6,30},{8,16},{10,18},{12,20},{14,22},{16,8},... | collective-permute-start | bytes 190472 | tf_op jit(solution)/shard_map/ppermute | solution.py:233
  29.5 0.1 collective-permute-start.8
  29.6 0.0 collective-permute-done.12
  29.7 3.2 %collective-permute-done.10 = f16[248,128]{1,0:T(8,128)(2,1)S(1)} collective-permute-done((f16[248,128]{1,0:T(8,128)(2,1)S(1)}, f16[248,128]{1,0:T(8,128)(2,1)S(1)}, u32[]{:S(2)}, u32[]{:S(2)}) %collective-permute-start.10) | collective-permute-done | bytes 63520 | tf_op jit(solution)/shard_map/ppermute | solution.py:233
  32.9 0.0 collective-permute-done.9
  33.0 1.2 %collective-permute-done.8 = f16[360,128]{1,0:T(8,128)(2,1)S(1)} collective-permute-done((f16[360,128]{1,0:T(8,128)(2,1)S(1)}, f16[360,128]{1,0:T(8,128)(2,1)S(1)}, u32[]{:S(2)}, u32[]{:S(2)}) %collective-permute-start.8) | collective-permute-done | bytes 92192 | tf_op jit(solution)/shard_map/ppermute | solution.py:233
  34.2 0.7 %fusion.1 = f32[352,128]{1,0:T(8,128)} fusion(f32[352,128]{1,0:T(8,128)S(1)} %get-tuple-element.27, f32[360,128]{1,0:T(8,128)S(1)} %convert_element_type.29, f32[112,128]{1,0:T(8,128)S(1)} %slice_multiply_fusion.3, f32[240,128]{1,0:T(8,128)S(1)} %fusion.2, f32[128]{0:T(128)S(1)} %fusion.12), kind=kLoop, calls=%fused_computation.2 | loop fusion | flops 180224 | bytes 721408 | tf_op jit(solution)/shard_map/add | solution.py:324
  (19 shorter events, 0.2 us)
Async XLA Ops:
  0.0 6.7 %copy-start = (bf16[1,1,2,48,704]{4,3,2,1,0:T(8,128)(2,1)S(1)}, bf16[1,1,2,48,704]{4,3,2,1,0:T(8,128)(2,1)}, u32[]{:S(2)}) copy-start(bf16[1,1,2,48,704]{4,3,2,1,0:T(8,128)(2,1)} %param.11) | copy-start | bytes 405508
  2.2 6.3 %collective-permute-start.1 = (bf16[48,1152]{1,0:T(8,128)(2,1)}, bf16[48,1152]{1,0:T(8,128)(2,1)S(1)}, u32[]{:S(2)}, u32[]{:S(2)}) collective-permute-start(bf16[48,1152]{1,0:T(8,128)(2,1)} %get-tuple-element.23), channel_id=1, source_target_pairs={{0,1},{1,0},{2,3},{3,2},{4,5},{5,4},{6,7},{7,6},{8,9},{9,8},{10,11... | collective-permute-start | bytes 331784 | tf_op jit(solution)/shard_map/ppermute | solution.py:228
  5.2 5.0 %collective-permute-start = (bf16[48,1152]{1,0:T(8,128)(2,1)}, bf16[48,1152]{1,0:T(8,128)(2,1)S(1)}, u32[]{:S(2)}, u32[]{:S(2)}) collective-permute-start(bf16[48,1152]{1,0:T(8,128)(2,1)} %get-tuple-element.19.refs_0_), channel_id=1, source_target_pairs={{0,4},{2,6},{4,0},{6,2},{8,12},{10,14},{12,8},{14,10},{16,20},{18,... | collective-permute-start | bytes 331784 | tf_op jit(solution)/shard_map/ppermute | solution.py:233
  6.7 0.9 %copy-start.1 = (bf16[48,1152]{1,0:T(8,128)(2,1)S(1)}, bf16[48,1152]{1,0:T(8,128)(2,1)}, u32[]{:S(2)}) copy-start(bf16[48,1152]{1,0:T(8,128)(2,1)} %get-tuple-element.19.refs_0_) | copy-start | bytes 331780
  10.2 5.9 %collective-permute-start.2 = (bf16[48,1536]{1,0:T(8,128)(2,1)S(1)}, bf16[48,1536]{1,0:T(8,128)(2,1)S(1)}, u32[]{:S(2)}, u32[]{:S(2)}) collective-permute-start(bf16[48,1536]{1,0:T(8,128)(2,1)S(1)} %shard_map.67.refs_1_), channel_id=1, source_target_pairs={{0,4},{2,6},{4,0},{6,2},{8,12},{10,14},{12,8},{14,10},{16,20},{18,... | collective-permute-start | bytes 442376 | tf_op jit(solution)/shard_map/ppermute | solution.py:233
  11.7 4.4 %collective-permute-start.4 = (f32[1,128]{1,0:T(1,128)S(1)}, f32[1,128]{1,0:T(1,128)S(1)}, u32[]{:S(2)}, u32[]{:S(2)}) collective-permute-start(f32[1,128]{1,0:T(1,128)S(1)} %shard_map.66.squares.refs_4_), channel_id=1, source_target_pairs={{0,5},{1,4},{2,7},{3,6},{4,1},{5,0},{6,3},{7,2},{8,13},{9,12},{10,... | collective-permute-start | bytes 1544 | tf_op jit(solution)/shard_map/ppermute | solution.py:240
  12.1 4.1 %collective-permute-start.3 = (f32[1,128]{1,0:T(1,128)S(1)}, f32[1,128]{1,0:T(1,128)S(1)}, u32[]{:S(2)}, u32[]{:S(2)}) collective-permute-start(f32[1,128]{1,0:T(1,128)S(1)} %shard_map.66.squares.refs_4_), channel_id=1, source_target_pairs={{0,1},{1,0},{2,3},{3,2},{4,5},{5,4},{6,7},{7,6},{8,9},{9,8},{10,11... | collective-permute-start | bytes 1544 | tf_op jit(solution)/shard_map/ppermute | solution.py:228
  13.7 3.1 %collective-permute-start.5 = (bf16[48,384]{1,0:T(8,128)(2,1)S(1)}, bf16[48,384]{1,0:T(8,128)(2,1)S(1)}, u32[]{:S(2)}, u32[]{:S(2)}) collective-permute-start(bf16[48,384]{1,0:T(8,128)(2,1)S(1)} %get-tuple-element.25), channel_id=1, source_target_pairs={{0,2},{2,0},{4,6},{6,4},{8,10},{10,8},{12,14},{14,12},{16,18},{18,... | collective-permute-start | bytes 110600 | tf_op jit(solution)/shard_map/ppermute | solution.py:233
  13.7 3.4 %collective-permute-start.6 = (bf16[48,384]{1,0:T(8,128)(2,1)S(1)}, bf16[48,384]{1,0:T(8,128)(2,1)S(1)}, u32[]{:S(2)}, u32[]{:S(2)}) collective-permute-start(bf16[48,384]{1,0:T(8,128)(2,1)S(1)} %get-tuple-element.26), channel_id=1, source_target_pairs={{0,6},{2,4},{4,2},{6,0},{8,14},{10,12},{12,10},{14,8},{16,22},{18,... | collective-permute-start | bytes 110600 | tf_op jit(solution)/shard_map/ppermute | solution.py:233
  16.4 1.8 %collective-permute-start.7 = (bf16[192,1024]{1,0:T(8,128)(2,1)S(1)}, bf16[192,1024]{1,0:T(8,128)(2,1)S(1)}, u32[]{:S(2)}, u32[]{:S(2)}) collective-permute-start(bf16[192,1024]{1,0:T(8,128)(2,1)S(1)} %shard_map.68.cots), channel_id=1, source_target_pairs={{0,2},{2,0},{4,6},{6,4},{8,10},{10,8},{12,14},{14,12},{16,18},{18,... | collective-permute-start | bytes 1179656 | tf_op jit(solution)/shard_map/ppermute | solution.py:233
  18.8 4.0 %collective-permute-start.11 = (f16[120,128]{1,0:T(8,128)(2,1)S(1)}, f16[120,128]{1,0:T(8,128)(2,1)S(1)}, u32[]{:S(2)}, u32[]{:S(2)}) collective-permute-start(f16[120,128]{1,0:T(8,128)(2,1)S(1)} %convert_element_type.34), channel_id=1, source_target_pairs={{0,8},{2,10},{4,12},{6,14},{8,0},{10,2},{12,4},{14,6},{16,24},{18,... | collective-permute-start | bytes 92168 | tf_op jit(solution)/shard_map/ppermute | solution.py:233
  22.8 6.8 %collective-permute-start.12 = (f16[120,128]{1,0:T(8,128)(2,1)S(1)}, f16[120,128]{1,0:T(8,128)(2,1)S(1)}, u32[]{:S(2)}, u32[]{:S(2)}) collective-permute-start(f16[120,128]{1,0:T(8,128)(2,1)S(1)} %pad_maximum_fusion), channel_id=1, source_target_pairs={{0,16},{2,18},{4,20},{6,22},{8,24},{10,26},{12,28},{14,30},{16,0},... | collective-permute-start | bytes 92168 | tf_op jit(solution)/shard_map/ppermute | solution.py:233
  25.5 7.4 %collective-permute-start.10 = (f16[248,128]{1,0:T(8,128)(2,1)S(1)}, f16[248,128]{1,0:T(8,128)(2,1)S(1)}, u32[]{:S(2)}, u32[]{:S(2)}) collective-permute-start(f16[248,128]{1,0:T(8,128)(2,1)S(1)} %convert_element_type.32), channel_id=1, source_target_pairs={{0,16},{2,18},{4,20},{6,22},{8,24},{10,26},{12,28},{14,30},{16,0},... | collective-permute-start | bytes 190472 | tf_op jit(solution)/shard_map/ppermute | solution.py:233
  25.9 7.0 %collective-permute-start.9 = (f16[248,128]{1,0:T(8,128)(2,1)S(1)}, f16[248,128]{1,0:T(8,128)(2,1)S(1)}, u32[]{:S(2)}, u32[]{:S(2)}) collective-permute-start(f16[248,128]{1,0:T(8,128)(2,1)S(1)} %convert_element_type.30), channel_id=1, source_target_pairs={{0,24},{2,26},{4,28},{6,30},{8,16},{10,18},{12,20},{14,22},{16,8},... | collective-permute-start | bytes 190472 | tf_op jit(solution)/shard_map/ppermute | solution.py:233
  29.5 4.6 %collective-permute-start.8 = (f16[360,128]{1,0:T(8,128)(2,1)S(1)}, f16[360,128]{1,0:T(8,128)(2,1)S(1)}, u32[]{:S(2)}, u32[]{:S(2)}) collective-permute-start(f16[360,128]{1,0:T(8,128)(2,1)S(1)} %convert_element_type.28), channel_id=1, source_target_pairs={{0,8},{2,10},{4,12},{6,14},{8,0},{10,2},{12,4},{14,6},{16,24},{18,... | collective-permute-start | bytes 276488 | tf_op jit(solution)/shard_map/ppermute | solution.py:233

commit v7 on v3

--- a/solution.py
+++ b/solution.py
@@ -188,16 +188,24 @@
     width = cots.shape[1]
     pieces = width // LANES
     part = start[...] + multiply([cut, across], cots, units)
-    for p, out in enumerate([keep, *leave]):
+    leave = list(leave)
+    for p in range(part.shape[0] // pad):
         values = part[p * pad : p * pad + rows]
         if p:
             most = jnp.max(jnp.max(jnp.abs(values), axis=0, keepdims=True), axis=1, keepdims=True)
             exponent = jnp.ceil(jnp.log2(jnp.maximum(most, 2.0**-100)))
             values = values * jnp.exp2(-exponent)
-            below = out.shape[0] - rows * pieces
-            out[rows * pieces :] = jnp.broadcast_to(exponent, (below, LANES))
-        for j in range(pieces):
-            out[pl.ds(j, rows, stride=pieces), :] = values[:, j * LANES : (j + 1) * LANES]
+        done = 0
+        for out in [keep] if p == 0 else [leave.pop(0) for _ in range(1 if p == 1 else 2)]:
+            held = out.shape[0] if p == 0 else out.shape[0] - 8
+            count = held // pieces
+            for j in range(pieces):
+                out[pl.ds(j, count, stride=pieces), :] = values[
+                    done : done + count, j * LANES : (j + 1) * LANES
+                ]
+            if p:
+                out[held:] = jnp.broadcast_to(exponent, (8, LANES))
+            done += count
 
 
 def call(body, outs, args, fetched=(), scratch=(), limit=32, flops=1):
@@ -299,16 +307,35 @@
     )
 
     held = rows * (width // LANES)
-    sent = held + 8
+    pieces = width // LANES
+    upper = rows // 2 * pieces
+    lower = held - upper
+    sizes = [held, held + 8] + [upper + 8, lower + 8] * (spread - 2)
     part, *leave = call(
         lambda *refs: product(rows, pad, *refs),
-        [shape((held if p == 0 else sent, LANES), F32) for p in range(spread)],
+        [shape((size, LANES), F32) for size in sizes],
         (start, over_dp(cuts[1], 1), over_dp(cuts[3], 3), other_cots),
         scratch=(pltpu.VMEM((2 * slots, across), BF16),),
     )
-    for p in range(1, spread):
-        got = over_dp(leave[p - 1].astype(jnp.float16), p * MATES).astype(F32)
-        part = part + got[:held] * jnp.exp2(got[held : held + 1])
+    uppers, lowers = [None, None] + leave[1::2], [None, None] + leave[2::2]
+
+    def over_spread(array, p):
+        return over_dp(array.astype(jnp.float16), p * MATES).astype(F32)
+
+    def value(array):
+        return array[:-8] * jnp.exp2(array[-8:-7])
+
+    sums = {}
+    for p in range(2, spread, 2):
+        got = over_spread(lowers[p + 1], 1)
+        top = jnp.maximum(got[-8:-7], lowers[p][-8:-7])
+        added = got[:-8] * jnp.exp2(got[-8:-7] - top)
+        added = added + lowers[p][:-8] * jnp.exp2(lowers[p][-8:-7] - top)
+        sums[p] = jnp.concatenate([added, jnp.broadcast_to(top, (8, LANES))], axis=0)
+    come = sum(value(over_spread(uppers[p], p)) for p in range(spread - 1, 1, -1))
+    come_lower = sum(value(over_spread(sums[p], p)) for p in sums)
+    come = jnp.concatenate([come, come_lower], axis=0)
+    part = part + value(over_spread(leave[0], 1)) + come
     return part.reshape(rows, 1, width)
 
 

time: 31.6 us -> 31.1 us (0.984)
  waiting for transfers between devices: 10.8 us -> 5.93 us
  starting transfers between devices: 14.3 us -> 18.6 us
    ppermute x8 -> x10, waiting for transfers between devices: 9.69 us -> 4.78 us  [over_dp(): return lax.ppermute(array, 'dp', [(i, i ^ k) for i in range(n_dp)])]
    ppermute x8 -> x10, starting transfers between devices: 9.24 us -> 13.5 us  [over_dp(): return lax.ppermute(array, 'dp', [(i, i ^ k) for i in range(n_dp)])]
    add x1 -> x2, other arithmetic: 0.73 us -> 0.74 us  [the longest x1 0.72 us: shards(): part = part + value(over_spread(leave[0], 1)) + come]
  transfers between devices with their start and end apart: 11 -> 13, of which waited for: 7 -> 7; matrix products, arithmetic and copies ran while one was open for 0% -> 1% of each run, Pallas kernels for 5% -> 5%
where the time goes in v7:
time: 31.1 us; the launch traced here: 31 us
  starting transfers between devices  18.6 us (60%)
  waiting for transfers between devices  5.93 us (19%)
  Pallas kernels  4.47 us (14%)
  other arithmetic  0.92 us (3%)
  local copies, waits for them, and re-layouts  0.91 us (3%)
    ppermute x10, starting transfers between devices, over_dp(): return lax.ppermute(array, 'dp', [(i, i ^ k) for i in range(n_dp)])  13.5 us
    ppermute x10, waiting for transfers between devices, over_dp(): return lax.ppermute(array, 'dp', [(i, i ^ k) for i in range(n_dp)])  4.78 us
    ppermute x2, starting transfers between devices, over_experts(): lax.ppermute(array, 'expert', [(s, (s - k) % sources) for s in range(sour...  4.53 us
    pallas_call x7, Pallas kernels, call(): pl.pallas_call(body, out_shape=tuple(outs), in_specs=[anywhere if i in fe...  4.47 us
    unnamed x4, local copies, waits for them, and re-layouts  0.9 us
    ppermute x1, waiting for transfers between devices, over_both(): return lax.ppermute(array, ('dp', 'expert'), pairs)  0.83 us
    add x1, other arithmetic, shards(): part = part + value(over_spread(leave[0], 1)) + come  0.72 us
  transfers between devices with their start and end apart: 13, of which 7 were waited for; matrix products, arithmetic and copies ran while one was open for 1% of the time, Pallas kernels for 5%

profile of v7, /device:TPU:0, one launch (start us, length us, event | category | flops | bytes accessed | tf_op | source)
XLA Modules:
  0.0 31.0 jit_solution(4403422210209260324)
XLA Ops:
  0.0 0.0 copy-start
  0.0 2.2 %shard_map.64 = (bf16[48,1024]{1,0:T(8,128)(2,1)}, bf16[48,1152]{1,0:T(8,128)(2,1)}, bf16[48,1152]{1,0:T(8,128)(2,1)}) custom-call(s32[6,256]{1,0:T(8,128)} %bitcast.19, f32[6,256]{1,0:T(8,128)} %bitcast.20, s32[1,256]{1,0:T(1,128)} %refs_2_.1, f32[1,8]{1,0:T(1,128)} %refs_3_.1, bf16[256,1024]{1,0:T(8,128)(2,1)} %refs_4_.1), custom_call_target="tpu_custom_call" | custom-call | flops 1 | bytes 1 | tf_op jit(solution)/shard_map/pallas_call | solution.py:214
  2.2 3.0 %collective-permute-start.1 = (bf16[48,1152]{1,0:T(8,128)(2,1)}, bf16[48,1152]{1,0:T(8,128)(2,1)S(1)}, u32[]{:S(2)}, u32[]{:S(2)}) collective-permute-start(bf16[48,1152]{1,0:T(8,128)(2,1)} %get-tuple-element.25), channel_id=1, source_target_pairs={{0,1},{1,0},{2,3},{3,2},{4,5},{5,4},{6,7},{7,6},{8,9},{9,8},{10,11... | collective-permute-start | bytes 331784 | tf_op jit(solution)/shard_map/ppermute | solution.py:242
  5.2 1.5 %collective-permute-start = (bf16[48,1024]{1,0:T(8,128)(2,1)}, bf16[48,1024]{1,0:T(8,128)(2,1)S(1)}, u32[]{:S(2)}, u32[]{:S(2)}) collective-permute-start(bf16[48,1024]{1,0:T(8,128)(2,1)} %get-tuple-element.22), channel_id=1, source_target_pairs={{0,4},{2,6},{4,0},{6,2},{8,12},{10,14},{12,8},{14,10},{16,20},{18,... | collective-permute-start | bytes 294920 | tf_op jit(solution)/shard_map/ppermute | solution.py:247
  6.7 0.0 copy-done
  6.7 0.0 copy-start.1
  6.7 0.9 %copy-done.1 = bf16[48,1152]{1,0:T(8,128)(2,1)S(1)} copy-done((bf16[48,1152]{1,0:T(8,128)(2,1)S(1)}, bf16[48,1152]{1,0:T(8,128)(2,1)}, u32[]{:S(2)}) %copy-start.1) | copy-done | bytes 110616
  7.6 0.6 %shard_map.65 = (bf16[48,1152]{1,0:T(8,128)(2,1)S(1)}, f32[96,96]{1,0:T(8,128)S(1)}, bf16[48,384]{1,0:T(8,128)(2,1)S(1)}, bf16[48,384]{1,0:T(8,128)(2,1)S(1)}, b...) custom-call(bf16[48,1152]{1,0:T(8,128)(2,1)S(1)} %copy-done.1, bf16[2,48,704]{2,1,0:T(8,128)(2,1)S(1)} %bitcast.18), custom_call_target="tpu_custom_call" | custom-call | flops 1 | bytes 1 | tf_op jit(solution)/shard_map/pallas_call | solution.py:214
  8.2 0.3 %collective-permute-done.1.refs_2_.refs_4_ = bf16[48,1152]{1,0:T(8,128)(2,1)S(1)} collective-permute-done((bf16[48,1152]{1,0:T(8,128)(2,1)}, bf16[48,1152]{1,0:T(8,128)(2,1)S(1)}, u32[]{:S(2)}, u32[]{:S(2)}) %collective-permute-start.1) | collective-permute-done | bytes 110624 | tf_op jit(solution)/shard_map/ppermute | solution.py:242
  8.5 0.3 %shard_map.66.refs_2_.refs_4_ = f32[1,128]{1,0:T(1,128)S(1)} custom-call(f32[96,96]{1,0:T(8,128)S(1)} %get-tuple-element.24.refs_0_, bf16[48,1152]{1,0:T(8,128)(2,1)S(1)} %get-tuple-element.23.refs_1_.refs_0_, bf16[48,1152]{1,0:T(8,128)(2,1)S(1)} %collective-permute-done.1.refs_2_.refs_4_), custom_call_target="tpu_custom_call" | custom-call | flops 4294967296 | bytes 1 | tf_op jit(solution)/shard_map/pallas_call | solution.py:214
  8.8 1.2 %collective-permute-done.refs_0_.refs_2_ = bf16[48,1024]{1,0:T(8,128)(2,1)S(1)} collective-permute-done((bf16[48,1024]{1,0:T(8,128)(2,1)}, bf16[48,1024]{1,0:T(8,128)(2,1)S(1)}, u32[]{:S(2)}, u32[]{:S(2)}) %collective-permute-start) | collective-permute-done | bytes 98336 | tf_op jit(solution)/shard_map/ppermute | solution.py:247
  10.0 0.1 shard_map.67.refs_1_
  10.1 1.6 %collective-permute-start.2 = (bf16[48,1408]{1,0:T(8,128)(2,1)S(1)}, bf16[48,1408]{1,0:T(8,128)(2,1)S(1)}, u32[]{:S(2)}, u32[]{:S(2)}) collective-permute-start(bf16[48,1408]{1,0:T(8,128)(2,1)S(1)} %shard_map.67.refs_1_), channel_id=1, source_target_pairs={{0,4},{2,6},{4,0},{6,2},{8,12},{10,14},{12,8},{14,10},{16,20},{18,... | collective-permute-start | bytes 405512 | tf_op jit(solution)/shard_map/ppermute | solution.py:247
  11.7 0.5 %collective-permute-start.4 = (f32[1,128]{1,0:T(1,128)S(1)}, f32[1,128]{1,0:T(1,128)S(1)}, u32[]{:S(2)}, u32[]{:S(2)}) collective-permute-start(f32[1,128]{1,0:T(1,128)S(1)} %shard_map.66.refs_2_.refs_4_), channel_id=1, source_target_pairs={{0,5},{1,4},{2,7},{3,6},{4,1},{5,0},{6,3},{7,2},{8,13},{9,12},{10,... | collective-permute-start | bytes 1544 | tf_op jit(solution)/shard_map/ppermute | solution.py:254
  12.2 1.5 %collective-permute-start.3 = (f32[1,128]{1,0:T(1,128)S(1)}, f32[1,128]{1,0:T(1,128)S(1)}, u32[]{:S(2)}, u32[]{:S(2)}) collective-permute-start(f32[1,128]{1,0:T(1,128)S(1)} %shard_map.66.refs_2_.refs_4_), channel_id=1, source_target_pairs={{0,1},{1,0},{2,3},{3,2},{4,5},{5,4},{6,7},{7,6},{8,9},{9,8},{10,11... | collective-permute-start | bytes 1544 | tf_op jit(solution)/shard_map/ppermute | solution.py:242
  13.7 0.0 collective-permute-start.5
  13.7 1.6 %collective-permute-start.6 = (bf16[48,384]{1,0:T(8,128)(2,1)S(1)}, bf16[48,384]{1,0:T(8,128)(2,1)S(1)}, u32[]{:S(2)}, u32[]{:S(2)}) collective-permute-start(bf16[48,384]{1,0:T(8,128)(2,1)S(1)} %get-tuple-element.28), channel_id=1, source_target_pairs={{0,6},{2,4},{4,2},{6,0},{8,14},{10,12},{12,10},{14,8},{16,22},{18,... | collective-permute-start | bytes 110600 | tf_op jit(solution)/shard_map/ppermute | solution.py:247
  15.3 0.8 %collective-permute-done.4.refs_6_ = f32[1,128]{1,0:T(1,128)S(1)} collective-permute-done((f32[1,128]{1,0:T(1,128)S(1)}, f32[1,128]{1,0:T(1,128)S(1)}, u32[]{:S(2)}, u32[]{:S(2)}) %collective-permute-start.4) | collective-permute-done | bytes 544 | tf_op jit(solution)/shard_map/ppermute | solution.py:254
  16.1 0.0 collective-permute-done.3.refs_5_
  16.1 0.0 collective-permute-done.2.refs_3_.rest_across
  16.1 0.4 %shard_map.68.cots = bf16[192,1024]{1,0:T(8,128)(2,1)S(1)} custom-call(bf16[48,1152]{1,0:T(8,128)(2,1)S(1)} %get-tuple-element.23.refs_1_.refs_0_, bf16[48,1408]{1,0:T(8,128)(2,1)S(1)} %shard_map.67.refs_1_, bf16[48,1024]{1,0:T(8,128)(2,1)S(1)} %collective-permute-done.refs_0_.refs_2_, bf16[48,1408]{1,0:T(8,128)(2,1)S(1)} %collective-permute-done.2.refs_3_.rest_across, ...), custom_call_target="tpu_custom_call" | custom-call | flops 1 | bytes 1 | tf_op jit(solution)/shard_map/pallas_call | solution.py:214
  16.5 0.1 collective-permute-start.7
  16.6 0.4 %shard_map.69.refs_0_ = f32[192,1024]{1,0:T(8,128)S(1)} custom-call(bf16[48,384]{1,0:T(8,128)(2,1)S(1)} %get-tuple-element.21.cut, bf16[48,1408]{1,0:T(8,128)(2,1)S(1)} %collective-permute-done.2.refs_3_.rest_across, bf16[192,1024]{1,0:T(8,128)(2,1)S(1)} %shard_map.68.cots), custom_call_target="tpu_custom_call" | custom-call | flops 4294967296 | bytes 1 | tf_op jit(solution)/shard_map/pallas_call | solution.py:214
  17.0 0.0 collective-permute-done.5.refs_1_
  17.0 0.1 collective-permute-done.6.refs_2_
  17.1 1.2 %collective-permute-done.7.refs_3_ = bf16[192,1024]{1,0:T(8,128)(2,1)S(1)} collective-permute-done((bf16[192,1024]{1,0:T(8,128)(2,1)S(1)}, bf16[192,1024]{1,0:T(8,128)(2,1)S(1)}, u32[]{:S(2)}, u32[]{:S(2)}) %collective-permute-start.7) | collective-permute-done | bytes 393248 | tf_op jit(solution)/shard_map/ppermute | solution.py:247
  18.3 0.6 %shard_map.70 = (f32[352,128]{1,0:T(8,128)S(1)}, f32[360,128]{1,0:T(8,128)S(1)}, f32[184,128]{1,0:T(8,128)S(1)}, f32[184,128]{1,0:T(8,128)S(1)}, f32[184,128]{1,0:T(8,128)S(1)}, /*index=5*/f32[184,128]{1,0:T(8,128)S(1)}) custom-call(f32[192,1024]{1,0:T(8,128)S(1)} %shard_map.69.refs_0_, bf16[48,384]{1,0:T(8,128)(2,1)S(1)} %collective-permute-done.5.refs_1_, ...), custom_call_target="tpu_custom_call" | custom-call | flops 1 | bytes 1 | tf_op jit(solution)/shard_map/pallas_call | solution.py:214
  18.9 1.6 %collective-permute-start.11 = (f16[184,128]{1,0:T(8,128)(2,1)S(1)}, f16[184,128]{1,0:T(8,128)(2,1)S(1)}, u32[]{:S(2)}, u32[]{:S(2)}) collective-permute-start(f16[184,128]{1,0:T(8,128)(2,1)S(1)} %convert_element_type.34), channel_id=1, source_target_pairs={{0,8},{2,10},{4,12},{6,14},{8,0},{10,2},{12,4},{14,6},{16,24},{18,... | collective-permute-start | bytes 141320 | tf_op jit(solution)/shard_map/ppermute | solution.py:247
  20.6 2.7 %collective-permute-start.10 = (f16[184,128]{1,0:T(8,128)(2,1)S(1)}, f16[184,128]{1,0:T(8,128)(2,1)S(1)}, u32[]{:S(2)}, u32[]{:S(2)}) collective-permute-start(f16[184,128]{1,0:T(8,128)(2,1)S(1)} %convert_element_type.32), channel_id=1, source_target_pairs={{0,16},{2,18},{4,20},{6,22},{8,24},{10,26},{12,28},{14,30},{16,0},... | collective-permute-start | bytes 141320 | tf_op jit(solution)/shard_map/ppermute | solution.py:247
  23.3 0.2 collective-permute-start.9
  23.5 0.7 %collective-permute-start.8 = (f16[360,128]{1,0:T(8,128)(2,1)S(1)}, f16[360,128]{1,0:T(8,128)(2,1)S(1)}, u32[]{:S(2)}, u32[]{:S(2)}) collective-permute-start(f16[360,128]{1,0:T(8,128)(2,1)S(1)} %convert_element_type.28), channel_id=1, source_target_pairs={{0,8},{2,10},{4,12},{6,14},{8,0},{10,2},{12,4},{14,6},{16,24},{18,... | collective-permute-start | bytes 276488 | tf_op jit(solution)/shard_map/ppermute | solution.py:247
  24.2 0.0 collective-permute-done.11
  24.3 3.6 %collective-permute-start.12 = (f16[184,128]{1,0:T(8,128)(2,1)S(1)}, f16[184,128]{1,0:T(8,128)(2,1)S(1)}, u32[]{:S(2)}, u32[]{:S(2)}) collective-permute-start(f16[184,128]{1,0:T(8,128)(2,1)S(1)} %pad_maximum_fusion), channel_id=1, source_target_pairs={{0,16},{2,18},{4,20},{6,22},{8,24},{10,26},{12,28},{14,30},{16,0},... | collective-permute-start | bytes 141320 | tf_op jit(solution)/shard_map/ppermute | solution.py:247
  27.9 0.0 collective-permute-done.10
  27.9 1.8 %collective-permute-done.9 = f16[184,128]{1,0:T(8,128)(2,1)S(1)} collective-permute-done((f16[184,128]{1,0:T(8,128)(2,1)S(1)}, f16[184,128]{1,0:T(8,128)(2,1)S(1)}, u32[]{:S(2)}, u32[]{:S(2)}) %collective-permute-start.9) | collective-permute-done | bytes 47136 | tf_op jit(solution)/shard_map/ppermute | solution.py:247
  29.7 0.0 collective-permute-done.8
  29.8 0.4 %collective-permute-done.12 = f16[184,128]{1,0:T(8,128)(2,1)S(1)} collective-permute-done((f16[184,128]{1,0:T(8,128)(2,1)S(1)}, f16[184,128]{1,0:T(8,128)(2,1)S(1)}, u32[]{:S(2)}, u32[]{:S(2)}) %collective-permute-start.12) | collective-permute-done | bytes 47136 | tf_op jit(solution)/shard_map/ppermute | solution.py:247
  30.3 0.7 %fusion.1 = f32[352,128]{1,0:T(8,128)} fusion(f32[352,128]{1,0:T(8,128)S(1)} %get-tuple-element.29, f32[360,128]{1,0:T(8,128)S(1)} %convert_element_type.29, f32[176,128]{1,0:T(8,128)S(1)} %slice_multiply_fusion.1, f32[176,128]{1,0:T(8,128)S(1)} %fusion.4, f32[128]{0:T(128)S(1)} %fusion.12), kind=kLoop, calls=%fused_computation.2 | loop fusion | flops 180224 | bytes 721408 | tf_op jit(solution)/shard_map/add | solution.py:338
  (19 shorter events, 0.2 us)
Async XLA Ops:
  0.0 6.7 %copy-start = (bf16[1,1,2,48,704]{4,3,2,1,0:T(8,128)(2,1)S(1)}, bf16[1,1,2,48,704]{4,3,2,1,0:T(8,128)(2,1)}, u32[]{:S(2)}) copy-start(bf16[1,1,2,48,704]{4,3,2,1,0:T(8,128)(2,1)} %param.11) | copy-start | bytes 405508
  2.2 6.3 %collective-permute-start.1 = (bf16[48,1152]{1,0:T(8,128)(2,1)}, bf16[48,1152]{1,0:T(8,128)(2,1)S(1)}, u32[]{:S(2)}, u32[]{:S(2)}) collective-permute-start(bf16[48,1152]{1,0:T(8,128)(2,1)} %get-tuple-element.25), channel_id=1, source_target_pairs={{0,1},{1,0},{2,3},{3,2},{4,5},{5,4},{6,7},{7,6},{8,9},{9,8},{10,11... | collective-permute-start | bytes 331784 | tf_op jit(solution)/shard_map/ppermute | solution.py:242
  5.2 4.8 %collective-permute-start = (bf16[48,1024]{1,0:T(8,128)(2,1)}, bf16[48,1024]{1,0:T(8,128)(2,1)S(1)}, u32[]{:S(2)}, u32[]{:S(2)}) collective-permute-start(bf16[48,1024]{1,0:T(8,128)(2,1)} %get-tuple-element.22), channel_id=1, source_target_pairs={{0,4},{2,6},{4,0},{6,2},{8,12},{10,14},{12,8},{14,10},{16,20},{18,... | collective-permute-start | bytes 294920 | tf_op jit(solution)/shard_map/ppermute | solution.py:247
  6.7 0.9 %copy-start.1 = (bf16[48,1152]{1,0:T(8,128)(2,1)S(1)}, bf16[48,1152]{1,0:T(8,128)(2,1)}, u32[]{:S(2)}) copy-start(bf16[48,1152]{1,0:T(8,128)(2,1)} %get-tuple-element.20.refs_0_) | copy-start | bytes 331780
  10.1 6.0 %collective-permute-start.2 = (bf16[48,1408]{1,0:T(8,128)(2,1)S(1)}, bf16[48,1408]{1,0:T(8,128)(2,1)S(1)}, u32[]{:S(2)}, u32[]{:S(2)}) collective-permute-start(bf16[48,1408]{1,0:T(8,128)(2,1)S(1)} %shard_map.67.refs_1_), channel_id=1, source_target_pairs={{0,4},{2,6},{4,0},{6,2},{8,12},{10,14},{12,8},{14,10},{16,20},{18,... | collective-permute-start | bytes 405512 | tf_op jit(solution)/shard_map/ppermute | solution.py:247
  11.7 4.4 %collective-permute-start.4 = (f32[1,128]{1,0:T(1,128)S(1)}, f32[1,128]{1,0:T(1,128)S(1)}, u32[]{:S(2)}, u32[]{:S(2)}) collective-permute-start(f32[1,128]{1,0:T(1,128)S(1)} %shard_map.66.refs_2_.refs_4_), channel_id=1, source_target_pairs={{0,5},{1,4},{2,7},{3,6},{4,1},{5,0},{6,3},{7,2},{8,13},{9,12},{10,... | collective-permute-start | bytes 1544 | tf_op jit(solution)/shard_map/ppermute | solution.py:254
  12.2 3.9 %collective-permute-start.3 = (f32[1,128]{1,0:T(1,128)S(1)}, f32[1,128]{1,0:T(1,128)S(1)}, u32[]{:S(2)}, u32[]{:S(2)}) collective-permute-start(f32[1,128]{1,0:T(1,128)S(1)} %shard_map.66.refs_2_.refs_4_), channel_id=1, source_target_pairs={{0,1},{1,0},{2,3},{3,2},{4,5},{5,4},{6,7},{7,6},{8,9},{9,8},{10,11... | collective-permute-start | bytes 1544 | tf_op jit(solution)/shard_map/ppermute | solution.py:242
  13.7 3.3 %collective-permute-start.5 = (bf16[48,384]{1,0:T(8,128)(2,1)S(1)}, bf16[48,384]{1,0:T(8,128)(2,1)S(1)}, u32[]{:S(2)}, u32[]{:S(2)}) collective-permute-start(bf16[48,384]{1,0:T(8,128)(2,1)S(1)} %get-tuple-element.27), channel_id=1, source_target_pairs={{0,2},{2,0},{4,6},{6,4},{8,10},{10,8},{12,14},{14,12},{16,18},{18,... | collective-permute-start | bytes 110600 | tf_op jit(solution)/shard_map/ppermute | solution.py:247
  13.7 3.4 %collective-permute-start.6 = (bf16[48,384]{1,0:T(8,128)(2,1)S(1)}, bf16[48,384]{1,0:T(8,128)(2,1)S(1)}, u32[]{:S(2)}, u32[]{:S(2)}) collective-permute-start(bf16[48,384]{1,0:T(8,128)(2,1)S(1)} %get-tuple-element.28), channel_id=1, source_target_pairs={{0,6},{2,4},{4,2},{6,0},{8,14},{10,12},{12,10},{14,8},{16,22},{18,... | collective-permute-start | bytes 110600 | tf_op jit(solution)/shard_map/ppermute | solution.py:247
  16.5 1.8 %collective-permute-start.7 = (bf16[192,1024]{1,0:T(8,128)(2,1)S(1)}, bf16[192,1024]{1,0:T(8,128)(2,1)S(1)}, u32[]{:S(2)}, u32[]{:S(2)}) collective-permute-start(bf16[192,1024]{1,0:T(8,128)(2,1)S(1)} %shard_map.68.cots), channel_id=1, source_target_pairs={{0,2},{2,0},{4,6},{6,4},{8,10},{10,8},{12,14},{14,12},{16,18},{18,... | collective-permute-start | bytes 1179656 | tf_op jit(solution)/shard_map/ppermute | solution.py:247
  18.9 5.3 %collective-permute-start.11 = (f16[184,128]{1,0:T(8,128)(2,1)S(1)}, f16[184,128]{1,0:T(8,128)(2,1)S(1)}, u32[]{:S(2)}, u32[]{:S(2)}) collective-permute-start(f16[184,128]{1,0:T(8,128)(2,1)S(1)} %convert_element_type.34), channel_id=1, source_target_pairs={{0,8},{2,10},{4,12},{6,14},{8,0},{10,2},{12,4},{14,6},{16,24},{18,... | collective-permute-start | bytes 141320 | tf_op jit(solution)/shard_map/ppermute | solution.py:247
  20.6 7.3 %collective-permute-start.10 = (f16[184,128]{1,0:T(8,128)(2,1)S(1)}, f16[184,128]{1,0:T(8,128)(2,1)S(1)}, u32[]{:S(2)}, u32[]{:S(2)}) collective-permute-start(f16[184,128]{1,0:T(8,128)(2,1)S(1)} %convert_element_type.32), channel_id=1, source_target_pairs={{0,16},{2,18},{4,20},{6,22},{8,24},{10,26},{12,28},{14,30},{16,0},... | collective-permute-start | bytes 141320 | tf_op jit(solution)/shard_map/ppermute | solution.py:247
  23.3 6.4 %collective-permute-start.9 = (f16[184,128]{1,0:T(8,128)(2,1)S(1)}, f16[184,128]{1,0:T(8,128)(2,1)S(1)}, u32[]{:S(2)}, u32[]{:S(2)}) collective-permute-start(f16[184,128]{1,0:T(8,128)(2,1)S(1)} %convert_element_type.30), channel_id=1, source_target_pairs={{0,24},{2,26},{4,28},{6,30},{8,16},{10,18},{12,20},{14,22},{16,8},... | collective-permute-start | bytes 141320 | tf_op jit(solution)/shard_map/ppermute | solution.py:247
  23.5 6.2 %collective-permute-start.8 = (f16[360,128]{1,0:T(8,128)(2,1)S(1)}, f16[360,128]{1,0:T(8,128)(2,1)S(1)}, u32[]{:S(2)}, u32[]{:S(2)}) collective-permute-start(f16[360,128]{1,0:T(8,128)(2,1)S(1)} %convert_element_type.28), channel_id=1, source_target_pairs={{0,8},{2,10},{4,12},{6,14},{8,0},{10,2},{12,4},{14,6},{16,24},{18,... | collective-permute-start | bytes 276488 | tf_op jit(solution)/shard_map/ppermute | solution.py:247
  24.3 5.9 %collective-permute-start.12 = (f16[184,128]{1,0:T(8,128)(2,1)S(1)}, f16[184,128]{1,0:T(8,128)(2,1)S(1)}, u32[]{:S(2)}, u32[]{:S(2)}) collective-permute-start(f16[184,128]{1,0:T(8,128)(2,1)S(1)} %pad_maximum_fusion), channel_id=1, source_target_pairs={{0,16},{2,18},{4,20},{6,22},{8,24},{10,26},{12,28},{14,30},{16,0},... | collective-permute-start | bytes 141320 | tf_op jit(solution)/shard_map/ppermute | solution.py:247

commit v8 on v4

--- a/solution.py
+++ b/solution.py
@@ -306,22 +306,24 @@
     uppers, lowers = [None, None] + leave[1::2], [None, None] + leave[2::2]
 
     def over_spread(array, p):
-        return over_dp(array.astype(jnp.float16), p * MATES).astype(F32)
+        return over_dp(array.astype(jnp.float16), p * MATES)
 
     def value(array):
         return array[:-8] * jnp.exp2(array[-8:-7])
 
     sums = {}
     for p in range(2, spread, 2):
-        got = over_spread(lowers[p + 1], 1)
+        got = over_spread(lowers[p + 1], 1).astype(F32)
         top = jnp.maximum(got[-8:-7], lowers[p][-8:-7])
         added = got[:-8] * jnp.exp2(got[-8:-7] - top)
         added = added + lowers[p][:-8] * jnp.exp2(lowers[p][-8:-7] - top)
         sums[p] = jnp.concatenate([added, jnp.broadcast_to(top, (8, LANES))], axis=0)
-    come = sum(value(over_spread(uppers[p], p)) for p in range(spread - 1, 1, -1))
-    come_lower = sum(value(over_spread(sums[p], p)) for p in sums)
-    come = jnp.concatenate([come, come_lower], axis=0)
-    part = part + value(over_spread(leave[0], 1)) + come
+    far = list(range(spread - 1, 1, -1))
+    come = [over_spread(leave[0], 1)] + [over_spread(sums[p], p) for p in sums]
+    come += [over_spread(uppers[p], p) for p in far]
+    whole, *halves = [value(array.astype(F32)) for array in lax.optimization_barrier(come)]
+    lower_sum, upper_sum = sum(halves[: len(sums)]), sum(halves[len(sums) :])
+    part = part + whole + jnp.concatenate([upper_sum, lower_sum], axis=0)
     return part.reshape(rows, 1, width)
 
 

time: 31 us -> 31.1 us (level)
  transfers between devices with their start and end apart: 13 -> 13, of which waited for: 7 -> 7; matrix products, arithmetic and copies ran while one was open for 1% -> 0% of each run, Pallas kernels for 5% -> 5%
where the time goes in v8:
time: 31.1 us; the launch traced here: 31 us
  starting transfers between devices  18.5 us (59%)
  waiting for transfers between devices  6.15 us (20%)
  Pallas kernels  4.28 us (14%)
  local copies, waits for them, and re-layouts  0.94 us (3%)
  other arithmetic  0.91 us (3%)
    ppermute x10, starting transfers between devices, over_dp(): return lax.ppermute(array, 'dp', [(i, i ^ k) for i in range(n_dp)])  13.5 us
    ppermute x10, waiting for transfers between devices, over_dp(): return lax.ppermute(array, 'dp', [(i, i ^ k) for i in range(n_dp)])  5.03 us
    ppermute x2, starting transfers between devices, over_experts(): lax.ppermute(array, 'expert', [(s, (s - k) % sources) for s in range(sour...  4.67 us
    pallas_call x7, Pallas kernels, call(): pl.pallas_call(body, out_shape=tuple(outs), in_specs=[anywhere if i in fe...  4.28 us
    unnamed x4, local copies, waits for them, and re-layouts  0.93 us
    ppermute x1, waiting for transfers between devices, over_both(): return lax.ppermute(array, ('dp', 'expert'), pairs)  0.83 us
    add x1, other arithmetic, shards(): part = part + whole + jnp.concatenate([upper_sum, lower_sum], axis=0)  0.71 us
  transfers between devices with their start and end apart: 13, of which 7 were waited for; matrix products, arithmetic and copies ran while one was open for 0% of the time, Pallas kernels for 5%

profile of v8, /device:TPU:0, one launch (start us, length us, event | category | flops | bytes accessed | tf_op | source)
XLA Modules:
  0.0 31.0 jit_solution(8322858289652163597)
XLA Ops:
  0.0 0.0 copy-start
  0.0 2.2 %shard_map.64 = (bf16[48,1152]{1,0:T(8,128)(2,1)}, bf16[48,1152]{1,0:T(8,128)(2,1)}) custom-call(s32[6,256]{1,0:T(8,128)} %bitcast.19, f32[6,256]{1,0:T(8,128)} %bitcast.20, s32[1,256]{1,0:T(1,128)} %refs_2_.1, f32[1,8]{1,0:T(1,128)} %refs_3_.1, bf16[256,1024]{1,0:T(8,128)(2,1)} %refs_4_.1), custom_call_target="tpu_custom_call" | custom-call | flops 1 | bytes 1 | tf_op jit(solution)/shard_map/pallas_call | solution.py:200
  2.2 3.0 %collective-permute-start.1 = (bf16[48,1152]{1,0:T(8,128)(2,1)}, bf16[48,1152]{1,0:T(8,128)(2,1)S(1)}, u32[]{:S(2)}, u32[]{:S(2)}) collective-permute-start(bf16[48,1152]{1,0:T(8,128)(2,1)} %get-tuple-element.27), channel_id=1, source_target_pairs={{0,1},{1,0},{2,3},{3,2},{4,5},{5,4},{6,7},{7,6},{8,9},{9,8},{10,11... | collective-permute-start | bytes 331784 | tf_op jit(solution)/shard_map/ppermute | solution.py:228
  5.2 1.5 %collective-permute-start = (bf16[48,1152]{1,0:T(8,128)(2,1)}, bf16[48,1152]{1,0:T(8,128)(2,1)S(1)}, u32[]{:S(2)}, u32[]{:S(2)}) collective-permute-start(bf16[48,1152]{1,0:T(8,128)(2,1)} %get-tuple-element.23.refs_0_), channel_id=1, source_target_pairs={{0,4},{2,6},{4,0},{6,2},{8,12},{10,14},{12,8},{14,10},{16,20},{18,... | collective-permute-start | bytes 331784 | tf_op jit(solution)/shard_map/ppermute | solution.py:233
  6.7 0.0 copy-done
  6.7 0.0 copy-start.1
  6.7 0.9 %copy-done.1 = bf16[48,1152]{1,0:T(8,128)(2,1)S(1)} copy-done((bf16[48,1152]{1,0:T(8,128)(2,1)S(1)}, bf16[48,1152]{1,0:T(8,128)(2,1)}, u32[]{:S(2)}) %copy-start.1) | copy-done | bytes 110616
  7.6 0.6 %shard_map.65 = (bf16[48,1152]{1,0:T(8,128)(2,1)S(1)}, f32[96,96]{1,0:T(8,128)S(1)}, bf16[48,384]{1,0:T(8,128)(2,1)S(1)}, bf16[48,384]{1,0:T(8,128)(2,1)S(1)}, b...) custom-call(bf16[48,1152]{1,0:T(8,128)(2,1)S(1)} %copy-done.1, bf16[2,48,704]{2,1,0:T(8,128)(2,1)S(1)} %bitcast.18), custom_call_target="tpu_custom_call" | custom-call | flops 4294967296 | bytes 1 | tf_op jit(solution)/shard_map/pallas_call | solution.py:200
  8.2 0.3 collective-permute-done.1.refs_2_.refs_0_
  8.5 0.3 %shard_map.66.squares.refs_4_ = f32[1,128]{1,0:T(1,128)S(1)} custom-call(f32[96,96]{1,0:T(8,128)S(1)} %get-tuple-element.25.refs_0_, bf16[48,1152]{1,0:T(8,128)(2,1)S(1)} %get-tuple-element.26.refs_1_.refs_0_, bf16[48,1152]{1,0:T(8,128)(2,1)S(1)} %collective-permute-done.1.refs_2_.refs_0_), custom_call_target="tpu_custom_call" | custom-call | flops 4294967296 | bytes 1 | tf_op jit(solution)/shard_map/pallas_call | solution.py:200
  8.8 1.4 %collective-permute-done.across.refs_2_ = bf16[48,1152]{1,0:T(8,128)(2,1)S(1)} collective-permute-done((bf16[48,1152]{1,0:T(8,128)(2,1)}, bf16[48,1152]{1,0:T(8,128)(2,1)S(1)}, u32[]{:S(2)}, u32[]{:S(2)}) %collective-permute-start) | collective-permute-done | bytes 110624 | tf_op jit(solution)/shard_map/ppermute | solution.py:233
  10.2 0.1 shard_map.67.refs_1_
  10.2 1.5 %collective-permute-start.2 = (bf16[48,1536]{1,0:T(8,128)(2,1)S(1)}, bf16[48,1536]{1,0:T(8,128)(2,1)S(1)}, u32[]{:S(2)}, u32[]{:S(2)}) collective-permute-start(bf16[48,1536]{1,0:T(8,128)(2,1)S(1)} %shard_map.67.refs_1_), channel_id=1, source_target_pairs={{0,4},{2,6},{4,0},{6,2},{8,12},{10,14},{12,8},{14,10},{16,20},{18,... | collective-permute-start | bytes 442376 | tf_op jit(solution)/shard_map/ppermute | solution.py:233
  11.7 0.4 %collective-permute-start.4 = (f32[1,128]{1,0:T(1,128)S(1)}, f32[1,128]{1,0:T(1,128)S(1)}, u32[]{:S(2)}, u32[]{:S(2)}) collective-permute-start(f32[1,128]{1,0:T(1,128)S(1)} %shard_map.66.squares.refs_4_), channel_id=1, source_target_pairs={{0,5},{1,4},{2,7},{3,6},{4,1},{5,0},{6,3},{7,2},{8,13},{9,12},{10,... | collective-permute-start | bytes 1544 | tf_op jit(solution)/shard_map/ppermute | solution.py:240
  12.1 1.6 %collective-permute-start.3 = (f32[1,128]{1,0:T(1,128)S(1)}, f32[1,128]{1,0:T(1,128)S(1)}, u32[]{:S(2)}, u32[]{:S(2)}) collective-permute-start(f32[1,128]{1,0:T(1,128)S(1)} %shard_map.66.squares.refs_4_), channel_id=1, source_target_pairs={{0,1},{1,0},{2,3},{3,2},{4,5},{5,4},{6,7},{7,6},{8,9},{9,8},{10,11... | collective-permute-start | bytes 1544 | tf_op jit(solution)/shard_map/ppermute | solution.py:228
  13.7 0.0 collective-permute-start.5
  13.7 1.6 %collective-permute-start.6 = (bf16[48,384]{1,0:T(8,128)(2,1)S(1)}, bf16[48,384]{1,0:T(8,128)(2,1)S(1)}, u32[]{:S(2)}, u32[]{:S(2)}) collective-permute-start(bf16[48,384]{1,0:T(8,128)(2,1)S(1)} %get-tuple-element.30), channel_id=1, source_target_pairs={{0,6},{2,4},{4,2},{6,0},{8,14},{10,12},{12,10},{14,8},{16,22},{18,... | collective-permute-start | bytes 110600 | tf_op jit(solution)/shard_map/ppermute | solution.py:233
  15.3 0.8 %collective-permute-done.4.refs_6_ = f32[1,128]{1,0:T(1,128)S(1)} collective-permute-done((f32[1,128]{1,0:T(1,128)S(1)}, f32[1,128]{1,0:T(1,128)S(1)}, u32[]{:S(2)}, u32[]{:S(2)}) %collective-permute-start.4) | collective-permute-done | bytes 544 | tf_op jit(solution)/shard_map/ppermute | solution.py:240
  16.2 0.0 collective-permute-done.3.refs_5_
  16.2 0.0 collective-permute-done.2.refs_3_.rest_across
  16.2 0.2 shard_map.68.cots
  16.4 0.1 collective-permute-start.7
  16.5 0.4 %shard_map.69.refs_0_ = f32[192,1024]{1,0:T(8,128)S(1)} custom-call(bf16[48,384]{1,0:T(8,128)(2,1)S(1)} %get-tuple-element.24.cut, bf16[48,1536]{1,0:T(8,128)(2,1)S(1)} %collective-permute-done.2.refs_3_.rest_across, bf16[192,1024]{1,0:T(8,128)(2,1)S(1)} %shard_map.68.cots), custom_call_target="tpu_custom_call" | custom-call | flops 4294967296 | bytes 1 | tf_op jit(solution)/shard_map/pallas_call | solution.py:200
  16.9 0.0 collective-permute-done.5.refs_1_
  16.9 0.3 collective-permute-done.6.refs_2_
  17.1 1.1 %collective-permute-done.7.refs_3_ = bf16[192,1024]{1,0:T(8,128)(2,1)S(1)} collective-permute-done((bf16[192,1024]{1,0:T(8,128)(2,1)S(1)}, bf16[192,1024]{1,0:T(8,128)(2,1)S(1)}, u32[]{:S(2)}, u32[]{:S(2)}) %collective-permute-start.7) | collective-permute-done | bytes 393248 | tf_op jit(solution)/shard_map/ppermute | solution.py:233
  18.2 0.6 %shard_map.70 = (f32[352,128]{1,0:T(8,128)S(1)}, f32[360,128]{1,0:T(8,128)S(1)}, f32[184,128]{1,0:T(8,128)S(1)}, f32[184,128]{1,0:T(8,128)S(1)}, f32[184,128]{1,0:T(8,128)S(1)}, /*index=5*/f32[184,128]{1,0:T(8,128)S(1)}) custom-call(f32[192,1024]{1,0:T(8,128)S(1)} %shard_map.69.refs_0_, bf16[48,384]{1,0:T(8,128)(2,1)S(1)} %collective-permute-done.5.refs_1_, ...), custom_call_target="tpu_custom_call" | custom-call | flops 1 | bytes 1 | tf_op jit(solution)/shard_map/pallas_call | solution.py:200
  18.8 1.6 %collective-permute-start.9 = (f16[184,128]{1,0:T(8,128)(2,1)S(1)}, f16[184,128]{1,0:T(8,128)(2,1)S(1)}, u32[]{:S(2)}, u32[]{:S(2)}) collective-permute-start(f16[184,128]{1,0:T(8,128)(2,1)S(1)} %convert_element_type.29), channel_id=1, source_target_pairs={{0,8},{2,10},{4,12},{6,14},{8,0},{10,2},{12,4},{14,6},{16,24},{18,... | collective-permute-start | bytes 141320 | tf_op jit(solution)/shard_map/ppermute | solution.py:233
  20.5 2.7 %collective-permute-start.12 = (f16[184,128]{1,0:T(8,128)(2,1)S(1)}, f16[184,128]{1,0:T(8,128)(2,1)S(1)}, u32[]{:S(2)}, u32[]{:S(2)}) collective-permute-start(f16[184,128]{1,0:T(8,128)(2,1)S(1)} %convert_element_type.32), channel_id=1, source_target_pairs={{0,16},{2,18},{4,20},{6,22},{8,24},{10,26},{12,28},{14,30},{16,0},... | collective-permute-start | bytes 141320 | tf_op jit(solution)/shard_map/ppermute | solution.py:233
  23.1 0.2 collective-permute-start.11
  23.4 0.7 %collective-permute-start.8 = (f16[360,128]{1,0:T(8,128)(2,1)S(1)}, f16[360,128]{1,0:T(8,128)(2,1)S(1)}, u32[]{:S(2)}, u32[]{:S(2)}) collective-permute-start(f16[360,128]{1,0:T(8,128)(2,1)S(1)} %convert_element_type.28), channel_id=1, source_target_pairs={{0,8},{2,10},{4,12},{6,14},{8,0},{10,2},{12,4},{14,6},{16,24},{18,... | collective-permute-start | bytes 276488 | tf_op jit(solution)/shard_map/ppermute | solution.py:233
  24.1 0.0 collective-permute-done.9
  24.2 3.6 %collective-permute-start.10 = (f16[184,128]{1,0:T(8,128)(2,1)S(1)}, f16[184,128]{1,0:T(8,128)(2,1)S(1)}, u32[]{:S(2)}, u32[]{:S(2)}) collective-permute-start(f16[184,128]{1,0:T(8,128)(2,1)S(1)} %pad_maximum_fusion), channel_id=1, source_target_pairs={{0,16},{2,18},{4,20},{6,22},{8,24},{10,26},{12,28},{14,30},{16,0},... | collective-permute-start | bytes 141320 | tf_op jit(solution)/shard_map/ppermute | solution.py:233
  27.8 0.0 collective-permute-done.12
  27.8 1.8 %collective-permute-done.11 = f16[184,128]{1,0:T(8,128)(2,1)S(1)} collective-permute-done((f16[184,128]{1,0:T(8,128)(2,1)S(1)}, f16[184,128]{1,0:T(8,128)(2,1)S(1)}, u32[]{:S(2)}, u32[]{:S(2)}) %collective-permute-start.11) | collective-permute-done | bytes 47136 | tf_op jit(solution)/shard_map/ppermute | solution.py:233
  29.6 0.0 collective-permute-done.8
  29.6 0.5 %collective-permute-done.10 = f16[184,128]{1,0:T(8,128)(2,1)S(1)} collective-permute-done((f16[184,128]{1,0:T(8,128)(2,1)S(1)}, f16[184,128]{1,0:T(8,128)(2,1)S(1)}, u32[]{:S(2)}, u32[]{:S(2)}) %collective-permute-start.10) | collective-permute-done | bytes 47136 | tf_op jit(solution)/shard_map/ppermute | solution.py:233
  30.3 0.7 %fusion.1 = f32[352,128]{1,0:T(8,128)} fusion(f32[352,128]{1,0:T(8,128)S(1)} %get-tuple-element.31, f32[360,128]{1,0:T(8,128)S(1)} %convert_element_type.33, f32[176,128]{1,0:T(8,128)S(1)} %slice_multiply_fusion.1, f32[176,128]{1,0:T(8,128)S(1)} %fusion.2, f32[128]{0:T(128)S(1)} %fusion.12), kind=kLoop, calls=%fused_computation.2 | loop fusion | flops 180224 | bytes 721408 | tf_op jit(solution)/shard_map/add | solution.py:326
  (18 shorter events, 0.2 us)
Async XLA Ops:
  0.0 6.7 %copy-start = (bf16[1,1,2,48,704]{4,3,2,1,0:T(8,128)(2,1)S(1)}, bf16[1,1,2,48,704]{4,3,2,1,0:T(8,128)(2,1)}, u32[]{:S(2)}) copy-start(bf16[1,1,2,48,704]{4,3,2,1,0:T(8,128)(2,1)} %param.11) | copy-start | bytes 405508
  2.2 6.3 %collective-permute-start.1 = (bf16[48,1152]{1,0:T(8,128)(2,1)}, bf16[48,1152]{1,0:T(8,128)(2,1)S(1)}, u32[]{:S(2)}, u32[]{:S(2)}) collective-permute-start(bf16[48,1152]{1,0:T(8,128)(2,1)} %get-tuple-element.27), channel_id=1, source_target_pairs={{0,1},{1,0},{2,3},{3,2},{4,5},{5,4},{6,7},{7,6},{8,9},{9,8},{10,11... | collective-permute-start | bytes 331784 | tf_op jit(solution)/shard_map/ppermute | solution.py:228
  5.2 5.0 %collective-permute-start = (bf16[48,1152]{1,0:T(8,128)(2,1)}, bf16[48,1152]{1,0:T(8,128)(2,1)S(1)}, u32[]{:S(2)}, u32[]{:S(2)}) collective-permute-start(bf16[48,1152]{1,0:T(8,128)(2,1)} %get-tuple-element.23.refs_0_), channel_id=1, source_target_pairs={{0,4},{2,6},{4,0},{6,2},{8,12},{10,14},{12,8},{14,10},{16,20},{18,... | collective-permute-start | bytes 331784 | tf_op jit(solution)/shard_map/ppermute | solution.py:233
  6.7 0.9 %copy-start.1 = (bf16[48,1152]{1,0:T(8,128)(2,1)S(1)}, bf16[48,1152]{1,0:T(8,128)(2,1)}, u32[]{:S(2)}) copy-start(bf16[48,1152]{1,0:T(8,128)(2,1)} %get-tuple-element.23.refs_0_) | copy-start | bytes 331780
  10.2 5.9 %collective-permute-start.2 = (bf16[48,1536]{1,0:T(8,128)(2,1)S(1)}, bf16[48,1536]{1,0:T(8,128)(2,1)S(1)}, u32[]{:S(2)}, u32[]{:S(2)}) collective-permute-start(bf16[48,1536]{1,0:T(8,128)(2,1)S(1)} %shard_map.67.refs_1_), channel_id=1, source_target_pairs={{0,4},{2,6},{4,0},{6,2},{8,12},{10,14},{12,8},{14,10},{16,20},{18,... | collective-permute-start | bytes 442376 | tf_op jit(solution)/shard_map/ppermute | solution.py:233
  11.7 4.4 %collective-permute-start.4 = (f32[1,128]{1,0:T(1,128)S(1)}, f32[1,128]{1,0:T(1,128)S(1)}, u32[]{:S(2)}, u32[]{:S(2)}) collective-permute-start(f32[1,128]{1,0:T(1,128)S(1)} %shard_map.66.squares.refs_4_), channel_id=1, source_target_pairs={{0,5},{1,4},{2,7},{3,6},{4,1},{5,0},{6,3},{7,2},{8,13},{9,12},{10,... | collective-permute-start | bytes 1544 | tf_op jit(solution)/shard_map/ppermute | solution.py:240
  12.1 4.1 %collective-permute-start.3 = (f32[1,128]{1,0:T(1,128)S(1)}, f32[1,128]{1,0:T(1,128)S(1)}, u32[]{:S(2)}, u32[]{:S(2)}) collective-permute-start(f32[1,128]{1,0:T(1,128)S(1)} %shard_map.66.squares.refs_4_), channel_id=1, source_target_pairs={{0,1},{1,0},{2,3},{3,2},{4,5},{5,4},{6,7},{7,6},{8,9},{9,8},{10,11... | collective-permute-start | bytes 1544 | tf_op jit(solution)/shard_map/ppermute | solution.py:228
  13.7 3.1 %collective-permute-start.5 = (bf16[48,384]{1,0:T(8,128)(2,1)S(1)}, bf16[48,384]{1,0:T(8,128)(2,1)S(1)}, u32[]{:S(2)}, u32[]{:S(2)}) collective-permute-start(bf16[48,384]{1,0:T(8,128)(2,1)S(1)} %get-tuple-element.29), channel_id=1, source_target_pairs={{0,2},{2,0},{4,6},{6,4},{8,10},{10,8},{12,14},{14,12},{16,18},{18,... | collective-permute-start | bytes 110600 | tf_op jit(solution)/shard_map/ppermute | solution.py:233
  13.7 3.4 %collective-permute-start.6 = (bf16[48,384]{1,0:T(8,128)(2,1)S(1)}, bf16[48,384]{1,0:T(8,128)(2,1)S(1)}, u32[]{:S(2)}, u32[]{:S(2)}) collective-permute-start(bf16[48,384]{1,0:T(8,128)(2,1)S(1)} %get-tuple-element.30), channel_id=1, source_target_pairs={{0,6},{2,4},{4,2},{6,0},{8,14},{10,12},{12,10},{14,8},{16,22},{18,... | collective-permute-start | bytes 110600 | tf_op jit(solution)/shard_map/ppermute | solution.py:233
  16.4 1.8 %collective-permute-start.7 = (bf16[192,1024]{1,0:T(8,128)(2,1)S(1)}, bf16[192,1024]{1,0:T(8,128)(2,1)S(1)}, u32[]{:S(2)}, u32[]{:S(2)}) collective-permute-start(bf16[192,1024]{1,0:T(8,128)(2,1)S(1)} %shard_map.68.cots), channel_id=1, source_target_pairs={{0,2},{2,0},{4,6},{6,4},{8,10},{10,8},{12,14},{14,12},{16,18},{18,... | collective-permute-start | bytes 1179656 | tf_op jit(solution)/shard_map/ppermute | solution.py:233
  18.8 5.3 %collective-permute-start.9 = (f16[184,128]{1,0:T(8,128)(2,1)S(1)}, f16[184,128]{1,0:T(8,128)(2,1)S(1)}, u32[]{:S(2)}, u32[]{:S(2)}) collective-permute-start(f16[184,128]{1,0:T(8,128)(2,1)S(1)} %convert_element_type.29), channel_id=1, source_target_pairs={{0,8},{2,10},{4,12},{6,14},{8,0},{10,2},{12,4},{14,6},{16,24},{18,... | collective-permute-start | bytes 141320 | tf_op jit(solution)/shard_map/ppermute | solution.py:233
  20.5 7.3 %collective-permute-start.12 = (f16[184,128]{1,0:T(8,128)(2,1)S(1)}, f16[184,128]{1,0:T(8,128)(2,1)S(1)}, u32[]{:S(2)}, u32[]{:S(2)}) collective-permute-start(f16[184,128]{1,0:T(8,128)(2,1)S(1)} %convert_element_type.32), channel_id=1, source_target_pairs={{0,16},{2,18},{4,20},{6,22},{8,24},{10,26},{12,28},{14,30},{16,0},... | collective-permute-start | bytes 141320 | tf_op jit(solution)/shard_map/ppermute | solution.py:233
  23.1 6.4 %collective-permute-start.11 = (f16[184,128]{1,0:T(8,128)(2,1)S(1)}, f16[184,128]{1,0:T(8,128)(2,1)S(1)}, u32[]{:S(2)}, u32[]{:S(2)}) collective-permute-start(f16[184,128]{1,0:T(8,128)(2,1)S(1)} %convert_element_type.31), channel_id=1, source_target_pairs={{0,24},{2,26},{4,28},{6,30},{8,16},{10,18},{12,20},{14,22},{16,8},... | collective-permute-start | bytes 141320 | tf_op jit(solution)/shard_map/ppermute | solution.py:233
  23.4 6.2 %collective-permute-start.8 = (f16[360,128]{1,0:T(8,128)(2,1)S(1)}, f16[360,128]{1,0:T(8,128)(2,1)S(1)}, u32[]{:S(2)}, u32[]{:S(2)}) collective-permute-start(f16[360,128]{1,0:T(8,128)(2,1)S(1)} %convert_element_type.28), channel_id=1, source_target_pairs={{0,8},{2,10},{4,12},{6,14},{8,0},{10,2},{12,4},{14,6},{16,24},{18,... | collective-permute-start | bytes 276488 | tf_op jit(solution)/shard_map/ppermute | solution.py:233
  24.2 5.9 %collective-permute-start.10 = (f16[184,128]{1,0:T(8,128)(2,1)S(1)}, f16[184,128]{1,0:T(8,128)(2,1)S(1)}, u32[]{:S(2)}, u32[]{:S(2)}) collective-permute-start(f16[184,128]{1,0:T(8,128)(2,1)S(1)} %pad_maximum_fusion), channel_id=1, source_target_pairs={{0,16},{2,18},{4,20},{6,22},{8,24},{10,26},{12,28},{14,30},{16,0},... | collective-permute-start | bytes 141320 | tf_op jit(solution)/shard_map/ppermute | solution.py:233
